TPU v7x, 32 devices: a whole 2x2x4 slice. The times are simulated.
32 devices in a mesh: tm: 4 (over y, x), rows: 8 (over z, core).
Axes of the slice: x: 2, y: 2, z: 4, core: 2. Of those that a mesh axis runs over, the one named last changes fastest.
Arguments:
- heights: bfloat16 [128, 1024, 1024], P('tm', 'rows'), may hold values from -6 to 6
Outputs:
- spectrum: float32 [64, 1024, 1024], P(None, ('tm', 'rows'))
All inputs are finite; a program needn't handle non-finite values.
Results may differ from a plain program's by a relative error of at most 0.0035.
Values may be sent and summed in bfloat16 or wider, within the bound.
No kernel may reach another device: no remote copies, remote signals or barrier semaphores. Data moves between devices by JAX's collectives and lax.ppermute only.
A program may use at most 128 MiB of HBM per device.

v0:
```python
import functools
import math

import jax
import jax.numpy as jnp
from jax import lax
from jax.sharding import PartitionSpec as P


def spatial_table(length, tm_count, rows_count):
    column = jnp.arange(2 * length, dtype=jnp.int32)
    column_part = column % 2
    column_slot = column // 2
    per_device = length // (tm_count * rows_count)
    stride = tm_count * per_device
    owner_rank = column_slot // stride
    remainder = column_slot % stride
    wavenumber = (
        remainder // per_device * (length // tm_count)
        + owner_rank * per_device
        + remainder % per_device
    )
    position = jnp.arange(length, dtype=jnp.int32)
    angles = (position[:, None] * wavenumber[None, :] % length).astype(jnp.float32) * (
        2.0 * math.pi / length
    )
    values = jnp.where(column_part[None, :] == 0, jnp.cos(angles), -jnp.sin(angles))
    return (values / math.sqrt(length)).astype(jnp.bfloat16)


def make_column_table(length):
    position = jnp.arange(length, dtype=jnp.int32)
    angles = (position[:, None] * position[None, :] % length).astype(jnp.float32) * (
        2.0 * math.pi / length
    )
    values = jnp.concatenate([jnp.cos(angles), jnp.sin(angles)], 1)
    return (values / math.sqrt(length)).astype(jnp.bfloat16)


def time_table(window_len):
    time_step = jnp.arange(window_len, dtype=jnp.int32)
    hann_taper = 0.5 - 0.5 * jnp.cos(time_step.astype(jnp.float32) * (2.0 * math.pi / window_len))
    angles = (time_step[:, None] * time_step[None, :] % window_len).astype(jnp.float32) * (
        2.0 * math.pi / window_len
    )
    tables = jnp.stack(
        [jnp.cos(angles) * hann_taper[None, :], jnp.sin(angles) * hann_taper[None, :]], 0
    )
    return (tables.astype(jnp.bfloat16), jnp.sum(hann_taper * hann_taper))


def column_modes(mixed_rows, col_table):
    number, length, width = mixed_rows.shape
    block_size = math.gcd(number, max(1, 512 // width))

    def column_one_block(frame_block):
        product = jnp.einsum(
            "fxc,xk->fck", frame_block, col_table, preferred_element_type=jnp.float32
        )
        product = product.reshape(block_size, width // 2, 2, 2, length)
        real_part = product[:, :, 0, 0] + product[:, :, 1, 1]
        imag_part = product[:, :, 1, 0] - product[:, :, 0, 1]
        return jnp.stack([real_part, imag_part], 1).astype(jnp.bfloat16)

    result = lax.map(
        column_one_block, mixed_rows.reshape(number // block_size, block_size, length, width)
    )
    return result.reshape(number, 2, width // 2, length)


def window_pair(first_half, second_half, time_taper):
    hop_size = first_half.shape[0]
    number = first_half.shape[2]
    length = first_half.shape[3]
    block_size = math.gcd(number, 8)
    early_taper = time_taper[:, :, :hop_size]
    late_taper = time_taper[:, :, hop_size:]

    def window_one_block(block_index, accumulated):
        early_piece = lax.dynamic_slice_in_dim(first_half, block_index * block_size, block_size, 2)
        late_piece = lax.dynamic_slice_in_dim(second_half, block_index * block_size, block_size, 2)
        product = jnp.einsum(
            "swt,tpqx->swpqx", early_taper, early_piece, preferred_element_type=jnp.float32
        )
        product = product + jnp.einsum(
            "swt,tpqx->swpqx", late_taper, late_piece, preferred_element_type=jnp.float32
        )
        real_part = product[0, :, 0] + product[1, :, 1]
        imag_part = product[0, :, 1] - product[1, :, 0]
        return lax.dynamic_update_slice_in_dim(
            accumulated, real_part * real_part + imag_part * imag_part, block_index * block_size, 1
        )

    start = jnp.zeros((time_taper.shape[1], number, length), jnp.float32)
    return lax.fori_loop(0, number // block_size, window_one_block, start)


def all_windows(mode_field, time_taper, hop_size):
    block_count = mode_field.shape[0] // hop_size
    blocks = mode_field.reshape((block_count, hop_size) + mode_field.shape[1:])

    def one_window(window_index, accumulated):
        first_half = lax.dynamic_index_in_dim(blocks, window_index, 0, keepdims=False)
        second_half = lax.dynamic_index_in_dim(blocks, window_index + 1, 0, keepdims=False)
        return accumulated + window_pair(first_half, second_half, time_taper)

    start = jnp.zeros((time_taper.shape[1], mode_field.shape[2], mode_field.shape[3]), jnp.float32)
    return lax.fori_loop(0, block_count - 1, one_window, start)


def body(heights):
    frames, rows_dev, length = heights.shape
    tm_count = lax.axis_size("tm")
    rows_count = lax.axis_size("rows")
    time_taper, energy = time_table(2 * frames)
    row_table, col_table = lax.optimization_barrier(
        (spatial_table(length, tm_count, rows_count), make_column_table(length))
    )
    mixed_rows = jnp.dot(
        heights.reshape(frames * rows_dev, length), row_table, preferred_element_type=jnp.float32
    )
    mixed_rows = mixed_rows.astype(jnp.bfloat16).reshape(frames, rows_dev, 2 * length)
    transform = functools.partial(column_modes, col_table=col_table)
    mode_field = transform(
        lax.all_to_all(mixed_rows, "rows", split_axis=2, concat_axis=1, tiled=True)
    )
    windows_fn = functools.partial(all_windows, time_taper=time_taper, hop_size=frames)
    summed = windows_fn(lax.all_to_all(mode_field, "tm", split_axis=2, concat_axis=0, tiled=True))
    return summed / ((tm_count - 1) * energy)


def solution(mesh):
    in_specs = (P("tm", "rows", None),)
    out_specs = P(None, ("tm", "rows"), None)
    return jax.shard_map(body, mesh=mesh, in_specs=in_specs, out_specs=out_specs, check_vma=False)
```

profile of v0, /device:TPU:13, one launch (start us, length us, event | category | flops | bytes accessed | tf_op | source)
XLA Modules:
  0.0 1056.9 jit_solution(16496094058831062077)
XLA Ops:
  0.0 16.3 %fusion.34 = (f32[1024,1024]{0,1:T(8,128)S(1)}, f32[1024,1024]{0,1:T(8,128)S(1)}) fusion(), kind=kLoop, calls=%fused_computation.56 | loop fusion | flops 14680064 | bytes 8388608 | tf_op jit(solution)/shard_map/sin | solution.py:36
  19.1 36.0 %multiply_convert_fusion = bf16[1024,2048]{0,1:T(8,128)(2,1)S(1)} fusion(s32[2048]{0:T(1024)S(1)} %fusion.49, pred[2048]{0:T(1024)(128)(4,1)S(1)} %fusion.42), kind=kLoop, calls=%fused_computation.42 | loop fusion | flops 37748736 | bytes 4204544 | tf_op jit(solution)/shard_map/convert_element_type | solution.py:28
  55.1 23.9 %convert_bitcast_fusion = bf16[256,8,32,128]{3,1,2,0:T(8,128)(2,1)} fusion(bf16[1024,2048]{0,1:T(8,128)(2,1)S(1)} %multiply_convert_fusion, bf16[4096,1024]{1,0:T(8,128)(2,1)} %bitcast.113), kind=kOutput, calls=%fused_computation.33 | convolution fusion | flops 17188257792 | bytes 29360128 | tf_op jit(solution)/shard_map/dot_general | solution.py:119
  79.0 15.1 %copy.58 = bf16[256,8,32,128]{3,2,1,0:T(8,128)(2,1)} copy(bf16[256,8,32,128]{3,1,2,0:T(8,128)(2,1)} %convert_bitcast_fusion) | data formatting | bytes 33554432
  94.1 6.4 all-to-all-start
  100.5 360.1 %all-to-all-done = bf16[32,128,2048]{1,0,2:T(8,128)(2,1)} async-done(((bf16[32,128,2048]{1,0,2:T(8,128)(2,1)}), bf16[32,128,2048]{1,0,2:T(8,128)(2,1)}, u32[]{:S(2)}, u32[]{:S(2)}) %all-to-all-start) | async-done | bytes 16777248 | tf_op jit(solution)/shard_map/all_to_all | solution.py:125
  460.6 23.7 %copy.36 = bf16[32,8,128,256]{3,2,1,0:T(8,128)(2,1)} copy(bf16[32,8,128,256]{2,0,3,1:T(8,128)(2,1)} %bitcast.24) | data formatting | bytes 33554432 | tf_op jit(solution)/shard_map/all_to_all | solution.py:125
  484.3 136.3 %while.61 = (s32[]{:T(128)}, bf16[16,2,2,128,1024]{4,3,2,1,0:T(8,128)(2,1)}, bf16[16,2,1024,256]{3,2,1,0:T(8,128)(2,1)}, bf16[1024,2048]{0,1:T(8,128)(2,1)}, s32[]{:T(128)}) while((s32[]{:T(128)}, bf16[16,2,2,128,1024]{4,3,2,1,0:T(8,128)(2,1)}, bf16[16,2,1024,256]{3,2,1,0:T(8,128)(2,1)}, bf16[1024,2048]{0,1:T(8,128)(2,1)}, s32[]{:T(128)}) %tuple.108), condition=%wide.region_1.2_spmd, body=%wide.region_0.1_spmd.sunk | while | flops 2149056512 | bytes 20972096 | solution.py:65
  486.7 4.8 fusion.79
  495.2 4.7 fusion.79
  503.7 4.7 fusion.79
  520.7 4.7 fusion.79
  529.2 4.7 fusion.79
  537.8 4.7 fusion.79
  571.9 4.7 fusion.79
  588.9 4.8 fusion.79
  620.6 31.0 %copy.39 = bf16[32,2,128,1024]{3,1,0,2:T(2,128)(2,1)} copy(bf16[32,2,128,1024]{3,2,1,0:T(8,128)(2,1)} %bitcast.26) | data formatting | bytes 33554432 | tf_op jit(solution)/shard_map/reshape | solution.py:68
  651.6 7.2 all-to-all-start.1
  660.2 180.5 %all-to-all-done.1 = bf16[32,2,128,1024]{3,1,0,2:T(2,128)(2,1)} async-done(((bf16[32,2,128,1024]{3,1,0,2:T(2,128)(2,1)}), bf16[32,2,128,1024]{3,1,0,2:T(2,128)(2,1)}, u32[]{:S(2)}, u32[]{:S(2)}) %all-to-all-start.1) | async-done | bytes 16777248 | tf_op jit(solution)/shard_map/all_to_all | solution.py:128
  840.7 15.7 %copy.40 = bf16[32,2,128,1024]{3,2,1,0:T(8,128)(2,1)S(1)} copy(bf16[32,2,128,1024]{3,1,0,2:T(2,128)(2,1)} %all-to-all-done.1) | data formatting | bytes 33554432 | tf_op jit(solution)/shard_map/all_to_all | solution.py:128
  856.4 11.1 %copy.41 = bf16[4,32,2,32,1024]{4,1,3,2,0:T(8,128)(2,1)} copy(bf16[4,32,2,32,1024]{4,3,0,2,1:T(8,128)(2,1)S(1)} %bitcast.109) | data formatting | bytes 33554432
  867.5 176.3 %while.63 = (s32[]{:T(128)}, f32[64,32,1024]{2,0,1:T(8,128)}, bf16[4,32,2,32,1024]{4,1,3,2,0:T(8,128)(2,1)}, bf16[2,64,64]{1,2,0:T(8,128)(2,1)S(1)}, s32[]{:T(12...) while((s32[]{:T(128)}, f32[64,32,1024]{2,0,1:T(8,128)}, ...), condition=%wide.region_5.6_spmd.clone, body=%wide.region_2.5_spmd.clone.sunk | while | flops 277348352 | bytes 88129960 | solution.py:108
  867.5 8.6 dynamic-slice_bitcast_fusion.3
  880.4 34.4 %while.64 = (s32[]{:T(128)}, f32[64,32,1024]{2,0,1:T(8,128)}, bf16[32,2,32,1024]{3,0,2,1:T(8,128)(2,1)}, bf16[2,64,32]{1,2,0:T(8,128)(2,1)S(1)}, bf16[32,2,32,10...) while((s32[]{:T(128)}, f32[64,32,1024]{2,0,1:T(8,128)}, ...), condition=%wide.region_4.4_spmd, body=%wide.region_3.3_spmd.sunk | while | flops 273154048 | bytes 37765280 | solution.py:95
  914.8 9.8 select_add_fusion.2
  924.7 8.6 dynamic-slice_bitcast_fusion.3
  937.5 34.4 %while.64 = (s32[]{:T(128)}, f32[64,32,1024]{2,0,1:T(8,128)}, bf16[32,2,32,1024]{3,0,2,1:T(8,128)(2,1)}, bf16[2,64,32]{1,2,0:T(8,128)(2,1)S(1)}, bf16[32,2,32,10...) while((s32[]{:T(128)}, f32[64,32,1024]{2,0,1:T(8,128)}, ...), condition=%wide.region_4.4_spmd, body=%wide.region_3.3_spmd.sunk | while | flops 273154048 | bytes 37765280 | solution.py:95
  971.9 12.2 %select_add_fusion.2 = f32[64,32,1024]{2,0,1:T(8,128)} fusion(f32[64,32,1024]{2,0,1:T(8,128)} %get-tuple-element.450, f32[64,32,1024]{2,0,1:T(8,128)} %get-tuple-element.516, pred[]{:T(512)S(6)} %compare.42), kind=kLoop, calls=%fused_computation.30.clone.1 | loop fusion | flops 4194304 | bytes 25165824 | tf_op jit(solution)/shard_map/while/body/eval_jaxpr/add | solution.py:105
  984.1 8.6 dynamic-slice_bitcast_fusion.3
  997.0 34.4 %while.64 = (s32[]{:T(128)}, f32[64,32,1024]{2,0,1:T(8,128)}, bf16[32,2,32,1024]{3,0,2,1:T(8,128)(2,1)}, bf16[2,64,32]{1,2,0:T(8,128)(2,1)S(1)}, bf16[32,2,32,10...) while((s32[]{:T(128)}, f32[64,32,1024]{2,0,1:T(8,128)}, ...), condition=%wide.region_4.4_spmd, body=%wide.region_3.3_spmd.sunk | while | flops 273154048 | bytes 37765280 | solution.py:95
  1031.4 12.2 %select_add_fusion.2 = f32[64,32,1024]{2,0,1:T(8,128)} fusion(f32[64,32,1024]{2,0,1:T(8,128)} %get-tuple-element.450, f32[64,32,1024]{2,0,1:T(8,128)} %get-tuple-element.516, pred[]{:T(512)S(6)} %compare.42), kind=kLoop, calls=%fused_computation.30.clone.1 | loop fusion | flops 4194304 | bytes 25165824 | tf_op jit(solution)/shard_map/while/body/eval_jaxpr/add | solution.py:105
  1048.2 8.3 copy.43
  (140 shorter events, 221.7 us)
Async XLA Ops:
  94.1 366.5 %all-to-all-start = ((bf16[32,128,2048]{1,0,2:T(8,128)(2,1)}), bf16[32,128,2048]{1,0,2:T(8,128)(2,1)}, u32[]{:S(2)}, u32[]{:S(2)}) async-start(bf16[32,128,2048]{1,0,2:T(8,128)(2,1)} %bitcast.108), calls=%async_computation | async-start | bytes 33554432 | tf_op jit(solution)/shard_map/all_to_all | solution.py:125
  651.6 189.1 %all-to-all-start.1 = ((bf16[32,2,128,1024]{3,1,0,2:T(2,128)(2,1)}), bf16[32,2,128,1024]{3,1,0,2:T(2,128)(2,1)}, u32[]{:S(2)}, u32[]{:S(2)}) async-start(bf16[32,2,128,1024]{3,1,0,2:T(2,128)(2,1)} %copy.39), calls=%async_computation.1 | async-start | bytes 33554432 | tf_op jit(solution)/shard_map/all_to_all | solution.py:128
where the time goes:
time: 1070 us; the launch traced here: 1060 us
  waiting for transfers between devices  541 us (51%)
  local copies, waits for them, and re-layouts  182 us (17%)
  matrix products  173 us (16%)
  other arithmetic  146 us (14%)
  starting transfers between devices  13.6 us (1%)
    all_to_all x1, waiting for transfers between devices, body(): lax.all_to_all(mixed_rows, 'rows', split_axis=2, concat_axis=1, tiled=True)  360 us
    all_to_all x1, waiting for transfers between devices, body(): lax.all_to_all(mode_field, 'tm', split_axis=2, concat_axis=0, tiled=True)  181 us
    dot_general x16, matrix products, column_one_block(): jnp.einsum('fxc,xk->fck', frame_block, col_table, preferred_element_type=...  76 us
    dot_general x12, matrix products, window_one_block(): jnp.einsum('swt,tpqx->swpqx', late_taper, late_piece, preferred_element_t...  41.9 us
    dynamic_slice x32, local copies, waits for them, and re-layouts, column_modes(): lax.map(column_one_block, mixed_rows.reshape(number // block_size, block_...  38.4 us
    convert_element_type x1, other arithmetic, spatial_table(): return (values / math.sqrt(length)).astype(jnp.bfloat16)  36 us
    add x3, other arithmetic, one_window(): return accumulated + window_pair(first_half, second_half, time_taper)  34.2 us
    reshape x1, local copies, waits for them, and re-layouts, column_modes(): return result.reshape(number, 2, width // 2, length)  31 us
  transfers between devices with their start and end apart: 2, of which 2 were waited for; matrix products, arithmetic and copies ran while one was open for 0% of the time, Pallas kernels for 0%

commit v1 on v0

v1 whole, which is shorter than its diff:
```python
import functools
import math

import jax
import jax.numpy as jnp
import ml_dtypes
import numpy as np
from jax import lax
from jax.experimental import pallas as pl
from jax.experimental.pallas import tpu as pltpu
from jax.sharding import PartitionSpec as P

AXES = ("tm", "rows")
LANES = 128
TILE = 8
VMEM_BYTES = 56 * 1024 * 1024


def to_bf16(values):
    return values.astype(ml_dtypes.bfloat16)


def unit_angles(left, right, modulus):
    return (np.outer(left, right) % modulus).astype(np.float32) * np.float32(2.0 * math.pi / modulus)


def y_table(length, wavenumbers):
    angles = unit_angles(wavenumbers, np.arange(length), length)
    pairs = np.stack([np.cos(angles), -np.sin(angles)], 1) / np.float32(math.sqrt(length))
    return to_bf16(pairs.reshape(2 * len(wavenumbers), length))


def x_table(length):
    angles = unit_angles(np.arange(length), np.arange(length), length)
    return to_bf16(
        np.concatenate([np.cos(angles), np.sin(angles)], 1) / np.float32(math.sqrt(length))
    )


def window_table(hop, windows):
    size = 2 * hop
    steps = np.arange(size)
    hann = np.float32(0.5) - np.float32(0.5) * np.cos(
        steps.astype(np.float32) * np.float32(2.0 * math.pi / size)
    )
    angles = unit_angles(steps, steps, size)
    cosine = to_bf16(np.cos(angles) * hann[None, :])
    sine = to_bf16(np.sin(angles) * hann[None, :])
    frames = hop * (windows + 1)
    table = np.zeros((windows, 2, size, 2, frames), ml_dtypes.bfloat16)
    for window in range(windows):
        at = slice(window * hop, window * hop + size)
        table[window, 0, :, 0, at] = cosine
        table[window, 0, :, 1, at] = sine
        table[window, 1, :, 1, at] = cosine
        table[window, 1, :, 0, at] = -sine
    return table.reshape(windows * 2 * size, 2 * frames), float(np.sum(hann * hann))


def reversal(size):
    matrix = np.zeros((size, size), ml_dtypes.bfloat16)
    matrix[np.arange(size), (size - np.arange(size)) % size] = 1
    return matrix


def row_transform_kernel(table_ref, heights_ref, out_ref, scratch):
    frames, rows, length = heights_ref.shape
    for frame in range(0, frames, 2):
        pair = heights_ref[frame : frame + 2].reshape(2 * rows, length)
        product = lax.dot_general(
            table_ref[...], pair, (((1,), (1,)), ((), ())), preferred_element_type=jnp.float32
        )
        scratch[:, frame, :] = product[:, :rows]
        scratch[:, frame + 1, :] = product[:, rows:]
    out_ref[...] = scratch[...].astype(jnp.bfloat16)


def row_transform(heights, table):
    frames, rows, length = heights.shape
    columns = table.shape[0]
    if rows != LANES:
        return jnp.einsum(
            "cy,fxy->cfx", table, heights, preferred_element_type=jnp.float32
        ).astype(jnp.bfloat16)
    step = 16
    return pl.pallas_call(
        row_transform_kernel,
        out_shape=jax.ShapeDtypeStruct((columns, frames, rows), jnp.bfloat16),
        grid=(frames // step,),
        in_specs=[
            pl.BlockSpec((columns, length), lambda i: (0, 0)),
            pl.BlockSpec((step, rows, length), lambda i: (i, 0, 0)),
        ],
        out_specs=pl.BlockSpec((columns, step, rows), lambda i: (0, i, 0)),
        scratch_shapes=[pltpu.VMEM((columns, step, rows), jnp.float32)],
        compiler_params=pltpu.CompilerParams(vmem_limit_bytes=VMEM_BYTES),
        cost_estimate=pl.CostEstimate(
            flops=2 * columns * frames * rows * length,
            bytes_accessed=2 * (heights.size + columns * length + columns * frames * rows),
            transcendentals=0,
        ),
        name="row_transform",
    )(table, heights)


def spectrum_kernel(scale, mirrored, *refs):
    if mirrored:
        pieces_ref, x_ref, window_ref, flip_w_ref, flip_k_ref, own_ref, mirror_ref, scratch = refs
    else:
        pieces_ref, x_ref, window_ref, own_ref = refs
    blocks, width, _, part, frames, rows = pieces_ref.shape
    length = x_ref.shape[0]
    all_frames = blocks * frames
    size = 2 * frames
    field = jnp.concatenate(
        [
            jnp.concatenate([pieces_ref[t, s, 0, p] for s in range(width)], 1)
            for p in range(part)
            for t in range(blocks)
        ],
        0,
    )
    chunk = math.gcd(length, 256)
    for at in range(0, length, chunk):
        cosine = jnp.dot(field, x_ref[:, at : at + chunk], preferred_element_type=jnp.float32)
        sine = jnp.dot(
            field, x_ref[:, length + at : length + at + chunk], preferred_element_type=jnp.float32
        )
        real_part = cosine[:all_frames] + sine[all_frames:]
        imag_part = cosine[all_frames:] - sine[:all_frames]
        modes = jnp.concatenate([real_part, imag_part], 0).astype(jnp.bfloat16)
        moved = jnp.dot(window_ref[...], modes, preferred_element_type=jnp.float32)
        power = moved * moved
        total = power[:size]
        for row in range(size, power.shape[0], size):
            total = total + power[row : row + size]
        total = total * scale
        own_ref[0, :, at : at + chunk] = total
        if mirrored:
            flipped = jnp.dot(
                flip_w_ref[...], total.astype(jnp.bfloat16), preferred_element_type=jnp.float32
            )
            row = pl.num_programs(0) - 1 - pl.program_id(0)
            scratch[row, :, at : at + chunk] = flipped.astype(jnp.bfloat16)
    if mirrored:

        @pl.when(pl.program_id(0) == pl.num_programs(0) - 1)
        def reverse():
            number = scratch.shape[0]
            flat = scratch[...].reshape(number * size, length)
            turned = jnp.dot(flat, flip_k_ref[...], preferred_element_type=jnp.float32)
            mirror_ref[...] = turned.astype(jnp.bfloat16).reshape(number, size, length)


def spectrum(pieces, tables, scale, mirrored):
    blocks, width, number, part, frames, rows = pieces.shape
    length = width * rows
    size = 2 * frames
    if rows != LANES:
        pieces = pieces.transpose(0, 2, 3, 4, 1, 5).reshape(blocks, 1, number, part, frames, length)
        width, rows = 1, length
    x_values, windows, flip_w, flip_k = tables
    whole = lambda array: pl.BlockSpec(array.shape, lambda i: (0,) * array.ndim)
    operands = [pieces, x_values, windows]
    in_specs = [
        pl.BlockSpec((blocks, width, 1, part, frames, rows), lambda i: (0, 0, i, 0, 0, 0)),
        whole(x_values),
        whole(windows),
    ]
    out_shape = [jax.ShapeDtypeStruct((number, size, length), jnp.float32)]
    out_specs = [pl.BlockSpec((1, size, length), lambda i: (i, 0, 0))]
    scratch_shapes = []
    if mirrored:
        operands += [flip_w, flip_k]
        in_specs += [whole(flip_w), whole(flip_k)]
        out_shape.append(jax.ShapeDtypeStruct((number, size, length), jnp.bfloat16))
        out_specs.append(pl.BlockSpec((number, size, length), lambda i: (0, 0, 0)))
        scratch_shapes.append(pltpu.VMEM((number, size, length), jnp.bfloat16))
    return pl.pallas_call(
        functools.partial(spectrum_kernel, scale, mirrored),
        out_shape=out_shape,
        grid=(number,),
        in_specs=in_specs,
        out_specs=out_specs,
        scratch_shapes=scratch_shapes,
        compiler_params=pltpu.CompilerParams(vmem_limit_bytes=VMEM_BYTES),
        cost_estimate=pl.CostEstimate(
            flops=number * 2 * length * (4 * blocks * frames * length + windows.size),
            bytes_accessed=2 * pieces.size + 6 * number * size * length,
            transcendentals=0,
        ),
        name="spectrum",
    )(*operands)


def turned(planes):
    return jnp.swapaxes(jnp.stack([plane.astype(jnp.float32) for plane in planes], 0), 0, 1)


def first_rows_kernel(high_ref, low_ref, edge_ref, mirror_ref, out_ref):
    octet = low_ref.shape[0] + 1
    out_ref[:, :octet] = turned([edge_ref[0]] + [low_ref[i] for i in range(octet - 1)])
    out_ref[:, octet : 2 * octet] = turned([high_ref[i] for i in range(octet)])
    out_ref[:, 2 * octet :] = turned([edge_ref[1]] + [mirror_ref[i] for i in range(octet - 1)])


def last_rows_kernel(given_ref, high_ref, low_ref, out_ref):
    del given_ref
    octet = low_ref.shape[0] + 1
    out_ref[...] = turned([high_ref[0]] + [low_ref[i] for i in range(octet - 1)])


def assemble(high, low, edge, high_mirror, low_mirror):
    octet, size, length = high.shape
    if octet % TILE:
        planes = [edge[:1], low, high, edge[1:], high_mirror, low_mirror]
        return jnp.concatenate([plane.astype(jnp.float32) for plane in planes], 0).transpose(1, 0, 2)
    step = 16
    over = lambda count: pl.BlockSpec((count, step, length), lambda i: (0, i, 0))
    out_shape = jax.ShapeDtypeStruct((size, 4 * octet, length), jnp.float32)
    params = pltpu.CompilerParams(vmem_limit_bytes=VMEM_BYTES)
    first = pl.pallas_call(
        first_rows_kernel,
        out_shape=out_shape,
        grid=(size // step,),
        in_specs=[over(octet), over(octet - 1), over(2), over(octet)],
        out_specs=pl.BlockSpec((step, 3 * octet, length), lambda i: (i, 0, 0)),
        compiler_params=params,
        name="first_rows",
    )(high, low, edge, high_mirror)
    return pl.pallas_call(
        last_rows_kernel,
        out_shape=out_shape,
        grid=(size // step,),
        in_specs=[
            pl.BlockSpec(memory_space=pl.ANY),
            pl.BlockSpec((1, step, length), lambda i: (octet - 1, i, 0)),
            over(octet - 1),
        ],
        out_specs=pl.BlockSpec((step, octet, length), lambda i: (i, 3, 0)),
        input_output_aliases={0: 0},
        compiler_params=params,
        name="last_rows",
    )(first, high_mirror, low_mirror)


def body(heights):
    frames, rows_dev, length = heights.shape
    tm_count = lax.axis_size("tm")
    rows_count = lax.axis_size("rows")
    devices = tm_count * rows_count
    owned = length // devices
    half = owned // 2
    windows, energy = window_table(frames, tm_count - 1)
    scale = 1.0 / ((tm_count - 1) * energy)
    tables = (x_table(length), windows, reversal(2 * frames), reversal(length))
    tables = tuple(jnp.asarray(table) for table in tables)
    opposite = [(device, devices - 1 - device) for device in range(devices)]

    def arrive(slots):
        wavenumbers = (np.arange(devices)[:, None] * owned + np.asarray(slots)[None, :]).reshape(-1)
        mixed = row_transform(heights, jnp.asarray(y_table(length, wavenumbers)))
        mixed = mixed.reshape(devices, len(slots), 2, frames, rows_dev)
        got = lax.all_to_all(mixed, AXES, split_axis=0, concat_axis=0, tiled=True)
        return got.reshape(tm_count, rows_count, len(slots), 2, frames, rows_dev)

    high_pieces = arrive(range(half // 2, half))
    low_pieces = arrive(range(1, half // 2))
    edge_pieces = arrive([0, half])
    high, high_mirror = spectrum(high_pieces, tables, scale, True)
    high_mirror = lax.ppermute(high_mirror, AXES, opposite)
    low, low_mirror = spectrum(low_pieces, tables, scale, True)
    low_mirror = lax.ppermute(low_mirror, AXES, opposite)
    (edge,) = spectrum(edge_pieces, tables, scale, False)
    return assemble(high, low, edge, high_mirror, low_mirror)


def solution(mesh):
    in_specs = (P("tm", "rows", None),)
    out_specs = P(None, ("tm", "rows"), None)
    return jax.shard_map(body, mesh=mesh, in_specs=in_specs, out_specs=out_specs, check_vma=False)
```

time: 1070 us -> 334 us (0.31); the launches traced: 1060 us -> 333 us
  waiting for transfers between devices: 541 us -> 185 us
  local copies, waits for them, and re-layouts: 182 us -> 2.88 us
  matrix products: 173 us -> 0 us
  other arithmetic: 146 us -> 0 us
  Pallas kernels: 0 us -> 120 us
  starting transfers between devices: 13.6 us -> 25.3 us
    all_to_all x2 -> x3, waiting for transfers between devices: 541 us -> 150 us  [arrive(): got = lax.all_to_all(mixed, AXES, split_axis=0, concat_axis=0, tiled=True)]
    dot_general x41 -> x0, matrix products: 173 us -> none  [the longest x16 76 us: column_one_block(): jnp.einsum('fxc,xk->fck', frame_block, col_table, preferred_element_type=...]
    pallas_call x0 -> x8, Pallas kernels: none -> 120 us  [the longest x3 78.6 us: spectrum(): pl.pallas_call(functools.partial(spectrum_kernel, scale, mirrored), out_s...]
    dynamic_update_slice x28 -> x0, other arithmetic: 47.5 us -> none  [the longest x12 30.4 us: window_one_block(): lax.dynamic_update_slice_in_dim(accumulated, real_part * real_part + imag...]
    all_to_all x2 -> x0, local copies, waits for them, and re-layouts: 39.4 us -> none  [the longest x1 23.7 us: body(): lax.all_to_all(mixed_rows, 'rows', split_axis=2, concat_axis=1, tiled=True)]
    convert_element_type x2 -> x0, other arithmetic: 38.7 us -> none  [the longest x1 36 us: spatial_table(): return (values / math.sqrt(length)).astype(jnp.bfloat16)]
    dynamic_slice x32 -> x0, local copies, waits for them, and re-layouts: 38.4 us -> none  [column_modes(): lax.map(column_one_block, mixed_rows.reshape(number // block_size, block_...]
    ppermute x0 -> x2, waiting for transfers between devices: none -> 35.4 us  [the longest x1 23.3 us: body(): high_mirror = lax.ppermute(high_mirror, AXES, opposite)]
  transfers between devices with their start and end apart: 2 -> 5, of which waited for: 2 -> 4; matrix products, arithmetic and copies ran while one was open for 0% -> 0% of each run, Pallas kernels for 0% -> 31%
where the time goes in v1:
time: 334 us; the launch traced here: 333 us
  waiting for transfers between devices  185 us (55%)
  Pallas kernels  120 us (36%)
  starting transfers between devices  25.3 us (8%)
    all_to_all x3, waiting for transfers between devices, arrive(): got = lax.all_to_all(mixed, AXES, split_axis=0, concat_axis=0, tiled=True)  150 us
    pallas_call x3, Pallas kernels, spectrum(): pl.pallas_call(functools.partial(spectrum_kernel, scale, mirrored), out_s...  78.6 us
    pallas_call x3, Pallas kernels, row_transform(): pl.pallas_call(row_transform_kernel, out_shape=jax.ShapeDtypeStruct((colu...  31.7 us
    ppermute x1, waiting for transfers between devices, body(): high_mirror = lax.ppermute(high_mirror, AXES, opposite)  23.3 us
    all_to_all x3, starting transfers between devices, arrive(): got = lax.all_to_all(mixed, AXES, split_axis=0, concat_axis=0, tiled=True)  21.7 us
    ppermute x1, waiting for transfers between devices, body(): low_mirror = lax.ppermute(low_mirror, AXES, opposite)  12.1 us
  transfers between devices with their start and end apart: 5, of which 4 were waited for; matrix products, arithmetic and copies ran while one was open for 0% of the time, Pallas kernels for 31%

profile of v1, /device:TPU:13, one launch (start us, length us, event | category | flops | bytes accessed | tf_op | source)
XLA Modules:
  0.0 333.4 jit_solution(4640210480739974020)
XLA Ops:
  0.0 11.7 %row_transform.4 = bf16[448,32,128]{2,1,0:T(8,128)(2,1)} custom-call(bf16[448,1024]{1,0:T(8,128)(2,1)} %constant.19.clone.table_ref, bf16[32,128,1024]{2,1,0:T(8,128)(2,1)} %heights_ref.5), custom_call_target="tpu_custom_call" | custom-call | flops 3758096384 | bytes 12976128 | tf_op jit(solution)/shard_map/row_transform/pallas_call | solution.py:86
  11.7 6.3 %all-to-all-start.1 = ((bf16[32,7,2,32,128]{4,3,2,1,0:T(8,128)(2,1)}), bf16[32,7,2,32,128]{4,3,2,1,0:T(8,128)(2,1)}, u32[]{:S(2)}, u32[]{:S(2)}) async-start(bf16[32,7,2,32,128]{4,3,2,1,0:T(8,128)(2,1)} %bitcast.8), calls=%async_computation.1 | async-start | bytes 7340032 | tf_op jit(solution)/shard_map/all_to_all | solution.py:264
  18.1 12.9 %row_transform.3 = bf16[512,32,128]{2,1,0:T(8,128)(2,1)} custom-call(bf16[512,1024]{1,0:T(8,128)(2,1)} %constant.18.clone.table_ref, bf16[32,128,1024]{2,1,0:T(8,128)(2,1)} %heights_ref.5), custom_call_target="tpu_custom_call" | custom-call | flops 4294967296 | bytes 13631488 | tf_op jit(solution)/shard_map/row_transform/pallas_call | solution.py:86
  30.9 66.4 %all-to-all-done.1 = bf16[32,7,2,32,128]{4,3,2,1,0:T(8,128)(2,1)} async-done(((bf16[32,7,2,32,128]{4,3,2,1,0:T(8,128)(2,1)}), bf16[32,7,2,32,128]{4,3,2,1,0:T(8,128)(2,1)}, u32[]{:S(2)}, u32[]{:S(2)}) %all-to-all-start.1) | async-done | bytes 3670048 | tf_op jit(solution)/shard_map/all_to_all | solution.py:264
  97.4 8.1 %all-to-all-start = ((bf16[32,8,2,32,128]{4,3,2,1,0:T(8,128)(2,1)}), bf16[32,8,2,32,128]{4,3,2,1,0:T(8,128)(2,1)}, u32[]{:S(2)}, u32[]{:S(2)}) async-start(bf16[32,8,2,32,128]{4,3,2,1,0:T(8,128)(2,1)} %bitcast.7), calls=%async_computation | async-start | bytes 8388608 | tf_op jit(solution)/shard_map/all_to_all | solution.py:264
  105.4 7.1 %row_transform.5 = bf16[128,32,128]{2,1,0:T(8,128)(2,1)} custom-call(bf16[128,1024]{1,0:T(8,128)(2,1)} %constant.20.clone.table_ref, bf16[32,128,1024]{2,1,0:T(8,128)(2,1)} %heights_ref.5), custom_call_target="tpu_custom_call" | custom-call | flops 1073741824 | bytes 9699328 | tf_op jit(solution)/shard_map/row_transform/pallas_call | solution.py:86
  112.6 83.3 %all-to-all-done = bf16[32,8,2,32,128]{4,3,2,1,0:T(8,128)(2,1)} async-done(((bf16[32,8,2,32,128]{4,3,2,1,0:T(8,128)(2,1)}), bf16[32,8,2,32,128]{4,3,2,1,0:T(8,128)(2,1)}, u32[]{:S(2)}, u32[]{:S(2)}) %all-to-all-start) | async-done | bytes 4194336 | tf_op jit(solution)/shard_map/all_to_all | solution.py:264
  195.9 7.3 %all-to-all-start.2 = ((bf16[32,2,2,32,128]{4,3,2,1,0:T(8,128)(2,1)}), bf16[32,2,2,32,128]{4,3,2,1,0:T(8,128)(2,1)S(1)}, u32[]{:S(2)}, u32[]{:S(2)}) async-start(bf16[32,2,2,32,128]{4,3,2,1,0:T(8,128)(2,1)} %bitcast.6), calls=%async_computation.2 | async-start | bytes 2097152 | tf_op jit(solution)/shard_map/all_to_all | solution.py:264
  203.3 36.5 %spectrum.3 = (f32[8,64,1024]{2,1,0:T(8,128)}, bf16[8,64,1024]{2,1,0:T(8,128)(2,1)}) custom-call(bf16[4,8,8,2,32,128]{5,4,3,2,1,0:T(8,128)(2,1)} %bitcast.1.refs_0_, bf16[1024,2048]{1,0:T(8,128)(2,1)} %constant.14.clone.refs_1_, bf16[384,256]{1,0:T(8,128)(2,1)} %constant.15.clone.refs_2_, bf16[64,64]{1,0:T(8,128)(2,1)} %constant.16.clone.refs_3_, ...), custom_call_target="tpu_custom_call" | custom-call | flops 10200547328 | bytes 7340032 | tf_op jit(solution)/shard_map/spectrum/pallas_call | solution.py:179
  239.8 2.4 collective-permute-start
  242.2 32.4 %spectrum.4 = (f32[7,64,1024]{2,1,0:T(8,128)}, bf16[7,64,1024]{2,1,0:T(8,128)(2,1)}) custom-call(bf16[4,8,7,2,32,128]{5,4,3,2,1,0:T(8,128)(2,1)} %bitcast.3.refs_0_, bf16[1024,2048]{1,0:T(8,128)(2,1)} %constant.14.clone.refs_1_, bf16[384,256]{1,0:T(8,128)(2,1)} %constant.15.clone.refs_2_, bf16[64,64]{1,0:T(8,128)(2,1)} %constant.16.clone.refs_3_, ...), custom_call_target="tpu_custom_call" | custom-call | flops 8925478912 | bytes 6422528 | tf_op jit(solution)/shard_map/spectrum/pallas_call | solution.py:179
  274.6 1.2 collective-permute-start.1
  275.8 0.0 all-to-all-done.2
  275.8 0.0 copy-start.1
  275.8 1.0 copy-done.1
  276.8 9.6 %spectrum.5.edge_ref = f32[2,64,1024]{2,1,0:T(8,128)} custom-call(bf16[4,8,2,2,32,128]{5,4,3,2,1,0:T(8,128)(2,1)} %bitcast.9, bf16[1024,2048]{1,0:T(8,128)(2,1)} %constant.14.clone.refs_1_, bf16[384,256]{1,0:T(8,128)(2,1)} %constant.15.clone.refs_2_), custom_call_target="tpu_custom_call" | custom-call | flops 2550136832 | bytes 1835008 | tf_op jit(solution)/shard_map/spectrum/pallas_call | solution.py:179
  286.4 23.3 %collective-permute-done.mirror_ref.high_ref = bf16[8,64,1024]{2,1,0:T(8,128)(2,1)S(1)} collective-permute-done((bf16[8,64,1024]{2,1,0:T(8,128)(2,1)}, bf16[8,64,1024]{2,1,0:T(8,128)(2,1)S(1)}, u32[]{:S(2)}, u32[]{:S(2)}) %collective-permute-start) | collective-permute-done | bytes 1048608 | tf_op jit(solution)/shard_map/ppermute | solution.py:271
  309.7 0.0 copy-start
  309.7 1.0 copy-done
  310.7 6.0 %first_rows.1.given_ref = f32[64,32,1024]{2,1,0:T(8,128)} custom-call(f32[8,64,1024]{2,1,0:T(8,128)} %get-tuple-element.9.high_ref, f32[7,64,1024]{2,1,0:T(8,128)} %get-tuple-element.10.low_ref, f32[2,64,1024]{2,1,0:T(8,128)} %spectrum.5.edge_ref, bf16[8,64,1024]{2,1,0:T(8,128)(2,1)} %copy-done), custom_call_target="tpu_custom_call" | custom-call | tf_op jit(solution)/shard_map/first_rows/pallas_call | solution.py:222
  316.7 12.1 %collective-permute-done.1.low_ref = bf16[7,64,1024]{2,1,0:T(8,128)(2,1)S(1)} collective-permute-done((bf16[7,64,1024]{2,1,0:T(8,128)(2,1)}, bf16[7,64,1024]{2,1,0:T(8,128)(2,1)S(1)}, u32[]{:S(2)}, u32[]{:S(2)}) %collective-permute-start.1) | collective-permute-done | bytes 917536 | tf_op jit(solution)/shard_map/ppermute | solution.py:273
  328.7 0.0 copy-start.2
  328.7 0.9 copy-done.2
  329.6 3.8 %last_rows.1 = f32[64,32,1024]{2,1,0:T(8,128)} custom-call(f32[64,32,1024]{2,1,0:T(8,128)} %first_rows.1.given_ref, bf16[8,64,1024]{2,1,0:T(8,128)(2,1)} %copy-done, bf16[7,64,1024]{2,1,0:T(8,128)(2,1)} %copy-done.2), custom_call_target="tpu_custom_call", output_to_operand_aliasing={{}: (0, {})} | custom-call | tf_op jit(solution)/shard_map/last_rows/pallas_call | solution.py:231
Async XLA Ops:
  11.7 85.7 %all-to-all-start.1 = ((bf16[32,7,2,32,128]{4,3,2,1,0:T(8,128)(2,1)}), bf16[32,7,2,32,128]{4,3,2,1,0:T(8,128)(2,1)}, u32[]{:S(2)}, u32[]{:S(2)}) async-start(bf16[32,7,2,32,128]{4,3,2,1,0:T(8,128)(2,1)} %bitcast.8), calls=%async_computation.1 | async-start | bytes 7340032 | tf_op jit(solution)/shard_map/all_to_all | solution.py:264
  97.4 98.5 %all-to-all-start = ((bf16[32,8,2,32,128]{4,3,2,1,0:T(8,128)(2,1)}), bf16[32,8,2,32,128]{4,3,2,1,0:T(8,128)(2,1)}, u32[]{:S(2)}, u32[]{:S(2)}) async-start(bf16[32,8,2,32,128]{4,3,2,1,0:T(8,128)(2,1)} %bitcast.7), calls=%async_computation | async-start | bytes 8388608 | tf_op jit(solution)/shard_map/all_to_all | solution.py:264
  195.9 79.9 %all-to-all-start.2 = ((bf16[32,2,2,32,128]{4,3,2,1,0:T(8,128)(2,1)}), bf16[32,2,2,32,128]{4,3,2,1,0:T(8,128)(2,1)S(1)}, u32[]{:S(2)}, u32[]{:S(2)}) async-start(bf16[32,2,2,32,128]{4,3,2,1,0:T(8,128)(2,1)} %bitcast.6), calls=%async_computation.2 | async-start | bytes 2097152 | tf_op jit(solution)/shard_map/all_to_all | solution.py:264
  239.8 69.9 %collective-permute-start = (bf16[8,64,1024]{2,1,0:T(8,128)(2,1)}, bf16[8,64,1024]{2,1,0:T(8,128)(2,1)S(1)}, u32[]{:S(2)}, u32[]{:S(2)}) collective-permute-start(bf16[8,64,1024]{2,1,0:T(8,128)(2,1)} %get-tuple-element.11), channel_id=1, source_target_pairs={{0,31},{1,30},{2,29},{3,28},{4,27},{5,26},{6,25},{7,24},{8,23},{9,... | collective-permute-start | bytes 3145736 | tf_op jit(solution)/shard_map/ppermute | solution.py:271
  274.6 54.1 %collective-permute-start.1 = (bf16[7,64,1024]{2,1,0:T(8,128)(2,1)}, bf16[7,64,1024]{2,1,0:T(8,128)(2,1)S(1)}, u32[]{:S(2)}, u32[]{:S(2)}) collective-permute-start(bf16[7,64,1024]{2,1,0:T(8,128)(2,1)} %get-tuple-element.12), channel_id=1, source_target_pairs={{0,31},{1,30},{2,29},{3,28},{4,27},{5,26},{6,25},{7,24},{8,23},{9,... | collective-permute-start | bytes 2752520 | tf_op jit(solution)/shard_map/ppermute | solution.py:273
  275.8 1.0 copy-start.1
  309.7 1.0 copy-start
  328.7 0.9 copy-start.2

commit v2 on v1

--- a/solution.py
+++ b/solution.py
@@ -13,6 +13,9 @@
 AXES = ("tm", "rows")
 LANES = 128
 TILE = 8
+SHARES = (4, 10, 15)
+SMALL = pl.CostEstimate(flops=1 << 20, bytes_accessed=1 << 20, transcendentals=0)
+LARGE = pl.CostEstimate(flops=1 << 40, bytes_accessed=1 << 20, transcendentals=0)
 VMEM_BYTES = 56 * 1024 * 1024
 
 
@@ -94,11 +97,7 @@
         out_specs=pl.BlockSpec((columns, step, rows), lambda i: (0, i, 0)),
         scratch_shapes=[pltpu.VMEM((columns, step, rows), jnp.float32)],
         compiler_params=pltpu.CompilerParams(vmem_limit_bytes=VMEM_BYTES),
-        cost_estimate=pl.CostEstimate(
-            flops=2 * columns * frames * rows * length,
-            bytes_accessed=2 * (heights.size + columns * length + columns * frames * rows),
-            transcendentals=0,
-        ),
+        cost_estimate=SMALL,
         name="row_transform",
     )(table, heights)
 
@@ -184,64 +183,65 @@
         out_specs=out_specs,
         scratch_shapes=scratch_shapes,
         compiler_params=pltpu.CompilerParams(vmem_limit_bytes=VMEM_BYTES),
-        cost_estimate=pl.CostEstimate(
-            flops=number * 2 * length * (4 * blocks * frames * length + windows.size),
-            bytes_accessed=2 * pieces.size + 6 * number * size * length,
-            transcendentals=0,
-        ),
+        cost_estimate=LARGE,
         name="spectrum",
     )(*operands)
 
 
-def turned(planes):
-    return jnp.swapaxes(jnp.stack([plane.astype(jnp.float32) for plane in planes], 0), 0, 1)
-
-
-def first_rows_kernel(high_ref, low_ref, edge_ref, mirror_ref, out_ref):
-    octet = low_ref.shape[0] + 1
-    out_ref[:, :octet] = turned([edge_ref[0]] + [low_ref[i] for i in range(octet - 1)])
-    out_ref[:, octet : 2 * octet] = turned([high_ref[i] for i in range(octet)])
-    out_ref[:, 2 * octet :] = turned([edge_ref[1]] + [mirror_ref[i] for i in range(octet - 1)])
-
-
-def last_rows_kernel(given_ref, high_ref, low_ref, out_ref):
-    del given_ref
-    octet = low_ref.shape[0] + 1
-    out_ref[...] = turned([high_ref[0]] + [low_ref[i] for i in range(octet - 1)])
-
-
-def assemble(high, low, edge, high_mirror, low_mirror):
-    octet, size, length = high.shape
-    if octet % TILE:
-        planes = [edge[:1], low, high, edge[1:], high_mirror, low_mirror]
-        return jnp.concatenate([plane.astype(jnp.float32) for plane in planes], 0).transpose(1, 0, 2)
+def rows_kernel(places, aliased, *refs):
+    planes, out_ref = refs[aliased:-1], refs[-1]
+    for at in range(0, len(places), TILE):
+        stack = [planes[which][plane].astype(jnp.float32) for which, plane in places[at : at + TILE]]
+        out_ref[:, at : at + TILE] = jnp.swapaxes(jnp.stack(stack, 0), 0, 1)
+
+
+def write_rows(given, arrays, places, start, total):
+    _, size, length = arrays[0].shape
     step = 16
-    over = lambda count: pl.BlockSpec((count, step, length), lambda i: (0, i, 0))
-    out_shape = jax.ShapeDtypeStruct((size, 4 * octet, length), jnp.float32)
-    params = pltpu.CompilerParams(vmem_limit_bytes=VMEM_BYTES)
-    first = pl.pallas_call(
-        first_rows_kernel,
-        out_shape=out_shape,
+    used = sorted({which for which, _ in places})
+    places = [(used.index(which), plane) for which, plane in places]
+    block = start // len(places)
+    return pl.pallas_call(
+        functools.partial(rows_kernel, places, len(given)),
+        out_shape=jax.ShapeDtypeStruct((size, total, length), jnp.float32),
         grid=(size // step,),
-        in_specs=[over(octet), over(octet - 1), over(2), over(octet)],
-        out_specs=pl.BlockSpec((step, 3 * octet, length), lambda i: (i, 0, 0)),
-        compiler_params=params,
-        name="first_rows",
-    )(high, low, edge, high_mirror)
-    return pl.pallas_call(
-        last_rows_kernel,
-        out_shape=out_shape,
-        grid=(size // step,),
-        in_specs=[
-            pl.BlockSpec(memory_space=pl.ANY),
-            pl.BlockSpec((1, step, length), lambda i: (octet - 1, i, 0)),
-            over(octet - 1),
+        in_specs=[pl.BlockSpec(memory_space=pl.ANY)] * len(given)
+        + [
+            pl.BlockSpec((arrays[which].shape[0], step, length), lambda i: (0, i, 0))
+            for which in used
         ],
-        out_specs=pl.BlockSpec((step, octet, length), lambda i: (i, 3, 0)),
-        input_output_aliases={0: 0},
-        compiler_params=params,
-        name="last_rows",
-    )(first, high_mirror, low_mirror)
+        out_specs=pl.BlockSpec((step, len(places), length), lambda i: (i, block, 0)),
+        input_output_aliases={0: 0} if given else {},
+        compiler_params=pltpu.CompilerParams(vmem_limit_bytes=VMEM_BYTES),
+        name="write_rows",
+    )(*given, *[arrays[which] for which in used])
+
+
+def assemble(slots, planes, images):
+    half = max(max(slot) for slot in slots)
+    total = 2 * half
+    arrays = planes + images
+    places = [None] * total
+    for which, slot in enumerate(slots):
+        for plane, row in enumerate(slot):
+            places[row] = (which, plane)
+            if which < len(images):
+                places[total - row] = (len(planes) + which, len(slot) - 1 - plane)
+    late = min(row for row in range(total) if places[row][0] == len(arrays) - 1)
+    late -= late % TILE
+    while late % (total - late):
+        late -= TILE
+    given = []
+    if late:
+        given.append(write_rows([], arrays, places[:late], 0, total))
+    return write_rows(given, arrays, places[late:], late, total)
+
+
+def split_rows(half):
+    rows = list(range(half - 1, 0, -1))
+    parts = [len(rows) * share // 15 for share in SHARES]
+    slots = [sorted(rows[lo:hi]) for lo, hi in zip([0] + parts, parts) if hi > lo]
+    return slots + [[0, half]]
 
 
 def body(heights):
@@ -250,29 +250,35 @@
     rows_count = lax.axis_size("rows")
     devices = tm_count * rows_count
     owned = length // devices
-    half = owned // 2
     windows, energy = window_table(frames, tm_count - 1)
     scale = 1.0 / ((tm_count - 1) * energy)
     tables = (x_table(length), windows, reversal(2 * frames), reversal(length))
     tables = tuple(jnp.asarray(table) for table in tables)
     opposite = [(device, devices - 1 - device) for device in range(devices)]
 
-    def arrive(slots):
-        wavenumbers = (np.arange(devices)[:, None] * owned + np.asarray(slots)[None, :]).reshape(-1)
+    def mix(heights, slot):
+        wavenumbers = (np.arange(devices)[:, None] * owned + np.asarray(slot)[None, :]).reshape(-1)
         mixed = row_transform(heights, jnp.asarray(y_table(length, wavenumbers)))
-        mixed = mixed.reshape(devices, len(slots), 2, frames, rows_dev)
+        return mixed.reshape(devices, len(slot), 2, frames, rows_dev)
+
+    def arrive(mixed):
         got = lax.all_to_all(mixed, AXES, split_axis=0, concat_axis=0, tiled=True)
-        return got.reshape(tm_count, rows_count, len(slots), 2, frames, rows_dev)
-
-    high_pieces = arrive(range(half // 2, half))
-    low_pieces = arrive(range(1, half // 2))
-    edge_pieces = arrive([0, half])
-    high, high_mirror = spectrum(high_pieces, tables, scale, True)
-    high_mirror = lax.ppermute(high_mirror, AXES, opposite)
-    low, low_mirror = spectrum(low_pieces, tables, scale, True)
-    low_mirror = lax.ppermute(low_mirror, AXES, opposite)
-    (edge,) = spectrum(edge_pieces, tables, scale, False)
-    return assemble(high, low, edge, high_mirror, low_mirror)
+        return got.reshape((tm_count, rows_count) + mixed.shape[1:])
+
+    slots = split_rows(owned // 2)
+    pieces = [arrive(mix(heights, slot)) for slot in slots[:2]]
+    planes, images = [], []
+    for at in range(len(slots) - 1):
+        if images:
+            pieces[at], images[-1] = lax.optimization_barrier((pieces[at], images[-1]))
+        plane, image = spectrum(pieces[at], tables, scale, True)
+        if at + 2 < len(slots):
+            plane, image, later = lax.optimization_barrier((plane, image, heights))
+            pieces.append(arrive(mix(later, slots[at + 2])))
+        planes.append(plane)
+        images.append(lax.ppermute(image, AXES, opposite))
+    planes += spectrum(pieces[-1], tables, scale, False)
+    return assemble(slots, planes, images)
 
 
 def solution(mesh):

time: 334 us -> 313 us (0.937)
  waiting for transfers between devices: 185 us -> 144 us
  starting transfers between devices: 25.3 us -> 37.5 us
  Pallas kernels: 120 us -> 128 us
    all_to_all x3 -> x4, waiting for transfers between devices: 150 us -> 110 us  [arrive(): got = lax.all_to_all(mixed, AXES, split_axis=0, concat_axis=0, tiled=True)]
    all_to_all x3 -> x4, starting transfers between devices: 21.7 us -> 30.4 us  [arrive(): got = lax.all_to_all(mixed, AXES, split_axis=0, concat_axis=0, tiled=True)]
    pallas_call x3 -> x4, Pallas kernels: 78.6 us -> 83 us  [spectrum(): pl.pallas_call(functools.partial(spectrum_kernel, scale, mirrored), out_s...]
    ppermute x2 -> x3, starting transfers between devices: 3.56 us -> 7.02 us  [body(): images.append(lax.ppermute(image, AXES, opposite))]
    pallas_call x3 -> x4, Pallas kernels: 31.7 us -> 35.1 us  [row_transform(): pl.pallas_call(row_transform_kernel, out_shape=jax.ShapeDtypeStruct((colu...]
    ppermute x2 -> x3, waiting for transfers between devices: 35.4 us -> 34.1 us  [body(): images.append(lax.ppermute(image, AXES, opposite))]
  transfers between devices with their start and end apart: 5 -> 7, of which waited for: 4 -> 6; matrix products, arithmetic and copies ran while one was open for 0% -> 0% of each run, Pallas kernels for 31% -> 37%
where the time goes in v2:
time: 313 us; the launch traced here: 311 us
  waiting for transfers between devices  144 us (46%)
  Pallas kernels  128 us (41%)
  starting transfers between devices  37.5 us (12%)
    all_to_all x4, waiting for transfers between devices, arrive(): got = lax.all_to_all(mixed, AXES, split_axis=0, concat_axis=0, tiled=True)  110 us
    pallas_call x4, Pallas kernels, spectrum(): pl.pallas_call(functools.partial(spectrum_kernel, scale, mirrored), out_s...  83 us
    pallas_call x4, Pallas kernels, row_transform(): pl.pallas_call(row_transform_kernel, out_shape=jax.ShapeDtypeStruct((colu...  35.1 us
    ppermute x3, waiting for transfers between devices, body(): images.append(lax.ppermute(image, AXES, opposite))  34.1 us
    all_to_all x4, starting transfers between devices, arrive(): got = lax.all_to_all(mixed, AXES, split_axis=0, concat_axis=0, tiled=True)  30.4 us
    pallas_call x2, Pallas kernels, write_rows(): pl.pallas_call(functools.partial(rows_kernel, places, len(given)), out_sh...  9.95 us
    ppermute x3, starting transfers between devices, body(): images.append(lax.ppermute(image, AXES, opposite))  7.02 us
  transfers between devices with their start and end apart: 7, of which 6 were waited for; matrix products, arithmetic and copies ran while one was open for 0% of the time, Pallas kernels for 37%

profile of v2, /device:TPU:13, one launch (start us, length us, event | category | flops | bytes accessed | tf_op | source)
XLA Modules:
  0.0 311.0 jit_solution(12253721511519472842)
XLA Ops:
  0.0 8.1 %row_transform.4 = bf16[256,32,128]{2,1,0:T(8,128)(2,1)} custom-call(bf16[256,1024]{1,0:T(8,128)(2,1)} %constant.20.clone.table_ref, bf16[32,128,1024]{2,1,0:T(8,128)(2,1)} %heights_ref.5), custom_call_target="tpu_custom_call" | custom-call | flops 1048576 | bytes 1048576 | tf_op jit(solution)/shard_map/row_transform/pallas_call | solution.py:89
  8.1 6.3 %all-to-all-start = ((bf16[32,4,2,32,128]{4,3,2,1,0:T(8,128)(2,1)}), bf16[32,4,2,32,128]{4,3,2,1,0:T(8,128)(2,1)S(1)}, u32[]{:S(2)}, u32[]{:S(2)}) async-start(bf16[32,4,2,32,128]{4,3,2,1,0:T(8,128)(2,1)} %bitcast.10), calls=%async_computation | async-start | bytes 4194304 | tf_op jit(solution)/shard_map/all_to_all | solution.py:265
  14.4 10.5 %row_transform.5 = bf16[384,32,128]{2,1,0:T(8,128)(2,1)} custom-call(bf16[384,1024]{1,0:T(8,128)(2,1)} %constant.21.clone.table_ref, bf16[32,128,1024]{2,1,0:T(8,128)(2,1)} %heights_ref.5), custom_call_target="tpu_custom_call" | custom-call | flops 1048576 | bytes 1048576 | tf_op jit(solution)/shard_map/row_transform/pallas_call | solution.py:89
  24.9 35.1 %all-to-all-done = bf16[32,4,2,32,128]{4,3,2,1,0:T(8,128)(2,1)S(1)} async-done(((bf16[32,4,2,32,128]{4,3,2,1,0:T(8,128)(2,1)}), bf16[32,4,2,32,128]{4,3,2,1,0:T(8,128)(2,1)S(1)}, u32[]{:S(2)}, u32[]{:S(2)}) %all-to-all-start) | async-done | bytes 2097184 | tf_op jit(solution)/shard_map/all_to_all | solution.py:265
  60.1 0.0 copy-start.1
  60.1 1.4 copy-done.1
  61.4 7.9 %all-to-all-start.1 = ((bf16[32,6,2,32,128]{4,3,2,1,0:T(8,128)(2,1)}), bf16[32,6,2,32,128]{4,3,2,1,0:T(8,128)(2,1)}, u32[]{:S(2)}, u32[]{:S(2)}) async-start(bf16[32,6,2,32,128]{4,3,2,1,0:T(8,128)(2,1)} %bitcast.8), calls=%async_computation.1 | async-start | bytes 6291456 | tf_op jit(solution)/shard_map/all_to_all | solution.py:265
  69.3 20.3 %spectrum.4 = (f32[4,64,1024]{2,1,0:T(8,128)}, bf16[4,64,1024]{2,1,0:T(8,128)(2,1)}) custom-call(bf16[4,8,4,2,32,128]{5,4,3,2,1,0:T(8,128)(2,1)} %bitcast.12, bf16[1024,2048]{1,0:T(8,128)(2,1)} %constant.16.clone.refs_1_, bf16[384,256]{1,0:T(8,128)(2,1)} %constant.17.clone.refs_2_, bf16[64,64]{1,0:T(8,128)(2,1)} %constant.18.clone.refs_3_, ...), custom_call_target="tpu_custom_call" | custom-call | flops 1099511627776 | bytes 1048576 | tf_op jit(solution)/shard_map/spectrum/pallas_call | solution.py:178
  89.6 2.4 collective-permute-start
  92.0 9.4 %row_transform.6 = bf16[320,32,128]{2,1,0:T(8,128)(2,1)} custom-call(bf16[320,1024]{1,0:T(8,128)(2,1)} %constant.22.clone.table_ref, bf16[32,128,1024]{2,1,0:T(8,128)(2,1)} %heights_ref.5), custom_call_target="tpu_custom_call" | custom-call | flops 1048576 | bytes 1048576 | tf_op jit(solution)/shard_map/row_transform/pallas_call | solution.py:89
  101.4 47.2 %all-to-all-done.1 = bf16[32,6,2,32,128]{4,3,2,1,0:T(8,128)(2,1)} async-done(((bf16[32,6,2,32,128]{4,3,2,1,0:T(8,128)(2,1)}), bf16[32,6,2,32,128]{4,3,2,1,0:T(8,128)(2,1)}, u32[]{:S(2)}, u32[]{:S(2)}) %all-to-all-start.1) | async-done | bytes 3145760 | tf_op jit(solution)/shard_map/all_to_all | solution.py:265
  148.6 8.2 %all-to-all-start.2 = ((bf16[32,5,2,32,128]{4,3,2,1,0:T(8,128)(2,1)}), bf16[32,5,2,32,128]{4,3,2,1,0:T(8,128)(2,1)}, u32[]{:S(2)}, u32[]{:S(2)}) async-start(bf16[32,5,2,32,128]{4,3,2,1,0:T(8,128)(2,1)} %bitcast.9), calls=%async_computation.2 | async-start | bytes 5242880 | tf_op jit(solution)/shard_map/all_to_all | solution.py:265
  156.7 9.3 %collective-permute-done.refs_4_ = bf16[4,64,1024]{2,1,0:T(8,128)(2,1)S(1)} collective-permute-done((bf16[4,64,1024]{2,1,0:T(8,128)(2,1)}, bf16[4,64,1024]{2,1,0:T(8,128)(2,1)S(1)}, u32[]{:S(2)}, u32[]{:S(2)}) %collective-permute-start) | collective-permute-done | bytes 524320 | tf_op jit(solution)/shard_map/ppermute | solution.py:279
  166.0 0.0 copy-start.2
  166.0 28.5 %spectrum.5 = (f32[6,64,1024]{2,1,0:T(8,128)}, bf16[6,64,1024]{2,1,0:T(8,128)(2,1)}) custom-call(bf16[4,8,6,2,32,128]{5,4,3,2,1,0:T(8,128)(2,1)} %bitcast.3.refs_0_, bf16[1024,2048]{1,0:T(8,128)(2,1)} %constant.16.clone.refs_1_, bf16[384,256]{1,0:T(8,128)(2,1)} %constant.17.clone.refs_2_, bf16[64,64]{1,0:T(8,128)(2,1)} %constant.18.clone.refs_3_, ...), custom_call_target="tpu_custom_call" | custom-call | flops 1099511627776 | bytes 1048576 | tf_op jit(solution)/shard_map/spectrum/pallas_call | solution.py:178
  194.5 0.0 copy-done.2
  194.5 3.5 %collective-permute-start.1 = (bf16[6,64,1024]{2,1,0:T(8,128)(2,1)}, bf16[6,64,1024]{2,1,0:T(8,128)(2,1)S(1)}, u32[]{:S(2)}, u32[]{:S(2)}) collective-permute-start(bf16[6,64,1024]{2,1,0:T(8,128)(2,1)} %get-tuple-element.30), channel_id=1, source_target_pairs={{0,31},{1,30},{2,29},{3,28},{4,27},{5,26},{6,25},{7,24},{8,23},{9,... | collective-permute-start | bytes 2359304 | tf_op jit(solution)/shard_map/ppermute | solution.py:279
  198.1 7.1 %row_transform.7 = bf16[128,32,128]{2,1,0:T(8,128)(2,1)} custom-call(bf16[128,1024]{1,0:T(8,128)(2,1)} %constant.23.clone.table_ref, bf16[32,128,1024]{2,1,0:T(8,128)(2,1)} %heights_ref.5), custom_call_target="tpu_custom_call" | custom-call | flops 1048576 | bytes 1048576 | tf_op jit(solution)/shard_map/row_transform/pallas_call | solution.py:89
  205.2 27.7 %all-to-all-done.2 = bf16[32,5,2,32,128]{4,3,2,1,0:T(8,128)(2,1)} async-done(((bf16[32,5,2,32,128]{4,3,2,1,0:T(8,128)(2,1)}), bf16[32,5,2,32,128]{4,3,2,1,0:T(8,128)(2,1)}, u32[]{:S(2)}, u32[]{:S(2)}) %all-to-all-start.2) | async-done | bytes 2621472 | tf_op jit(solution)/shard_map/all_to_all | solution.py:265
  232.8 8.1 %all-to-all-start.3 = ((bf16[32,2,2,32,128]{4,3,2,1,0:T(8,128)(2,1)}), bf16[32,2,2,32,128]{4,3,2,1,0:T(8,128)(2,1)}, u32[]{:S(2)}, u32[]{:S(2)}) async-start(bf16[32,2,2,32,128]{4,3,2,1,0:T(8,128)(2,1)} %bitcast.11), calls=%async_computation.3 | async-start | bytes 2097152 | tf_op jit(solution)/shard_map/all_to_all | solution.py:265
  240.9 23.3 %collective-permute-done.1.refs_5_.refs_1_ = bf16[6,64,1024]{2,1,0:T(8,128)(2,1)S(1)} collective-permute-done((bf16[6,64,1024]{2,1,0:T(8,128)(2,1)}, bf16[6,64,1024]{2,1,0:T(8,128)(2,1)S(1)}, u32[]{:S(2)}, u32[]{:S(2)}) %collective-permute-start.1) | collective-permute-done | bytes 786464 | tf_op jit(solution)/shard_map/ppermute | solution.py:279
  264.3 0.0 copy-start
  264.3 24.6 %spectrum.6 = (f32[5,64,1024]{2,1,0:T(8,128)}, bf16[5,64,1024]{2,1,0:T(8,128)(2,1)}) custom-call(bf16[4,8,5,2,32,128]{5,4,3,2,1,0:T(8,128)(2,1)} %bitcast.5.refs_0_, bf16[1024,2048]{1,0:T(8,128)(2,1)} %constant.16.clone.refs_1_, bf16[384,256]{1,0:T(8,128)(2,1)} %constant.17.clone.refs_2_, bf16[64,64]{1,0:T(8,128)(2,1)} %constant.18.clone.refs_3_, ...), custom_call_target="tpu_custom_call" | custom-call | flops 1099511627776 | bytes 1048576 | tf_op jit(solution)/shard_map/spectrum/pallas_call | solution.py:178
  288.9 0.0 copy-done
  288.9 1.1 collective-permute-start.2
  289.9 0.0 all-to-all-done.3
  290.0 9.6 %spectrum.7.refs_3_ = f32[2,64,1024]{2,1,0:T(8,128)} custom-call(bf16[4,8,2,2,32,128]{5,4,3,2,1,0:T(8,128)(2,1)} %bitcast.7.refs_0_, bf16[1024,2048]{1,0:T(8,128)(2,1)} %constant.16.clone.refs_1_, bf16[384,256]{1,0:T(8,128)(2,1)} %constant.17.clone.refs_2_), custom_call_target="tpu_custom_call" | custom-call | flops 1099511627776 | bytes 1048576 | tf_op jit(solution)/shard_map/spectrum/pallas_call | solution.py:178
  299.6 6.1 %write_rows.2.refs_0_ = f32[64,32,1024]{2,1,0:T(8,128)} custom-call(f32[4,64,1024]{2,1,0:T(8,128)} %get-tuple-element.23.refs_0_, f32[6,64,1024]{2,1,0:T(8,128)} %get-tuple-element.28.refs_1_, f32[5,64,1024]{2,1,0:T(8,128)} %get-tuple-element.32.refs_2_, f32[2,64,1024]{2,1,0:T(8,128)} %spectrum.7.refs_3_, bf16[4,64,1024]{2,1,0:T(8,128)(2,1)} %copy-done.2, ...), custom_call_target="tpu_custom_call" | custom-call | tf_op jit(solution)/shard_map/write_rows/pallas_call | solution.py:204
  305.6 1.5 collective-permute-done.2.refs_2_
  307.1 3.9 %write_rows.3 = f32[64,32,1024]{2,1,0:T(8,128)} custom-call(f32[64,32,1024]{2,1,0:T(8,128)} %write_rows.2.refs_0_, bf16[6,64,1024]{2,1,0:T(8,128)(2,1)} %copy-done, bf16[5,64,1024]{2,1,0:T(8,128)(2,1)} %collective-permute-done.2.refs_2_), custom_call_target="tpu_custom_call", output_to_operand_aliasing={{}: (0, {})} | custom-call | tf_op jit(solution)/shard_map/write_rows/pallas_call | solution.py:204
Async XLA Ops:
  8.1 52.0 %all-to-all-start = ((bf16[32,4,2,32,128]{4,3,2,1,0:T(8,128)(2,1)}), bf16[32,4,2,32,128]{4,3,2,1,0:T(8,128)(2,1)S(1)}, u32[]{:S(2)}, u32[]{:S(2)}) async-start(bf16[32,4,2,32,128]{4,3,2,1,0:T(8,128)(2,1)} %bitcast.10), calls=%async_computation | async-start | bytes 4194304 | tf_op jit(solution)/shard_map/all_to_all | solution.py:265
  60.1 1.4 copy-start.1
  61.4 87.1 %all-to-all-start.1 = ((bf16[32,6,2,32,128]{4,3,2,1,0:T(8,128)(2,1)}), bf16[32,6,2,32,128]{4,3,2,1,0:T(8,128)(2,1)}, u32[]{:S(2)}, u32[]{:S(2)}) async-start(bf16[32,6,2,32,128]{4,3,2,1,0:T(8,128)(2,1)} %bitcast.8), calls=%async_computation.1 | async-start | bytes 6291456 | tf_op jit(solution)/shard_map/all_to_all | solution.py:265
  89.6 76.3 %collective-permute-start = (bf16[4,64,1024]{2,1,0:T(8,128)(2,1)}, bf16[4,64,1024]{2,1,0:T(8,128)(2,1)S(1)}, u32[]{:S(2)}, u32[]{:S(2)}) collective-permute-start(bf16[4,64,1024]{2,1,0:T(8,128)(2,1)} %get-tuple-element.24), channel_id=1, source_target_pairs={{0,31},{1,30},{2,29},{3,28},{4,27},{5,26},{6,25},{7,24},{8,23},{9,... | collective-permute-start | bytes 1572872 | tf_op jit(solution)/shard_map/ppermute | solution.py:279
  148.6 84.3 %all-to-all-start.2 = ((bf16[32,5,2,32,128]{4,3,2,1,0:T(8,128)(2,1)}), bf16[32,5,2,32,128]{4,3,2,1,0:T(8,128)(2,1)}, u32[]{:S(2)}, u32[]{:S(2)}) async-start(bf16[32,5,2,32,128]{4,3,2,1,0:T(8,128)(2,1)} %bitcast.9), calls=%async_computation.2 | async-start | bytes 5242880 | tf_op jit(solution)/shard_map/all_to_all | solution.py:265
  166.0 28.5 %copy-start.2 = (bf16[4,64,1024]{2,1,0:T(8,128)(2,1)}, bf16[4,64,1024]{2,1,0:T(8,128)(2,1)S(1)}, u32[]{:S(2)}) copy-start(bf16[4,64,1024]{2,1,0:T(8,128)(2,1)S(1)} %collective-permute-done.refs_4_) | copy-start | bytes 1572868
  194.5 69.7 %collective-permute-start.1 = (bf16[6,64,1024]{2,1,0:T(8,128)(2,1)}, bf16[6,64,1024]{2,1,0:T(8,128)(2,1)S(1)}, u32[]{:S(2)}, u32[]{:S(2)}) collective-permute-start(bf16[6,64,1024]{2,1,0:T(8,128)(2,1)} %get-tuple-element.30), channel_id=1, source_target_pairs={{0,31},{1,30},{2,29},{3,28},{4,27},{5,26},{6,25},{7,24},{8,23},{9,... | collective-permute-start | bytes 2359304 | tf_op jit(solution)/shard_map/ppermute | solution.py:279
  232.8 57.1 %all-to-all-start.3 = ((bf16[32,2,2,32,128]{4,3,2,1,0:T(8,128)(2,1)}), bf16[32,2,2,32,128]{4,3,2,1,0:T(8,128)(2,1)}, u32[]{:S(2)}, u32[]{:S(2)}) async-start(bf16[32,2,2,32,128]{4,3,2,1,0:T(8,128)(2,1)} %bitcast.11), calls=%async_computation.3 | async-start | bytes 2097152 | tf_op jit(solution)/shard_map/all_to_all | solution.py:265
  264.3 24.6 %copy-start = (bf16[6,64,1024]{2,1,0:T(8,128)(2,1)}, bf16[6,64,1024]{2,1,0:T(8,128)(2,1)S(1)}, u32[]{:S(2)}) copy-start(bf16[6,64,1024]{2,1,0:T(8,128)(2,1)S(1)} %collective-permute-done.1.refs_5_.refs_1_) | copy-start | bytes 2359300
  288.9 18.3 %collective-permute-start.2 = (bf16[5,64,1024]{2,1,0:T(8,128)(2,1)}, bf16[5,64,1024]{2,1,0:T(8,128)(2,1)}, u32[]{:S(2)}, u32[]{:S(2)}) collective-permute-start(bf16[5,64,1024]{2,1,0:T(8,128)(2,1)} %get-tuple-element.36), channel_id=1, source_target_pairs={{0,31},{1,30},{2,29},{3,28},{4,27},{5,26},{6,25},{7,24},{8,23},{9,... | collective-permute-start | bytes 1966088 | tf_op jit(solution)/shard_map/ppermute | solution.py:279

commit v3 on v2

v3 whole, which is shorter than its diff:
```python
import functools
import math

import jax
import jax.numpy as jnp
import ml_dtypes
import numpy as np
from jax import lax
from jax.experimental import pallas as pl
from jax.experimental.pallas import tpu as pltpu
from jax.sharding import PartitionSpec as P

AXES = ("tm", "rows")
LANES = 128
TILE = 8
SHARES = (4, 11, 15)
SMALL = pl.CostEstimate(flops=1 << 20, bytes_accessed=1 << 20, transcendentals=0)
LARGE = pl.CostEstimate(flops=1 << 40, bytes_accessed=1 << 20, transcendentals=0)
VMEM_BYTES = 63 * 1024 * 1024
ROWS_VMEM_BYTES = 40 * 1024 * 1024
ROWS_STEP = 32


def to_bf16(values):
    return values.astype(ml_dtypes.bfloat16)


def unit_angles(left, right, modulus):
    return (np.outer(left, right) % modulus).astype(np.float32) * np.float32(2.0 * math.pi / modulus)


def y_table(length, wavenumbers, paired):
    angles = unit_angles(wavenumbers.reshape(-1), np.arange(length), length)
    pairs = np.stack([np.cos(angles), -np.sin(angles)], 1) / np.float32(math.sqrt(length))
    if paired is not None:
        pairs = pairs.reshape(wavenumbers.shape + (2, length))
        pairs[paired][1] = 1.0 / math.sqrt(length)
    return to_bf16(pairs.reshape(2 * wavenumbers.size, length))


def x_table(length):
    angles = unit_angles(np.arange(length), np.arange(length), length)
    return to_bf16(
        np.concatenate([np.cos(angles), np.sin(angles)], 1) / np.float32(math.sqrt(length))
    )


def window_table(hop, windows):
    size = 2 * hop
    steps = np.arange(size)
    hann = np.float32(0.5) - np.float32(0.5) * np.cos(
        steps.astype(np.float32) * np.float32(2.0 * math.pi / size)
    )
    angles = unit_angles(steps, steps, size)
    cosine = to_bf16(np.cos(angles) * hann[None, :])
    sine = to_bf16(np.sin(angles) * hann[None, :])
    frames = hop * (windows + 1)
    table = np.zeros((windows, 2, size, 2, frames), ml_dtypes.bfloat16)
    for window in range(windows):
        at = slice(window * hop, window * hop + size)
        table[window, 0, :, 0, at] = cosine
        table[window, 0, :, 1, at] = sine
        table[window, 1, :, 1, at] = cosine
        table[window, 1, :, 0, at] = -sine
    return table.reshape(windows * 2 * size, 2 * frames), float(np.sum(hann * hann))


def reversal(size):
    matrix = np.zeros((size, size), ml_dtypes.bfloat16)
    matrix[np.arange(size), (size - np.arange(size)) % size] = 1
    return matrix


def row_transform_kernel(table_ref, heights_ref, out_ref):
    frames, rows, length = heights_ref.shape
    planes = []
    for frame in range(0, frames, 2):
        pair = heights_ref[frame : frame + 2].reshape(2 * rows, length)
        product = lax.dot_general(
            table_ref[...], pair, (((1,), (1,)), ((), ())), preferred_element_type=jnp.float32
        )
        planes += [product[:, :rows], product[:, rows:]]
    out_ref[...] = jnp.swapaxes(jnp.stack(planes, 0), 0, 1).astype(jnp.bfloat16)


def row_transform(heights, table):
    frames, rows, length = heights.shape
    columns = table.shape[0]
    if rows != LANES:
        return jnp.einsum(
            "cy,fxy->cfx", table, heights, preferred_element_type=jnp.float32
        ).astype(jnp.bfloat16)
    step = 16
    return pl.pallas_call(
        row_transform_kernel,
        out_shape=jax.ShapeDtypeStruct((columns, frames, rows), jnp.bfloat16),
        grid=(frames // step,),
        in_specs=[
            pl.BlockSpec((columns, length), lambda i: (0, 0)),
            pl.BlockSpec((step, rows, length), lambda i: (i, 0, 0)),
        ],
        out_specs=pl.BlockSpec((columns, step, rows), lambda i: (0, i, 0)),
        compiler_params=pltpu.CompilerParams(vmem_limit_bytes=VMEM_BYTES),
        cost_estimate=SMALL,
        name="row_transform",
    )(table, heights)


def gather_field(pieces_ref):
    blocks, width, _, part, _, _ = pieces_ref.shape
    return jnp.concatenate(
        [
            jnp.concatenate([pieces_ref[t, s, 0, p] for s in range(width)], 1)
            for p in range(part)
            for t in range(blocks)
        ],
        0,
    )


def column_products(field, x_ref, at, chunk):
    length = x_ref.shape[0]
    return (
        jnp.dot(field, x_ref[:, at : at + chunk], preferred_element_type=jnp.float32),
        jnp.dot(
            field, x_ref[:, length + at : length + at + chunk], preferred_element_type=jnp.float32
        ),
    )


def mean_power(real_part, imag_part, window_ref, scale, size):
    modes = jnp.concatenate([real_part, imag_part], 0).astype(jnp.bfloat16)
    moved = jnp.dot(window_ref[...], modes, preferred_element_type=jnp.float32)
    power = moved * moved
    total = power[:size]
    for row in range(size, power.shape[0], size):
        total = total + power[row : row + size]
    return total * scale


def flipped(power, flip_w_ref):
    return jnp.dot(
        flip_w_ref[...], power.astype(jnp.bfloat16), preferred_element_type=jnp.float32
    ).astype(jnp.bfloat16)


def spectrum_kernel(
    scale, pieces_ref, x_ref, window_ref, flip_w_ref, flip_k_ref, own_ref, mirror_ref, scratch
):
    length = x_ref.shape[0]
    number, size, _ = scratch.shape
    field = gather_field(pieces_ref)
    frames = field.shape[0] // 2
    chunk = math.gcd(length, 256)
    for at in range(0, length, chunk):
        cosine, sine = column_products(field, x_ref, at, chunk)
        real_part = cosine[:frames] + sine[frames:]
        imag_part = cosine[frames:] - sine[:frames]
        total = mean_power(real_part, imag_part, window_ref, scale, size)
        own_ref[0, :, at : at + chunk] = total
        scratch[number - 1 - pl.program_id(0), :, at : at + chunk] = flipped(total, flip_w_ref)

    @pl.when(pl.program_id(0) == number - 1)
    def reverse():
        flat = scratch[...].reshape(number * size, length)
        turned = jnp.dot(flat, flip_k_ref[...], preferred_element_type=jnp.float32)
        mirror_ref[...] = turned.astype(jnp.bfloat16).reshape(number, size, length)


def edge_kernel(
    scale,
    paired_ref,
    pieces_ref,
    x_ref,
    window_ref,
    flip_w_ref,
    flip_k_ref,
    own_ref,
    mirror_ref,
    scratch,
):
    length = x_ref.shape[0]
    size = scratch.shape[1]
    paired = paired_ref[0] != 0
    apart = jnp.where(paired, 0.0, 1.0)
    field = gather_field(pieces_ref)
    frames = field.shape[0] // 2
    chunk = math.gcd(length, 256)
    for at in range(0, length, chunk):
        cosine, sine = column_products(field, x_ref, at, chunk)
        real_part = cosine[:frames] + apart * sine[frames:]
        imag_part = apart * cosine[frames:] - sine[:frames]
        total = mean_power(real_part, imag_part, window_ref, scale, size)
        other = mean_power(cosine[frames:], -sine[frames:], window_ref, scale, size)
        own_ref[0, :, at : at + chunk] = total
        mirror_ref[0, :, at : at + chunk] = other.astype(jnp.bfloat16)
        scratch[0, :, at : at + chunk] = flipped(total, flip_w_ref)

    @pl.when(jnp.logical_not(paired))
    def reverse():
        turned = jnp.dot(scratch[0], flip_k_ref[...], preferred_element_type=jnp.float32)
        mirror_ref[0] = turned.astype(jnp.bfloat16)


def spectrum(pieces, start, number, tables, scale, paired=None):
    blocks, width, _, part, frames, rows = pieces.shape
    length = width * rows
    size = 2 * frames
    if rows != LANES:
        pieces = pieces[:, :, start : start + number].transpose(0, 2, 3, 4, 1, 5)
        pieces = pieces.reshape(blocks, 1, number, part, frames, length)
        width, rows, start = 1, length, 0
    whole = lambda array: pl.BlockSpec(array.shape, lambda i, *_: (0,) * array.ndim)
    block = (blocks, width, 1, part, frames, rows)
    scalars = [] if paired is None else [paired]
    return pl.pallas_call(
        functools.partial(spectrum_kernel if paired is None else edge_kernel, scale),
        out_shape=[
            jax.ShapeDtypeStruct((number, size, length), jnp.float32),
            jax.ShapeDtypeStruct((number, size, length), jnp.bfloat16),
        ],
        grid_spec=pltpu.PrefetchScalarGridSpec(
            num_scalar_prefetch=len(scalars),
            grid=(number,),
            in_specs=[pl.BlockSpec(block, lambda i, *_: (0, 0, start + i, 0, 0, 0))]
            + [whole(table) for table in tables],
            out_specs=[
                pl.BlockSpec((1, size, length), lambda i, *_: (i, 0, 0)),
                pl.BlockSpec((number, size, length), lambda i, *_: (0, 0, 0)),
            ],
            scratch_shapes=[pltpu.VMEM((number, size, length), jnp.bfloat16)],
        ),
        compiler_params=pltpu.CompilerParams(vmem_limit_bytes=VMEM_BYTES),
        cost_estimate=LARGE if paired is None else SMALL,
        name="spectrum" if paired is None else "edge_spectrum",
    )(*scalars, pieces, *tables)


def rows_kernel(places, aliased, *refs):
    planes, out_ref = refs[aliased:-1], refs[-1]
    for at in range(0, len(places), TILE):
        stack = [planes[which][plane].astype(jnp.float32) for which, plane in places[at : at + TILE]]
        out_ref[:, at : at + TILE] = jnp.swapaxes(jnp.stack(stack, 0), 0, 1)


def write_rows(given, arrays, places, start, total):
    _, size, length = arrays[0].shape
    step = ROWS_STEP
    used = sorted({which for which, _ in places})
    places = [(used.index(which), plane) for which, plane in places]
    block = start // len(places)
    return pl.pallas_call(
        functools.partial(rows_kernel, places, len(given)),
        out_shape=jax.ShapeDtypeStruct((size, total, length), jnp.float32),
        grid=(size // step,),
        in_specs=[pl.BlockSpec(memory_space=pl.ANY)] * len(given)
        + [
            pl.BlockSpec((arrays[which].shape[0], step, length), lambda i: (0, i, 0))
            for which in used
        ],
        out_specs=pl.BlockSpec((step, len(places), length), lambda i: (i, block, 0)),
        input_output_aliases={0: 0} if given else {},
        compiler_params=pltpu.CompilerParams(vmem_limit_bytes=ROWS_VMEM_BYTES),
        name="write_rows",
    )(*given, *[arrays[which] for which in used])


def assemble(arrays, places, last):
    total = len(places)
    late = min(row for row in range(total) if places[row][0] == last)
    late -= late % TILE
    while late % (total - late):
        late -= TILE
    given = []
    if late:
        given.append(write_rows([], arrays, places[:late], 0, total))
    return write_rows(given, arrays, places[late:], late, total)


def split_rows(half):
    rows = list(range(half - 1, 0, -1))
    parts = [len(rows) * share // SHARES[-1] for share in SHARES]
    return [sorted(rows[lo:hi]) for lo, hi in zip([0] + parts, parts) if hi > lo]


def body(heights):
    frames, rows_dev, length = heights.shape
    tm_count = lax.axis_size("tm")
    rows_count = lax.axis_size("rows")
    devices = tm_count * rows_count
    owned = length // devices
    half = owned // 2
    middle = devices // 2
    windows, energy = window_table(frames, tm_count - 1)
    scale = 1.0 / ((tm_count - 1) * energy)
    tables = (x_table(length), windows, reversal(2 * frames), reversal(length))
    tables = tuple(jnp.asarray(table) for table in tables)
    device = lax.axis_index(AXES)
    opposite = [(d, devices - 1 - d) for d in range(devices)]
    edge_partner = [(d, devices - 1 - d if d < middle else (devices - d) % middle) for d in range(devices)]

    edges = np.array([d * owned + (half if d < middle else 0) for d in range(devices)])

    def mix(heights, slot, with_edge):
        wavenumbers = np.arange(devices)[:, None] * owned + np.asarray(slot)
        if with_edge:
            wavenumbers = np.concatenate([edges[:, None], wavenumbers], 1)
        table = y_table(length, wavenumbers, (middle, 0) if with_edge else None)
        mixed = row_transform(heights, jnp.asarray(table))
        return mixed.reshape(devices, -1, 2, frames, rows_dev)

    def arrive(mixed):
        got = lax.all_to_all(mixed, AXES, split_axis=0, concat_axis=0, tiled=True)
        return got.reshape((tm_count, rows_count) + mixed.shape[1:])

    slots = split_rows(half)
    pieces = [arrive(mix(heights, slot, at == 0)) for at, slot in enumerate(slots[:2])]
    paired = (device == middle).astype(jnp.int32).reshape(1)
    planes, images = [], []
    for at, slot in enumerate(slots):
        if 0 < at < len(slots) - 1:
            pieces[at], images, edge_image = lax.optimization_barrier(
                (pieces[at], images, edge_image)
            )
        plane, image = spectrum(pieces[at], int(at == 0), len(slot), tables, scale)
        if at == 0:
            edge, edge_image = spectrum(pieces[0], 0, 1, tables, scale, paired)
            edge_image = lax.ppermute(edge_image, AXES, edge_partner)
        if at + 2 < len(slots):
            plane, image, later = lax.optimization_barrier((plane, image, heights))
            pieces.append(arrive(mix(later, slots[at + 2], False)))
        planes.append(plane)
        images.append(lax.ppermute(image, AXES, opposite))
    edge_image = edge_image.astype(jnp.float32)
    lower = device < middle
    arrays = planes + images
    last = len(arrays) - 1
    arrays += [jnp.where(lower, edge_image, edge), jnp.where(lower, edge, edge_image)]
    places = [None] * owned
    places[0], places[half] = (last + 1, 0), (last + 2, 0)
    for at, slot in enumerate(slots):
        for plane, row in enumerate(slot):
            places[row] = (at, plane)
            places[owned - row] = (len(slots) + at, len(slot) - 1 - plane)
    return assemble(arrays, places, last)


def solution(mesh):
    in_specs = (P("tm", "rows", None),)
    out_specs = P(None, ("tm", "rows"), None)
    return jax.shard_map(body, mesh=mesh, in_specs=in_specs, out_specs=out_specs, check_vma=False)
```

time: 313 us -> 302 us (0.965)
  Pallas kernels: 128 us -> 110 us
  waiting for transfers between devices: 144 us -> 153 us
  starting transfers between devices: 37.5 us -> 31.9 us
    ppermute x3, waiting for transfers between devices: 34.1 us -> 14.3 us  [body(): images.append(lax.ppermute(image, AXES, opposite))]
    ppermute x0 -> x1, waiting for transfers between devices: none -> 16.3 us  [body(): edge_image = lax.ppermute(edge_image, AXES, edge_partner)]
    all_to_all x4 -> x3, waiting for transfers between devices: 110 us -> 123 us  [arrive(): got = lax.all_to_all(mixed, AXES, split_axis=0, concat_axis=0, tiled=True)]
    pallas_call x4 -> x3, Pallas kernels: 35.1 us -> 22.2 us  [row_transform(): pl.pallas_call(row_transform_kernel, out_shape=jax.ShapeDtypeStruct((colu...]
    all_to_all x4 -> x3, starting transfers between devices: 30.4 us -> 23.9 us  [arrive(): got = lax.all_to_all(mixed, AXES, split_axis=0, concat_axis=0, tiled=True)]
  transfers between devices with their start and end apart: 7 -> 7, of which waited for: 6 -> 5; matrix products, arithmetic and copies ran while one was open for 0% -> 0% of each run, Pallas kernels for 37% -> 33%
where the time goes in v3:
time: 302 us; the launch traced here: 299 us
  waiting for transfers between devices  153 us (51%)
  Pallas kernels  110 us (36%)
  starting transfers between devices  31.9 us (11%)
  local copies, waits for them, and re-layouts  3.95 us (1%)
    all_to_all x3, waiting for transfers between devices, arrive(): got = lax.all_to_all(mixed, AXES, split_axis=0, concat_axis=0, tiled=True)  123 us
    pallas_call x4, Pallas kernels, spectrum(): pl.pallas_call(functools.partial(spectrum_kernel if paired is None else e...  80.3 us
    all_to_all x3, starting transfers between devices, arrive(): got = lax.all_to_all(mixed, AXES, split_axis=0, concat_axis=0, tiled=True)  23.9 us
    pallas_call x3, Pallas kernels, row_transform(): pl.pallas_call(row_transform_kernel, out_shape=jax.ShapeDtypeStruct((colu...  22.2 us
    ppermute x1, waiting for transfers between devices, body(): edge_image = lax.ppermute(edge_image, AXES, edge_partner)  16.3 us
    ppermute x3, waiting for transfers between devices, body(): images.append(lax.ppermute(image, AXES, opposite))  14.3 us
    pallas_call x2, Pallas kernels, write_rows(): pl.pallas_call(functools.partial(rows_kernel, places, len(given)), out_sh...  7.07 us
    ppermute x3, starting transfers between devices, body(): images.append(lax.ppermute(image, AXES, opposite))  6.9 us
  transfers between devices with their start and end apart: 7, of which 5 were waited for; matrix products, arithmetic and copies ran while one was open for 0% of the time, Pallas kernels for 33%

profile of v3, /device:TPU:13, one launch (start us, length us, event | category | flops | bytes accessed | tf_op | source)
XLA Modules:
  0.0 299.1 jit_solution(3465630875165254881)
XLA Ops:
  0.0 7.2 %row_transform.3 = bf16[320,32,128]{2,1,0:T(8,128)(2,1)} custom-call(bf16[320,1024]{1,0:T(8,128)(2,1)} %constant.30.clone.table_ref, bf16[32,128,1024]{2,1,0:T(8,128)(2,1)} %heights_ref.4), custom_call_target="tpu_custom_call" | custom-call | flops 1048576 | bytes 1048576 | tf_op jit(solution)/shard_map/row_transform/pallas_call | solution.py:94
  7.2 6.4 %all-to-all-start = ((bf16[32,5,2,32,128]{4,3,2,1,0:T(8,128)(2,1)}), bf16[32,5,2,32,128]{4,3,2,1,0:T(8,128)(2,1)}, u32[]{:S(2)}, u32[]{:S(2)}) async-start(bf16[32,5,2,32,128]{4,3,2,1,0:T(8,128)(2,1)} %bitcast.8), calls=%async_computation | async-start | bytes 5242880 | tf_op jit(solution)/shard_map/all_to_all | solution.py:313
  13.5 8.7 %row_transform.4 = bf16[448,32,128]{2,1,0:T(8,128)(2,1)} custom-call(bf16[448,1024]{1,0:T(8,128)(2,1)} %constant.31.clone.table_ref, bf16[32,128,1024]{2,1,0:T(8,128)(2,1)} %heights_ref.4), custom_call_target="tpu_custom_call" | custom-call | flops 1048576 | bytes 1048576 | tf_op jit(solution)/shard_map/row_transform/pallas_call | solution.py:94
  22.2 48.1 %all-to-all-done = bf16[32,5,2,32,128]{4,3,2,1,0:T(8,128)(2,1)} async-done(((bf16[32,5,2,32,128]{4,3,2,1,0:T(8,128)(2,1)}), bf16[32,5,2,32,128]{4,3,2,1,0:T(8,128)(2,1)}, u32[]{:S(2)}, u32[]{:S(2)}) %all-to-all-start) | async-done | bytes 2621472 | tf_op jit(solution)/shard_map/all_to_all | solution.py:313
  70.4 8.0 %all-to-all-start.1 = ((bf16[32,7,2,32,128]{4,3,2,1,0:T(8,128)(2,1)}), bf16[32,7,2,32,128]{4,3,2,1,0:T(8,128)(2,1)}, u32[]{:S(2)}, u32[]{:S(2)}) async-start(bf16[32,7,2,32,128]{4,3,2,1,0:T(8,128)(2,1)} %bitcast.7), calls=%async_computation.1 | async-start | bytes 7340032 | tf_op jit(solution)/shard_map/all_to_all | solution.py:313
  78.4 20.3 %spectrum.3 = (f32[4,64,1024]{2,1,0:T(8,128)}, bf16[4,64,1024]{2,1,0:T(8,128)(2,1)}) custom-call(bf16[4,8,5,2,32,128]{5,4,3,2,1,0:T(8,128)(2,1)} %bitcast.1.pieces_ref, bf16[1024,2048]{1,0:T(8,128)(2,1)} %constant.26.clone.x_ref, bf16[384,256]{1,0:T(8,128)(2,1)} %constant.27.clone.window_ref, bf16[64,64]{1,0:T(8,128)(2,1)} %constant.28.clone.flip_w_ref, ...), custom_call_target="tpu_custom_call" | custom-call | flops 1099511627776 | bytes 1048576 | tf_op jit(solution)/shard_map/spectrum/pallas_call | solution.py:216
  98.7 2.4 collective-permute-start
  101.1 7.2 %edge_spectrum.1 = (f32[1,64,1024]{2,1,0:T(8,128)}, bf16[1,64,1024]{2,1,0:T(8,128)(2,1)}) custom-call(s32[1]{0:T(128)} %bitcast.4.paired_ref, bf16[4,8,5,2,32,128]{5,4,3,2,1,0:T(8,128)(2,1)} %bitcast.1.pieces_ref, bf16[1024,2048]{1,0:T(8,128)(2,1)} %constant.26.clone.x_ref, bf16[384,256]{1,0:T(8,128)(2,1)} %constant.27.clone.window_ref, ...), custom_call_target="tpu_custom_call" | custom-call | flops 1048576 | bytes 1048576 | tf_op jit(solution)/shard_map/edge_spectrum/pallas_call | solution.py:216
  108.3 1.1 collective-permute-start.1
  109.5 6.4 %row_transform.5 = bf16[256,32,128]{2,1,0:T(8,128)(2,1)} custom-call(bf16[256,1024]{1,0:T(8,128)(2,1)} %constant.32.clone.table_ref, bf16[32,128,1024]{2,1,0:T(8,128)(2,1)} %heights_ref.4), custom_call_target="tpu_custom_call" | custom-call | flops 1048576 | bytes 1048576 | tf_op jit(solution)/shard_map/row_transform/pallas_call | solution.py:94
  115.8 54.4 %all-to-all-done.1 = bf16[32,7,2,32,128]{4,3,2,1,0:T(8,128)(2,1)} async-done(((bf16[32,7,2,32,128]{4,3,2,1,0:T(8,128)(2,1)}), bf16[32,7,2,32,128]{4,3,2,1,0:T(8,128)(2,1)}, u32[]{:S(2)}, u32[]{:S(2)}) %all-to-all-start.1) | async-done | bytes 3670048 | tf_op jit(solution)/shard_map/all_to_all | solution.py:313
  170.3 9.5 %all-to-all-start.2 = ((bf16[32,4,2,32,128]{4,3,2,1,0:T(8,128)(2,1)}), bf16[32,4,2,32,128]{4,3,2,1,0:T(8,128)(2,1)}, u32[]{:S(2)}, u32[]{:S(2)}) async-start(bf16[32,4,2,32,128]{4,3,2,1,0:T(8,128)(2,1)} %bitcast.9), calls=%async_computation.2 | async-start | bytes 4194304 | tf_op jit(solution)/shard_map/all_to_all | solution.py:313
  179.8 16.3 %collective-permute-done.1 = bf16[1,64,1024]{2,1,0:T(8,128)(2,1)S(1)} collective-permute-done((bf16[1,64,1024]{2,1,0:T(8,128)(2,1)}, bf16[1,64,1024]{2,1,0:T(8,128)(2,1)S(1)}, u32[]{:S(2)}, u32[]{:S(2)}) %collective-permute-start.1) | collective-permute-done | bytes 131104 | tf_op jit(solution)/shard_map/ppermute | solution.py:328
  196.1 0.0 copy-start.4
  196.1 0.0 collective-permute-done.refs_3_
  196.1 32.5 %spectrum.4 = (f32[7,64,1024]{2,1,0:T(8,128)}, bf16[7,64,1024]{2,1,0:T(8,128)(2,1)}) custom-call(bf16[4,8,7,2,32,128]{5,4,3,2,1,0:T(8,128)(2,1)} %bitcast.3.pieces_ref, bf16[1024,2048]{1,0:T(8,128)(2,1)} %constant.26.clone.x_ref, bf16[384,256]{1,0:T(8,128)(2,1)} %constant.27.clone.window_ref, bf16[64,64]{1,0:T(8,128)(2,1)} %constant.28.clone.flip_w_ref, ...), custom_call_target="tpu_custom_call" | custom-call | flops 1099511627776 | bytes 1048576 | tf_op jit(solution)/shard_map/spectrum/pallas_call | solution.py:216
  228.6 0.0 copy-done.4
  228.6 0.1 collective-permute-start.2
  228.7 20.3 %all-to-all-done.2 = bf16[32,4,2,32,128]{4,3,2,1,0:T(8,128)(2,1)} async-done(((bf16[32,4,2,32,128]{4,3,2,1,0:T(8,128)(2,1)}), bf16[32,4,2,32,128]{4,3,2,1,0:T(8,128)(2,1)}, u32[]{:S(2)}, u32[]{:S(2)}) %all-to-all-start.2) | async-done | bytes 2097184 | tf_op jit(solution)/shard_map/all_to_all | solution.py:313
  249.0 0.0 copy-start.3
  249.0 20.3 %spectrum.5 = (f32[4,64,1024]{2,1,0:T(8,128)}, bf16[4,64,1024]{2,1,0:T(8,128)(2,1)}) custom-call(bf16[4,8,4,2,32,128]{5,4,3,2,1,0:T(8,128)(2,1)} %bitcast.6.pieces_ref, bf16[1024,2048]{1,0:T(8,128)(2,1)} %constant.26.clone.x_ref, bf16[384,256]{1,0:T(8,128)(2,1)} %constant.27.clone.window_ref, bf16[64,64]{1,0:T(8,128)(2,1)} %constant.28.clone.flip_w_ref, ...), custom_call_target="tpu_custom_call" | custom-call | flops 1099511627776 | bytes 1048576 | tf_op jit(solution)/shard_map/spectrum/pallas_call | solution.py:216
  269.3 4.4 %collective-permute-start.3 = (bf16[4,64,1024]{2,1,0:T(8,128)(2,1)}, bf16[4,64,1024]{2,1,0:T(8,128)(2,1)S(1)}, u32[]{:S(2)}, u32[]{:S(2)}) collective-permute-start(bf16[4,64,1024]{2,1,0:T(8,128)(2,1)} %get-tuple-element.32), channel_id=1, source_target_pairs={{0,31},{1,30},{2,29},{3,28},{4,27},{5,26},{6,25},{7,24},{8,23},{9,... | collective-permute-start | bytes 1572872 | tf_op jit(solution)/shard_map/ppermute | solution.py:333
  273.8 0.0 copy-done.3
  273.8 0.0 copy-done.5
  273.8 0.0 collective-permute-done.2.refs_4_.refs_1_
  273.8 0.0 copy-start
  273.8 1.5 copy-done
  275.3 1.2 copy-done.1
  276.6 1.2 copy-done.2
  277.8 4.5 %write_rows.2.refs_0_ = f32[64,32,1024]{2,1,0:T(8,128)} custom-call(f32[4,64,1024]{2,1,0:T(8,128)S(1)} %copy-done.1, f32[7,64,1024]{2,1,0:T(8,128)S(1)} %copy-done, f32[4,64,1024]{2,1,0:T(8,128)S(1)} %copy-done.2, bf16[4,64,1024]{2,1,0:T(8,128)(2,1)S(1)} %collective-permute-done.refs_3_, bf16[7,64,1024]{2,1,0:T(8,128)(2,1)} %collective-permute-done.2.refs_4_.refs_1_, ...), custom_call_target="tpu_custom_call" | custom-call | tf_op jit(solution)/shard_map/write_rows/pallas_call | solution.py:252
  282.3 14.3 %collective-permute-done.3.refs_2_ = bf16[4,64,1024]{2,1,0:T(8,128)(2,1)S(1)} collective-permute-done((bf16[4,64,1024]{2,1,0:T(8,128)(2,1)}, bf16[4,64,1024]{2,1,0:T(8,128)(2,1)S(1)}, u32[]{:S(2)}, u32[]{:S(2)}) %collective-permute-start.3) | collective-permute-done | bytes 524320 | tf_op jit(solution)/shard_map/ppermute | solution.py:333
  296.5 2.6 write_rows.3
  (4 shorter events, 0.0 us)
Async XLA Ops:
  7.2 63.2 %all-to-all-start = ((bf16[32,5,2,32,128]{4,3,2,1,0:T(8,128)(2,1)}), bf16[32,5,2,32,128]{4,3,2,1,0:T(8,128)(2,1)}, u32[]{:S(2)}, u32[]{:S(2)}) async-start(bf16[32,5,2,32,128]{4,3,2,1,0:T(8,128)(2,1)} %bitcast.8), calls=%async_computation | async-start | bytes 5242880 | tf_op jit(solution)/shard_map/all_to_all | solution.py:313
  70.4 99.9 %all-to-all-start.1 = ((bf16[32,7,2,32,128]{4,3,2,1,0:T(8,128)(2,1)}), bf16[32,7,2,32,128]{4,3,2,1,0:T(8,128)(2,1)}, u32[]{:S(2)}, u32[]{:S(2)}) async-start(bf16[32,7,2,32,128]{4,3,2,1,0:T(8,128)(2,1)} %bitcast.7), calls=%async_computation.1 | async-start | bytes 7340032 | tf_op jit(solution)/shard_map/all_to_all | solution.py:313
  98.7 97.4 %collective-permute-start = (bf16[4,64,1024]{2,1,0:T(8,128)(2,1)}, bf16[4,64,1024]{2,1,0:T(8,128)(2,1)S(1)}, u32[]{:S(2)}, u32[]{:S(2)}) collective-permute-start(bf16[4,64,1024]{2,1,0:T(8,128)(2,1)} %get-tuple-element.22), channel_id=1, source_target_pairs={{0,31},{1,30},{2,29},{3,28},{4,27},{5,26},{6,25},{7,24},{8,23},{9,... | collective-permute-start | bytes 1572872 | tf_op jit(solution)/shard_map/ppermute | solution.py:333
  108.3 87.8 %collective-permute-start.1 = (bf16[1,64,1024]{2,1,0:T(8,128)(2,1)}, bf16[1,64,1024]{2,1,0:T(8,128)(2,1)S(1)}, u32[]{:S(2)}, u32[]{:S(2)}) collective-permute-start(bf16[1,64,1024]{2,1,0:T(8,128)(2,1)} %get-tuple-element.23), channel_id=1, source_target_pairs={{0,31},{1,30},{2,29},{3,28},{4,27},{5,26},{6,25},{7,24},{8,23},{9,... | collective-permute-start | bytes 393224 | tf_op jit(solution)/shard_map/ppermute | solution.py:328
  170.3 78.7 %all-to-all-start.2 = ((bf16[32,4,2,32,128]{4,3,2,1,0:T(8,128)(2,1)}), bf16[32,4,2,32,128]{4,3,2,1,0:T(8,128)(2,1)}, u32[]{:S(2)}, u32[]{:S(2)}) async-start(bf16[32,4,2,32,128]{4,3,2,1,0:T(8,128)(2,1)} %bitcast.9), calls=%async_computation.2 | async-start | bytes 4194304 | tf_op jit(solution)/shard_map/all_to_all | solution.py:313
  196.1 32.5 %copy-start.4 = (bf16[1,64,1024]{2,1,0:T(8,128)(2,1)}, bf16[1,64,1024]{2,1,0:T(8,128)(2,1)S(1)}, u32[]{:S(2)}) copy-start(bf16[1,64,1024]{2,1,0:T(8,128)(2,1)S(1)} %collective-permute-done.1) | copy-start | bytes 393220
  228.6 45.2 %collective-permute-start.2 = (bf16[7,64,1024]{2,1,0:T(8,128)(2,1)}, bf16[7,64,1024]{2,1,0:T(8,128)(2,1)}, u32[]{:S(2)}, u32[]{:S(2)}) collective-permute-start(bf16[7,64,1024]{2,1,0:T(8,128)(2,1)} %get-tuple-element.29), channel_id=1, source_target_pairs={{0,31},{1,30},{2,29},{3,28},{4,27},{5,26},{6,25},{7,24},{8,23},{9,... | collective-permute-start | bytes 2752520 | tf_op jit(solution)/shard_map/ppermute | solution.py:333
  249.0 24.7 %copy-start.3 = (f32[1,64,1024]{2,1,0:T(8,128)S(1)}, f32[1,64,1024]{2,1,0:T(8,128)}, u32[]{:S(2)}) copy-start(f32[1,64,1024]{2,1,0:T(8,128)} %get-tuple-element.31) | copy-start | bytes 786436
  249.0 24.7 %copy-start.5 = (bf16[1,64,1024]{2,1,0:T(8,128)(2,1)S(1)}, bf16[1,64,1024]{2,1,0:T(8,128)(2,1)}, u32[]{:S(2)}) copy-start(bf16[1,64,1024]{2,1,0:T(8,128)(2,1)} %copy-done.4) | copy-start | bytes 393220
  269.3 27.2 %collective-permute-start.3 = (bf16[4,64,1024]{2,1,0:T(8,128)(2,1)}, bf16[4,64,1024]{2,1,0:T(8,128)(2,1)S(1)}, u32[]{:S(2)}, u32[]{:S(2)}) collective-permute-start(bf16[4,64,1024]{2,1,0:T(8,128)(2,1)} %get-tuple-element.32), channel_id=1, source_target_pairs={{0,31},{1,30},{2,29},{3,28},{4,27},{5,26},{6,25},{7,24},{8,23},{9,... | collective-permute-start | bytes 1572872 | tf_op jit(solution)/shard_map/ppermute | solution.py:333
  273.8 1.5 copy-start
  275.3 1.2 copy-start.1
  276.5 1.2 copy-start.2

commit v4 on v3

--- a/solution.py
+++ b/solution.py
@@ -10,10 +10,10 @@
 from jax.experimental.pallas import tpu as pltpu
 from jax.sharding import PartitionSpec as P
 
-AXES = ("tm", "rows")
+AXES = ("tm", "half", "near")
 LANES = 128
 TILE = 8
-SHARES = (4, 11, 15)
+SHARES = (9, 11, 15)
 SMALL = pl.CostEstimate(flops=1 << 20, bytes_accessed=1 << 20, transcendentals=0)
 LARGE = pl.CostEstimate(flops=1 << 40, bytes_accessed=1 << 20, transcendentals=0)
 VMEM_BYTES = 63 * 1024 * 1024
@@ -71,39 +71,44 @@
     return matrix
 
 
-def row_transform_kernel(table_ref, heights_ref, out_ref):
+def row_transform_kernel(which_ref, table_ref, heights_ref, out_ref):
+    del which_ref
     frames, rows, length = heights_ref.shape
     planes = []
     for frame in range(0, frames, 2):
         pair = heights_ref[frame : frame + 2].reshape(2 * rows, length)
         product = lax.dot_general(
-            table_ref[...], pair, (((1,), (1,)), ((), ())), preferred_element_type=jnp.float32
+            table_ref[0], pair, (((1,), (1,)), ((), ())), preferred_element_type=jnp.float32
         )
         planes += [product[:, :rows], product[:, rows:]]
     out_ref[...] = jnp.swapaxes(jnp.stack(planes, 0), 0, 1).astype(jnp.bfloat16)
 
 
-def row_transform(heights, table):
+def row_transform(which, heights, table, cost):
     frames, rows, length = heights.shape
-    columns = table.shape[0]
+    columns = table.shape[1]
     if rows != LANES:
+        picked = lax.dynamic_index_in_dim(table, which, 0, keepdims=False)
         return jnp.einsum(
-            "cy,fxy->cfx", table, heights, preferred_element_type=jnp.float32
+            "cy,fxy->cfx", picked, heights, preferred_element_type=jnp.float32
         ).astype(jnp.bfloat16)
     step = 16
     return pl.pallas_call(
         row_transform_kernel,
         out_shape=jax.ShapeDtypeStruct((columns, frames, rows), jnp.bfloat16),
-        grid=(frames // step,),
-        in_specs=[
-            pl.BlockSpec((columns, length), lambda i: (0, 0)),
-            pl.BlockSpec((step, rows, length), lambda i: (i, 0, 0)),
-        ],
-        out_specs=pl.BlockSpec((columns, step, rows), lambda i: (0, i, 0)),
+        grid_spec=pltpu.PrefetchScalarGridSpec(
+            num_scalar_prefetch=1,
+            grid=(frames // step,),
+            in_specs=[
+                pl.BlockSpec((1, columns, length), lambda i, which_ref: (which_ref[0], 0, 0)),
+                pl.BlockSpec((step, rows, length), lambda i, which_ref: (i, 0, 0)),
+            ],
+            out_specs=pl.BlockSpec((columns, step, rows), lambda i, which_ref: (0, i, 0)),
+        ),
         compiler_params=pltpu.CompilerParams(vmem_limit_bytes=VMEM_BYTES),
-        cost_estimate=SMALL,
+        cost_estimate=cost,
         name="row_transform",
-    )(table, heights)
+    )(jnp.asarray(which, jnp.int32).reshape(1), table, heights)
 
 
 def gather_field(pieces_ref):
@@ -151,7 +156,7 @@
     number, size, _ = scratch.shape
     field = gather_field(pieces_ref)
     frames = field.shape[0] // 2
-    chunk = math.gcd(length, 256)
+    chunk = length
     for at in range(0, length, chunk):
         cosine, sine = column_products(field, x_ref, at, chunk)
         real_part = cosine[:frames] + sine[frames:]
@@ -185,7 +190,7 @@
     apart = jnp.where(paired, 0.0, 1.0)
     field = gather_field(pieces_ref)
     frames = field.shape[0] // 2
-    chunk = math.gcd(length, 256)
+    chunk = length
     for at in range(0, length, chunk):
         cosine, sine = column_products(field, x_ref, at, chunk)
         real_part = cosine[:frames] + apart * sine[frames:]
@@ -202,7 +207,7 @@
         mirror_ref[0] = turned.astype(jnp.bfloat16)
 
 
-def spectrum(pieces, start, number, tables, scale, paired=None):
+def spectrum(pieces, start, number, tables, scale, cost, paired=None):
     blocks, width, _, part, frames, rows = pieces.shape
     length = width * rows
     size = 2 * frames
@@ -231,7 +236,7 @@
             scratch_shapes=[pltpu.VMEM((number, size, length), jnp.bfloat16)],
         ),
         compiler_params=pltpu.CompilerParams(vmem_limit_bytes=VMEM_BYTES),
-        cost_estimate=LARGE if paired is None else SMALL,
+        cost_estimate=cost,
         name="spectrum" if paired is None else "edge_spectrum",
     )(*scalars, pieces, *tables)
 
@@ -265,12 +270,9 @@
     )(*given, *[arrays[which] for which in used])
 
 
-def assemble(arrays, places, last):
+def assemble(arrays, places):
     total = len(places)
-    late = min(row for row in range(total) if places[row][0] == last)
-    late -= late % TILE
-    while late % (total - late):
-        late -= TILE
+    late = total // 2 if total // 2 % TILE == 0 else 0
     given = []
     if late:
         given.append(write_rows([], arrays, places[:late], 0, total))
@@ -279,14 +281,28 @@
 
 def split_rows(half):
     rows = list(range(half - 1, 0, -1))
-    parts = [len(rows) * share // SHARES[-1] for share in SHARES]
-    return [sorted(rows[lo:hi]) for lo, hi in zip([0] + parts, parts) if hi > lo]
+    parts = [0] + [len(rows) * share // SHARES[-1] for share in SHARES]
+    return [sorted(rows[lo:hi]) for lo, hi in zip(parts, parts[1:])]
+
+
+def exchange(blocks, axis, dim):
+    count = lax.axis_size(axis)
+    me = lax.axis_index(axis)
+    pick = lambda at: lax.dynamic_index_in_dim(blocks, at, dim)
+    moved = [pick(me)]
+    for shift in range(1, count):
+        to = [(i, (i + shift) % count) for i in range(count)]
+        moved.append(lax.ppermute(pick((me + shift) % count), axis, to))
+    rising = moved[:1] + moved[:0:-1]
+    joined = jnp.concatenate(rising + rising[:-1], dim)
+    return lax.dynamic_slice_in_dim(joined, (count - me) % count, count, dim)
 
 
 def body(heights):
     frames, rows_dev, length = heights.shape
     tm_count = lax.axis_size("tm")
-    rows_count = lax.axis_size("rows")
+    near_count = lax.axis_size("near")
+    rows_count = 2 * near_count
     devices = tm_count * rows_count
     owned = length // devices
     half = owned // 2
@@ -301,51 +317,82 @@
 
     edges = np.array([d * owned + (half if d < middle else 0) for d in range(devices)])
 
-    def mix(heights, slot, with_edge):
+    def mix(heights, slot, with_edge, cost):
         wavenumbers = np.arange(devices)[:, None] * owned + np.asarray(slot)
         if with_edge:
             wavenumbers = np.concatenate([edges[:, None], wavenumbers], 1)
         table = y_table(length, wavenumbers, (middle, 0) if with_edge else None)
-        mixed = row_transform(heights, jnp.asarray(table))
+        mixed = row_transform(0, heights, jnp.asarray(table)[None], cost)
         return mixed.reshape(devices, -1, 2, frames, rows_dev)
 
     def arrive(mixed):
         got = lax.all_to_all(mixed, AXES, split_axis=0, concat_axis=0, tiled=True)
         return got.reshape((tm_count, rows_count) + mixed.shape[1:])
 
+    def image_of(image, partner):
+        return lax.ppermute(image, AXES, partner)
+
     slots = split_rows(half)
-    pieces = [arrive(mix(heights, slot, at == 0)) for at, slot in enumerate(slots[:2])]
     paired = (device == middle).astype(jnp.int32).reshape(1)
-    planes, images = [], []
-    for at, slot in enumerate(slots):
-        if 0 < at < len(slots) - 1:
-            pieces[at], images, edge_image = lax.optimization_barrier(
-                (pieces[at], images, edge_image)
-            )
-        plane, image = spectrum(pieces[at], int(at == 0), len(slot), tables, scale)
-        if at == 0:
-            edge, edge_image = spectrum(pieces[0], 0, 1, tables, scale, paired)
-            edge_image = lax.ppermute(edge_image, AXES, edge_partner)
-        if at + 2 < len(slots):
-            plane, image, later = lax.optimization_barrier((plane, image, heights))
-            pieces.append(arrive(mix(later, slots[at + 2], False)))
-        planes.append(plane)
-        images.append(lax.ppermute(image, AXES, opposite))
+    planes, images = {}, {}
+
+    def powers(pieces, start, at, cost):
+        if slots[at]:
+            planes[at], image = spectrum(pieces, start, len(slots[at]), tables, scale, cost)
+            images[at] = image_of(image, opposite)
+
+    def mix_half(heights, slot, which):
+        receivers = np.arange(devices).reshape(tm_count, 2, near_count).transpose(1, 0, 2)
+        wavenumbers = receivers[..., None] * owned + np.asarray(slot)
+        table = y_table(length, wavenumbers, None).reshape(2, -1, length)
+        mixed = row_transform(which, heights, jnp.asarray(table), SMALL)
+        return mixed.reshape(tm_count, 1, near_count, len(slot), 2, frames, rows_dev)
+
+    later = heights
+    side = lax.axis_index("half")
+    if slots[1]:
+        away, later = lax.optimization_barrier((mix_half(later, slots[1], 1 - side), later))
+        away = lax.ppermute(away, "half", [(0, 1), (1, 0)])
+    first, later = lax.optimization_barrier((mix(later, slots[0], True, SMALL), later))
+    second, later = lax.optimization_barrier((mix(later, slots[2], False, LARGE), later))
+    if slots[1]:
+        away, later = lax.optimization_barrier((away, later))
+        home = mix_half(later, slots[1], side)
+        aside = jnp.concatenate([home, away, home], 1)
+        aside = lax.dynamic_slice_in_dim(aside, side, 2, 1)
+        aside = exchange(exchange(aside, "near", 2), "tm", 0)
+        aside = aside.reshape((tm_count, rows_count) + aside.shape[3:])
+    first = arrive(first)
+    second = arrive(second)
+    edge, edge_image = spectrum(first, 0, 1, tables, scale, SMALL, paired)
+    edge_image = image_of(edge_image, edge_partner)
+    first, edge = lax.optimization_barrier((first, edge))
+    if slots[1]:
+        first, aside = lax.optimization_barrier((first, aside))
+    powers(first, 1, 0, LARGE)
+    if slots[1]:
+        powers(aside, 0, 1, SMALL)
+    second, edge_image, planes = lax.optimization_barrier((second, edge_image, planes))
+    powers(second, 0, 2, LARGE)
     edge_image = edge_image.astype(jnp.float32)
     lower = device < middle
-    arrays = planes + images
+    arrays = [planes[at] for at in sorted(planes)] + [images[at] for at in sorted(images)]
     last = len(arrays) - 1
     arrays += [jnp.where(lower, edge_image, edge), jnp.where(lower, edge, edge_image)]
     places = [None] * owned
     places[0], places[half] = (last + 1, 0), (last + 2, 0)
-    for at, slot in enumerate(slots):
+    for at, slot in enumerate([slot for slot in slots if slot]):
         for plane, row in enumerate(slot):
             places[row] = (at, plane)
-            places[owned - row] = (len(slots) + at, len(slot) - 1 - plane)
-    return assemble(arrays, places, last)
+            places[owned - row] = (len(planes) + at, len(slot) - 1 - plane)
+    return assemble(arrays, places)
 
 
 def solution(mesh):
-    in_specs = (P("tm", "rows", None),)
-    out_specs = P(None, ("tm", "rows"), None)
-    return jax.shard_map(body, mesh=mesh, in_specs=in_specs, out_specs=out_specs, check_vma=False)
+    tm_count, rows_count = mesh.devices.shape
+    split = jax.sharding.Mesh(
+        mesh.devices.reshape(tm_count, 2, rows_count // 2), ("tm", "half", "near")
+    )
+    in_specs = (P("tm", ("half", "near"), None),)
+    out_specs = P(None, AXES, None)
+    return jax.shard_map(body, mesh=split, in_specs=in_specs, out_specs=out_specs, check_vma=False)

time: 302 us -> 298 us (0.987)
  Pallas kernels: 110 us -> 81.5 us
  waiting for transfers between devices: 153 us -> 166 us
  local copies, waits for them, and re-layouts: 3.95 us -> 16.5 us
    ppermute x4 -> x11, waiting for transfers between devices: 30.6 us -> 130 us  [the longest x6 71.8 us: exchange(): moved.append(lax.ppermute(pick((me + shift) % count), axis, to))]
    all_to_all x3 -> x2, waiting for transfers between devices: 123 us -> 36.4 us  [arrive(): got = lax.all_to_all(mixed, AXES, split_axis=0, concat_axis=0, tiled=True)]
    pallas_call x4, Pallas kernels: 80.3 us -> 46.3 us  [spectrum(): pl.pallas_call(functools.partial(spectrum_kernel if paired is None else e...]
    all_to_all x3 -> x2, starting transfers between devices: 23.9 us -> 16.4 us  [arrive(): got = lax.all_to_all(mixed, AXES, split_axis=0, concat_axis=0, tiled=True)]
    pallas_call x3 -> x4, Pallas kernels: 22.2 us -> 29 us  [row_transform(): pl.pallas_call(row_transform_kernel, out_shape=jax.ShapeDtypeStruct((colu...]
    unnamed x12 -> x18, local copies, waits for them, and re-layouts: 3.95 us -> 10.6 us
    ppermute x4 -> x11, starting transfers between devices: 8.03 us -> 13.9 us  [the longest x4 7.1 us: image_of(): return lax.ppermute(image, AXES, partner)]
    dynamic_slice x0 -> x3, local copies, waits for them, and re-layouts: none -> 4.14 us  [the longest x1 2.31 us: exchange(): return lax.dynamic_slice_in_dim(joined, (count - me) % count, count, dim)]
  transfers between devices with their start and end apart: 7 -> 13, of which waited for: 5 -> 9; matrix products, arithmetic and copies ran while one was open for 0% -> 5% of each run, Pallas kernels for 33% -> 24%
where the time goes in v4:
time: 298 us; the launch traced here: 297 us
  waiting for transfers between devices  166 us (56%)
  Pallas kernels  81.5 us (27%)
  starting transfers between devices  30.3 us (10%)
  local copies, waits for them, and re-layouts  16.5 us (6%)
    ppermute x6, waiting for transfers between devices, exchange(): moved.append(lax.ppermute(pick((me + shift) % count), axis, to))  71.8 us
    pallas_call x4, Pallas kernels, spectrum(): pl.pallas_call(functools.partial(spectrum_kernel if paired is None else e...  46.3 us
    ppermute x4, waiting for transfers between devices, image_of(): return lax.ppermute(image, AXES, partner)  43 us
    all_to_all x2, waiting for transfers between devices, arrive(): got = lax.all_to_all(mixed, AXES, split_axis=0, concat_axis=0, tiled=True)  36.4 us
    pallas_call x4, Pallas kernels, row_transform(): pl.pallas_call(row_transform_kernel, out_shape=jax.ShapeDtypeStruct((colu...  29 us
    all_to_all x2, starting transfers between devices, arrive(): got = lax.all_to_all(mixed, AXES, split_axis=0, concat_axis=0, tiled=True)  16.4 us
    ppermute x1, waiting for transfers between devices, body(): away = lax.ppermute(away, 'half', [(0, 1), (1, 0)])  14.8 us
    unnamed x18, local copies, waits for them, and re-layouts  10.6 us
  transfers between devices with their start and end apart: 13, of which 9 were waited for; matrix products, arithmetic and copies ran while one was open for 5% of the time, Pallas kernels for 24%

profile of v4, /device:TPU:13, one launch (start us, length us, event | category | flops | bytes accessed | tf_op | source)
XLA Modules:
  0.0 297.0 jit_solution(2253065304566379767)
XLA Ops:
  0.0 5.8 %row_transform.4 = bf16[64,32,128]{2,1,0:T(8,128)(2,1)} custom-call(s32[1]{0:T(128)} %bitcast.which_ref, bf16[2,64,1024]{2,1,0:T(8,128)(2,1)} %constant.353.clone.table_ref, bf16[32,128,1024]{2,1,0:T(8,128)(2,1)} %heights_ref.4), custom_call_target="tpu_custom_call" | custom-call | flops 1048576 | bytes 1048576 | tf_op jit(solution)/shard_map/row_transform/pallas_call | solution.py:96
  5.8 2.3 collective-permute-start.1
  8.1 11.1 %row_transform.5 = bf16[640,32,128]{2,1,0:T(8,128)(2,1)} custom-call(s32[1]{0:T(128)} %constant.337.clone.1.which_ref, bf16[1,640,1024]{2,1,0:T(8,128)(2,1)} %constant.357.table_ref, bf16[32,128,1024]{2,1,0:T(8,128)(2,1)} %heights_ref.4), custom_call_target="tpu_custom_call" | custom-call | flops 1048576 | bytes 1048576 | tf_op jit(solution)/shard_map/row_transform/pallas_call | solution.py:96
  19.2 4.6 %all-to-all-start.1 = ((bf16[32,10,2,32,128]{4,3,2,1,0:T(8,128)(2,1)}), bf16[32,10,2,32,128]{4,3,2,1,0:T(8,128)(2,1)}, u32[]{:S(2)}, u32[]{:S(2)}) async-start(bf16[32,10,2,32,128]{4,3,2,1,0:T(8,128)(2,1)} %bitcast.13), calls=%async_computation.1 | async-start | bytes 10485760 | tf_op jit(solution)/shard_map/all_to_all | solution.py:329
  23.8 6.3 %row_transform.6 = bf16[256,32,128]{2,1,0:T(8,128)(2,1)} custom-call(s32[1]{0:T(128)} %constant.337.clone.1.which_ref, bf16[1,256,1024]{2,1,0:T(8,128)(2,1)} %constant.356.table_ref, bf16[32,128,1024]{2,1,0:T(8,128)(2,1)} %heights_ref.4), custom_call_target="tpu_custom_call" | custom-call | flops 1099511627776 | bytes 1048576 | tf_op jit(solution)/shard_map/row_transform/pallas_call | solution.py:96
  30.1 14.8 %collective-permute-done.1 = bf16[4,1,4,2,2,32,128]{6,5,4,3,2,1,0:T(8,128)(2,1)} collective-permute-done((bf16[4,1,4,2,2,32,128]{6,5,4,3,2,1,0:T(8,128)(2,1)}, bf16[4,1,4,2,2,32,128]{6,5,4,3,2,1,0:T(8,128)(2,1)}, u32[]{:S(2)}, u32[]{:S(2)}) %collective-permute-start.1) | collective-permute-done | bytes 524320 | tf_op jit(solution)/shard_map/ppermute | solution.py:355
  45.0 5.8 %row_transform.7 = bf16[64,32,128]{2,1,0:T(8,128)(2,1)} custom-call(s32[1]{0:T(128)} %bitcast.7.which_ref, bf16[2,64,1024]{2,1,0:T(8,128)(2,1)} %constant.353.clone.table_ref, bf16[32,128,1024]{2,1,0:T(8,128)(2,1)} %heights_ref.4), custom_call_target="tpu_custom_call" | custom-call | flops 1048576 | bytes 1048576 | tf_op jit(solution)/shard_map/row_transform/pallas_call | solution.py:96
  50.8 1.6 pad_maximum_fusion
  52.4 1.0 constant_dynamic-slice_fusion.4
  54.3 1.6 collective-permute-start.4
  56.0 61.0 %collective-permute-done.2 = bf16[4,2,1,2,2,32,128]{6,5,4,3,2,1,0:T(8,128)(2,1)} collective-permute-done((bf16[4,2,1,2,2,32,128]{6,5,4,3,2,1,0:T(8,128)(2,1)}, bf16[4,2,1,2,2,32,128]{6,5,4,3,2,1,0:T(8,128)(2,1)}, u32[]{:S(2)}, u32[]{:S(2)}) %collective-permute-start.2) | collective-permute-done | bytes 262176 | tf_op jit(solution)/shard_map/ppermute | solution.py:295
  117.9 1.0 constant_dynamic-update-slice_fusion.3
  123.5 1.2 collective-permute-start.6
  124.7 3.6 %collective-permute-done.5 = bf16[1,2,4,2,2,32,128]{6,5,4,3,2,1,0:T(8,128)(2,1)S(1)} collective-permute-done((bf16[1,2,4,2,2,32,128]{6,5,4,3,2,1,0:T(8,128)(2,1)S(1)}, bf16[1,2,4,2,2,32,128]{6,5,4,3,2,1,0:T(8,128)(2,1)S(1)}, u32[]{:S(2)}, u32[]{:S(2)}) %collective-permute-start.5) | collective-permute-done | bytes 262176 | tf_op jit(solution)/shard_map/ppermute | solution.py:295
  130.7 6.3 %collective-permute-done.7 = bf16[1,2,4,2,2,32,128]{6,5,4,3,2,1,0:T(8,128)(2,1)S(1)} collective-permute-done((bf16[1,2,4,2,2,32,128]{6,5,4,3,2,1,0:T(8,128)(2,1)S(1)}, bf16[1,2,4,2,2,32,128]{6,5,4,3,2,1,0:T(8,128)(2,1)S(1)}, u32[]{:S(2)}, u32[]{:S(2)}) %collective-permute-start.7) | collective-permute-done | bytes 262176 | tf_op jit(solution)/shard_map/ppermute | solution.py:295
  140.0 2.3 constant_dynamic-slice_fusion
  142.3 1.4 all-to-all-done.1
  143.6 11.8 %all-to-all-start = ((bf16[32,4,2,32,128]{4,3,2,1,0:T(8,128)(2,1)}), bf16[32,4,2,32,128]{4,3,2,1,0:T(8,128)(2,1)}, u32[]{:S(2)}, u32[]{:S(2)}) async-start(bf16[32,4,2,32,128]{4,3,2,1,0:T(8,128)(2,1)} %bitcast.3), calls=%async_computation | async-start | bytes 4194304 | tf_op jit(solution)/shard_map/all_to_all | solution.py:329
  155.5 6.1 %edge_spectrum.1 = (f32[1,64,1024]{2,1,0:T(8,128)}, bf16[1,64,1024]{2,1,0:T(8,128)(2,1)}) custom-call(s32[1]{0:T(128)} %bitcast.5.paired_ref, bf16[4,8,10,2,32,128]{5,4,3,2,1,0:T(8,128)(2,1)} %bitcast.6.pieces_ref, bf16[1024,2048]{1,0:T(8,128)(2,1)} %constant.349.clone.x_ref, bf16[384,256]{1,0:T(8,128)(2,1)} %constant.350.clone.window_ref, ...), custom_call_target="tpu_custom_call" | custom-call | flops 1048576 | bytes 1048576 | tf_op jit(solution)/shard_map/edge_spectrum/pallas_call | solution.py:221
  161.6 2.1 collective-permute-start
  163.7 20.9 %spectrum.3 = (f32[9,64,1024]{2,1,0:T(8,128)}, bf16[9,64,1024]{2,1,0:T(8,128)(2,1)}) custom-call(bf16[4,8,10,2,32,128]{5,4,3,2,1,0:T(8,128)(2,1)} %bitcast.6.pieces_ref, bf16[1024,2048]{1,0:T(8,128)(2,1)} %constant.349.clone.x_ref, bf16[384,256]{1,0:T(8,128)(2,1)} %constant.350.clone.window_ref, bf16[64,64]{1,0:T(8,128)(2,1)} %constant.351.clone.flip_w_ref, ...), custom_call_target="tpu_custom_call" | custom-call | flops 1099511627776 | bytes 1048576 | tf_op jit(solution)/shard_map/spectrum/pallas_call | solution.py:221
  184.6 1.5 collective-permute-start.8
  186.0 7.7 %spectrum.4 = (f32[2,64,1024]{2,1,0:T(8,128)}, bf16[2,64,1024]{2,1,0:T(8,128)(2,1)}) custom-call(bf16[4,8,2,2,32,128]{5,4,3,2,1,0:T(8,128)(2,1)} %bitcast.14, bf16[1024,2048]{1,0:T(8,128)(2,1)} %constant.349.clone.x_ref, bf16[384,256]{1,0:T(8,128)(2,1)} %constant.350.clone.window_ref, bf16[64,64]{1,0:T(8,128)(2,1)} %constant.351.clone.flip_w_ref, ...), custom_call_target="tpu_custom_call" | custom-call | flops 1048576 | bytes 1048576 | tf_op jit(solution)/shard_map/spectrum/pallas_call | solution.py:221
  193.7 35.1 %all-to-all-done = bf16[32,4,2,32,128]{4,3,2,1,0:T(8,128)(2,1)} async-done(((bf16[32,4,2,32,128]{4,3,2,1,0:T(8,128)(2,1)}), bf16[32,4,2,32,128]{4,3,2,1,0:T(8,128)(2,1)}, u32[]{:S(2)}, u32[]{:S(2)}) %all-to-all-start) | async-done | bytes 2097184 | tf_op jit(solution)/shard_map/all_to_all | solution.py:329
  228.8 6.5 %collective-permute-done = bf16[1,64,1024]{2,1,0:T(8,128)(2,1)} collective-permute-done((bf16[1,64,1024]{2,1,0:T(8,128)(2,1)}, bf16[1,64,1024]{2,1,0:T(8,128)(2,1)}, u32[]{:S(2)}, u32[]{:S(2)}) %collective-permute-start) | collective-permute-done | bytes 131104 | tf_op jit(solution)/shard_map/ppermute | solution.py:333
  235.3 11.5 %spectrum.5 = (f32[4,64,1024]{2,1,0:T(8,128)}, bf16[4,64,1024]{2,1,0:T(8,128)(2,1)}) custom-call(bf16[4,8,4,2,32,128]{5,4,3,2,1,0:T(8,128)(2,1)} %bitcast.4.pieces_ref, bf16[1024,2048]{1,0:T(8,128)(2,1)} %constant.349.clone.x_ref, bf16[384,256]{1,0:T(8,128)(2,1)} %constant.350.clone.window_ref, bf16[64,64]{1,0:T(8,128)(2,1)} %constant.351.clone.flip_w_ref, ...), custom_call_target="tpu_custom_call" | custom-call | flops 1099511627776 | bytes 1048576 | tf_op jit(solution)/shard_map/spectrum/pallas_call | solution.py:221
  246.9 3.5 %collective-permute-start.9 = (bf16[2,64,1024]{2,1,0:T(8,128)(2,1)}, bf16[2,64,1024]{2,1,0:T(8,128)(2,1)S(1)}, u32[]{:S(2)}, u32[]{:S(2)}) collective-permute-start(bf16[2,64,1024]{2,1,0:T(8,128)(2,1)} %get-tuple-element.51), channel_id=1, source_target_pairs={{0,31},{1,30},{2,29},{3,28},{4,27},{5,26},{6,25},{7,24},{8,23},{9,... | collective-permute-start | bytes 786440 | tf_op jit(solution)/shard_map/ppermute | solution.py:333
  251.4 1.7 copy-done
  253.0 1.2 copy-done.1
  254.3 2.7 write_rows.2.refs_0_
  256.9 36.5 %collective-permute-done.9.refs_2_ = bf16[2,64,1024]{2,1,0:T(8,128)(2,1)S(1)} collective-permute-done((bf16[2,64,1024]{2,1,0:T(8,128)(2,1)}, bf16[2,64,1024]{2,1,0:T(8,128)(2,1)S(1)}, u32[]{:S(2)}, u32[]{:S(2)}) %collective-permute-start.9) | collective-permute-done | bytes 262176 | tf_op jit(solution)/shard_map/ppermute | solution.py:333
  293.4 3.6 %write_rows.3 = f32[64,32,1024]{2,1,0:T(8,128)} custom-call(f32[64,32,1024]{2,1,0:T(8,128)} %write_rows.2.refs_0_, bf16[9,64,1024]{2,1,0:T(8,128)(2,1)} %collective-permute-done.8.refs_1_, bf16[2,64,1024]{2,1,0:T(8,128)(2,1)S(1)} %collective-permute-done.9.refs_2_, ...), custom_call_target="tpu_custom_call", output_to_operand_aliasing={{}: (0, {})} | custom-call | tf_op jit(solution)/shard_map/write_rows/pallas_call | solution.py:257
  (29 shorter events, 12.8 us)
Async XLA Ops:
  5.8 39.2 %collective-permute-start.1 = (bf16[4,1,4,2,2,32,128]{6,5,4,3,2,1,0:T(8,128)(2,1)}, bf16[4,1,4,2,2,32,128]{6,5,4,3,2,1,0:T(8,128)(2,1)}, u32[]{:S(2)}, u32[]{:S(2)}) collective-permute-start(bf16[4,1,4,2,2,32,128]{6,5,4,3,2,1,0:T(8,128)(2,1)} %bitcast.16), channel_id=1, source_target_pairs={{0,4},{4,0},{1,5},{5,1},{2,6},{6,2},{3,7},{7,3},{8,12},{12,8},{9,1... | collective-permute-start | bytes 1572872 | tf_op jit(solution)/shard_map/ppermute | solution.py:355
  19.2 124.5 %all-to-all-start.1 = ((bf16[32,10,2,32,128]{4,3,2,1,0:T(8,128)(2,1)}), bf16[32,10,2,32,128]{4,3,2,1,0:T(8,128)(2,1)}, u32[]{:S(2)}, u32[]{:S(2)}) async-start(bf16[32,10,2,32,128]{4,3,2,1,0:T(8,128)(2,1)} %bitcast.13), calls=%async_computation.1 | async-start | bytes 10485760 | tf_op jit(solution)/shard_map/all_to_all | solution.py:329
  53.4 63.5 %collective-permute-start.2 = (bf16[4,2,1,2,2,32,128]{6,5,4,3,2,1,0:T(8,128)(2,1)}, bf16[4,2,1,2,2,32,128]{6,5,4,3,2,1,0:T(8,128)(2,1)}, u32[]{:S(2)}, u32[]{:S(2)}) collective-permute-start(bf16[4,2,1,2,2,32,128]{6,5,4,3,2,1,0:T(8,128)(2,1)} %get-tuple-element.60), channel_id=1, source_target_pairs={{0,3},{1,0},{2,1},{3,2},{4,7},{5,4},{6,5},{7,6},{8,11},{9,8},{10,9... | collective-permute-start | bytes 786440 | tf_op jit(solution)/shard_map/ppermute | solution.py:295
  54.3 63.6 %collective-permute-start.3 = (bf16[4,2,1,2,2,32,128]{6,5,4,3,2,1,0:T(8,128)(2,1)}, bf16[4,2,1,2,2,32,128]{6,5,4,3,2,1,0:T(8,128)(2,1)}, u32[]{:S(2)}, u32[]{:S(2)}) collective-permute-start(bf16[4,2,1,2,2,32,128]{6,5,4,3,2,1,0:T(8,128)(2,1)} %get-tuple-element.59), channel_id=1, source_target_pairs={{0,2},{1,3},{2,0},{3,1},{4,6},{5,7},{6,4},{7,5},{8,10},{9,11},{10,... | collective-permute-start | bytes 786440 | tf_op jit(solution)/shard_map/ppermute | solution.py:295
  54.3 64.6 %collective-permute-start.4 = (bf16[4,2,1,2,2,32,128]{6,5,4,3,2,1,0:T(8,128)(2,1)}, bf16[4,2,1,2,2,32,128]{6,5,4,3,2,1,0:T(8,128)(2,1)}, u32[]{:S(2)}, u32[]{:S(2)}) collective-permute-start(bf16[4,2,1,2,2,32,128]{6,5,4,3,2,1,0:T(8,128)(2,1)} %get-tuple-element.57), channel_id=1, source_target_pairs={{0,1},{1,2},{2,3},{3,0},{4,5},{5,6},{6,7},{7,4},{8,9},{9,10},{10,1... | collective-permute-start | bytes 786440 | tf_op jit(solution)/shard_map/ppermute | solution.py:295
  122.8 5.5 %collective-permute-start.5 = (bf16[1,2,4,2,2,32,128]{6,5,4,3,2,1,0:T(8,128)(2,1)S(1)}, bf16[1,2,4,2,2,32,128]{6,5,4,3,2,1,0:T(8,128)(2,1)S(1)}, u32[]{:S(2)}, u32[]{:S(2)}) collective-permute-start(bf16[1,2,4,2,2,32,128]{6,5,4,3,2,1,0:T(8,128)(2,1)S(1)} %get-tuple-element.56), channel_id=1, source_target_pairs={{0,24},{8,0},{16,8},{24,16},{1,25},{9,1},{17,9},{25,17},{2,26},{10... | collective-permute-start | bytes 786440 | tf_op jit(solution)/shard_map/ppermute | solution.py:295
  123.5 6.4 %collective-permute-start.6 = (bf16[1,2,4,2,2,32,128]{6,5,4,3,2,1,0:T(8,128)(2,1)S(1)}, bf16[1,2,4,2,2,32,128]{6,5,4,3,2,1,0:T(8,128)(2,1)S(1)}, u32[]{:S(2)}, u32[]{:S(2)}) collective-permute-start(bf16[1,2,4,2,2,32,128]{6,5,4,3,2,1,0:T(8,128)(2,1)S(1)} %get-tuple-element.55), channel_id=1, source_target_pairs={{0,16},{8,24},{16,0},{24,8},{1,17},{9,25},{17,1},{25,9},{2,18},{10... | collective-permute-start | bytes 786440 | tf_op jit(solution)/shard_map/ppermute | solution.py:295
  124.7 12.3 %collective-permute-start.7 = (bf16[1,2,4,2,2,32,128]{6,5,4,3,2,1,0:T(8,128)(2,1)S(1)}, bf16[1,2,4,2,2,32,128]{6,5,4,3,2,1,0:T(8,128)(2,1)S(1)}, u32[]{:S(2)}, u32[]{:S(2)}) collective-permute-start(bf16[1,2,4,2,2,32,128]{6,5,4,3,2,1,0:T(8,128)(2,1)S(1)} %get-tuple-element.53), channel_id=1, source_target_pairs={{0,8},{8,16},{16,24},{24,0},{1,9},{9,17},{17,25},{25,1},{2,10},{10... | collective-permute-start | bytes 786440 | tf_op jit(solution)/shard_map/ppermute | solution.py:295
  143.6 85.2 %all-to-all-start = ((bf16[32,4,2,32,128]{4,3,2,1,0:T(8,128)(2,1)}), bf16[32,4,2,32,128]{4,3,2,1,0:T(8,128)(2,1)}, u32[]{:S(2)}, u32[]{:S(2)}) async-start(bf16[32,4,2,32,128]{4,3,2,1,0:T(8,128)(2,1)} %bitcast.3), calls=%async_computation | async-start | bytes 4194304 | tf_op jit(solution)/shard_map/all_to_all | solution.py:329
  161.6 73.7 %collective-permute-start = (bf16[1,64,1024]{2,1,0:T(8,128)(2,1)}, bf16[1,64,1024]{2,1,0:T(8,128)(2,1)}, u32[]{:S(2)}, u32[]{:S(2)}) collective-permute-start(bf16[1,64,1024]{2,1,0:T(8,128)(2,1)} %get-tuple-element.33), channel_id=1, source_target_pairs={{0,31},{1,30},{2,29},{3,28},{4,27},{5,26},{6,25},{7,24},{8,23},{9,... | collective-permute-start | bytes 393224 | tf_op jit(solution)/shard_map/ppermute | solution.py:333
  184.6 108.9 %collective-permute-start.8 = (bf16[9,64,1024]{2,1,0:T(8,128)(2,1)}, bf16[9,64,1024]{2,1,0:T(8,128)(2,1)}, u32[]{:S(2)}, u32[]{:S(2)}) collective-permute-start(bf16[9,64,1024]{2,1,0:T(8,128)(2,1)} %get-tuple-element.50), channel_id=1, source_target_pairs={{0,31},{1,30},{2,29},{3,28},{4,27},{5,26},{6,25},{7,24},{8,23},{9,... | collective-permute-start | bytes 3538952 | tf_op jit(solution)/shard_map/ppermute | solution.py:333
  235.3 15.1 %copy-start.3 = (f32[1,64,1024]{2,1,0:T(8,128)S(1)}, f32[1,64,1024]{2,1,0:T(8,128)}, u32[]{:S(2)}) copy-start(f32[1,64,1024]{2,1,0:T(8,128)} %get-tuple-element.49) | copy-start | bytes 786436
  235.3 16.1 %copy-start.2 = (f32[2,64,1024]{2,1,0:T(8,128)S(1)}, f32[2,64,1024]{2,1,0:T(8,128)}, u32[]{:S(2)}) copy-start(f32[2,64,1024]{2,1,0:T(8,128)} %get-tuple-element.45.refs_1_) | copy-start | bytes 1572868
  246.9 46.6 %collective-permute-start.10 = (bf16[4,64,1024]{2,1,0:T(8,128)(2,1)}, bf16[4,64,1024]{2,1,0:T(8,128)(2,1)S(1)}, u32[]{:S(2)}, u32[]{:S(2)}) collective-permute-start(bf16[4,64,1024]{2,1,0:T(8,128)(2,1)} %get-tuple-element.52), channel_id=1, source_target_pairs={{0,31},{1,30},{2,29},{3,28},{4,27},{5,26},{6,25},{7,24},{8,23},{9,... | collective-permute-start | bytes 1572872 | tf_op jit(solution)/shard_map/ppermute | solution.py:333
  246.9 46.6 %collective-permute-start.9 = (bf16[2,64,1024]{2,1,0:T(8,128)(2,1)}, bf16[2,64,1024]{2,1,0:T(8,128)(2,1)S(1)}, u32[]{:S(2)}, u32[]{:S(2)}) collective-permute-start(bf16[2,64,1024]{2,1,0:T(8,128)(2,1)} %get-tuple-element.51), channel_id=1, source_target_pairs={{0,31},{1,30},{2,29},{3,28},{4,27},{5,26},{6,25},{7,24},{8,23},{9,... | collective-permute-start | bytes 786440 | tf_op jit(solution)/shard_map/ppermute | solution.py:333
  251.4 1.7 copy-start
  253.0 1.2 copy-start.1

commit v5 on v4

--- a/solution.py
+++ b/solution.py
@@ -13,7 +13,7 @@
 AXES = ("tm", "half", "near")
 LANES = 128
 TILE = 8
-SHARES = (9, 11, 15)
+SHARES = (8, 10, 11, 15)
 SMALL = pl.CostEstimate(flops=1 << 20, bytes_accessed=1 << 20, transcendentals=0)
 LARGE = pl.CostEstimate(flops=1 << 40, bytes_accessed=1 << 20, transcendentals=0)
 VMEM_BYTES = 63 * 1024 * 1024
@@ -348,20 +348,33 @@
         mixed = row_transform(which, heights, jnp.asarray(table), SMALL)
         return mixed.reshape(tm_count, 1, near_count, len(slot), 2, frames, rows_dev)
 
+    def joined(home, away):
+        return lax.dynamic_slice_in_dim(jnp.concatenate([home, away, home], 1), side, 2, 1)
+
+    def swapped(away):
+        return lax.ppermute(away, "half", [(0, 1), (1, 0)])
+
+    def pieces_of(parts):
+        parts = exchange(parts, "tm", 0)
+        return parts.reshape((tm_count, rows_count) + parts.shape[3:])
+
     later = heights
     side = lax.axis_index("half")
     if slots[1]:
-        away, later = lax.optimization_barrier((mix_half(later, slots[1], 1 - side), later))
-        away = lax.ppermute(away, "half", [(0, 1), (1, 0)])
+        aside, later = lax.optimization_barrier((mix_half(later, slots[1], 1 - side), later))
+        aside = swapped(aside)
     first, later = lax.optimization_barrier((mix(later, slots[0], True, SMALL), later))
-    second, later = lax.optimization_barrier((mix(later, slots[2], False, LARGE), later))
+    second, later = lax.optimization_barrier((mix(later, slots[3], False, LARGE), later))
     if slots[1]:
-        away, later = lax.optimization_barrier((away, later))
-        home = mix_half(later, slots[1], side)
-        aside = jnp.concatenate([home, away, home], 1)
-        aside = lax.dynamic_slice_in_dim(aside, side, 2, 1)
-        aside = exchange(exchange(aside, "near", 2), "tm", 0)
-        aside = aside.reshape((tm_count, rows_count) + aside.shape[3:])
+        aside, later = lax.optimization_barrier((aside, later))
+        aside = exchange(joined(mix_half(later, slots[1], side), aside), "near", 2)
+    if slots[2]:
+        late, late_home = mix_half(later, slots[2], 1 - side), mix_half(later, slots[2], side)
+        if slots[1]:
+            late, late_home, aside = lax.optimization_barrier((late, late_home, aside))
+        late = swapped(late)
+    if slots[1]:
+        aside = pieces_of(aside)
     first = arrive(first)
     second = arrive(second)
     edge, edge_image = spectrum(first, 0, 1, tables, scale, SMALL, paired)
@@ -369,11 +382,18 @@
     first, edge = lax.optimization_barrier((first, edge))
     if slots[1]:
         first, aside = lax.optimization_barrier((first, aside))
+    if slots[2]:
+        first, late = lax.optimization_barrier((first, late))
     powers(first, 1, 0, LARGE)
     if slots[1]:
         powers(aside, 0, 1, SMALL)
     second, edge_image, planes = lax.optimization_barrier((second, edge_image, planes))
-    powers(second, 0, 2, LARGE)
+    powers(second, 0, 3, LARGE)
+    if slots[2]:
+        late = exchange(joined(late_home, late), "near", 2)
+        late, planes = lax.optimization_barrier((late, planes))
+        late, images[0] = lax.optimization_barrier((pieces_of(late), images[0]))
+        powers(late, 0, 2, SMALL)
     edge_image = edge_image.astype(jnp.float32)
     lower = device < middle
     arrays = [planes[at] for at in sorted(planes)] + [images[at] for at in sorted(images)]

time: 298 us -> 287 us (0.963)
  waiting for transfers between devices: 166 us -> 125 us
  Pallas kernels: 81.5 us -> 95.9 us
  local copies, waits for them, and re-layouts: 16.5 us -> 25.3 us
  starting transfers between devices: 30.3 us -> 36.5 us
    ppermute x6 -> x12, waiting for transfers between devices: 71.8 us -> 51.5 us  [exchange(): moved.append(lax.ppermute(pick((me + shift) % count), axis, to))]
    ppermute x4 -> x5, waiting for transfers between devices: 43 us -> 28.5 us  [image_of(): return lax.ppermute(image, AXES, partner)]
    pallas_call x4 -> x6, Pallas kernels: 29 us -> 39.5 us  [row_transform(): pl.pallas_call(row_transform_kernel, out_shape=jax.ShapeDtypeStruct((colu...]
    all_to_all x2, waiting for transfers between devices: 36.4 us -> 27.2 us  [arrive(): got = lax.all_to_all(mixed, AXES, split_axis=0, concat_axis=0, tiled=True)]
    ppermute x6 -> x12, starting transfers between devices: 4.45 us -> 10.8 us  [exchange(): moved.append(lax.ppermute(pick((me + shift) % count), axis, to))]
    unnamed x18 -> x38, local copies, waits for them, and re-layouts: 10.6 us -> 16.5 us
    all_to_all x2, starting transfers between devices: 16.4 us -> 11.5 us  [arrive(): got = lax.all_to_all(mixed, AXES, split_axis=0, concat_axis=0, tiled=True)]
    ppermute x1 -> x2, starting transfers between devices: 2.31 us -> 7.02 us  [swapped(): return lax.ppermute(away, 'half', [(0, 1), (1, 0)])]
  transfers between devices with their start and end apart: 13 -> 21, of which waited for: 9 -> 12; matrix products, arithmetic and copies ran while one was open for 5% -> 8% of each run, Pallas kernels for 24% -> 30%
where the time goes in v5:
time: 287 us
  waiting for transfers between devices  125 us (44%)
  Pallas kernels  95.9 us (33%)
  starting transfers between devices  36.5 us (13%)
  local copies, waits for them, and re-layouts  25.3 us (9%)
  other arithmetic  3.59 us (1%)
    ppermute x12, waiting for transfers between devices, exchange(): moved.append(lax.ppermute(pick((me + shift) % count), axis, to))  51.5 us
    pallas_call x5, Pallas kernels, spectrum(): pl.pallas_call(functools.partial(spectrum_kernel if paired is None else e...  50.2 us
    pallas_call x6, Pallas kernels, row_transform(): pl.pallas_call(row_transform_kernel, out_shape=jax.ShapeDtypeStruct((colu...  39.5 us
    ppermute x5, waiting for transfers between devices, image_of(): return lax.ppermute(image, AXES, partner)  28.5 us
    all_to_all x2, waiting for transfers between devices, arrive(): got = lax.all_to_all(mixed, AXES, split_axis=0, concat_axis=0, tiled=True)  27.2 us
    ppermute x2, waiting for transfers between devices, swapped(): return lax.ppermute(away, 'half', [(0, 1), (1, 0)])  17.9 us
    unnamed x38, local copies, waits for them, and re-layouts  16.5 us
    all_to_all x2, starting transfers between devices, arrive(): got = lax.all_to_all(mixed, AXES, split_axis=0, concat_axis=0, tiled=True)  11.5 us
  transfers between devices with their start and end apart: 21, of which 12 were waited for; matrix products, arithmetic and copies ran while one was open for 8% of the time, Pallas kernels for 30%

profile of v5, /device:TPU:13, one launch (start us, length us, event | category | flops | bytes accessed | tf_op | source)
XLA Modules:
  0.0 286.6 jit_solution(16921266586613688533)
XLA Ops:
  0.0 5.8 %row_transform.6 = bf16[64,32,128]{2,1,0:T(8,128)(2,1)} custom-call(s32[1]{0:T(128)} %bitcast.which_ref, bf16[2,64,1024]{2,1,0:T(8,128)(2,1)} %constant.391.clone.table_ref, bf16[32,128,1024]{2,1,0:T(8,128)(2,1)} %heights_ref.6), custom_call_target="tpu_custom_call" | custom-call | flops 1048576 | bytes 1048576 | tf_op jit(solution)/shard_map/row_transform/pallas_call | solution.py:96
  5.8 2.3 collective-permute-start
  8.1 10.3 %row_transform.7 = bf16[576,32,128]{2,1,0:T(8,128)(2,1)} custom-call(s32[1]{0:T(128)} %constant.378.clone.1.which_ref, bf16[1,576,1024]{2,1,0:T(8,128)(2,1)} %constant.396.table_ref, bf16[32,128,1024]{2,1,0:T(8,128)(2,1)} %heights_ref.6), custom_call_target="tpu_custom_call" | custom-call | flops 1048576 | bytes 1048576 | tf_op jit(solution)/shard_map/row_transform/pallas_call | solution.py:96
  18.4 4.6 %all-to-all-start = ((bf16[32,9,2,32,128]{4,3,2,1,0:T(8,128)(2,1)}), bf16[32,9,2,32,128]{4,3,2,1,0:T(8,128)(2,1)}, u32[]{:S(2)}, u32[]{:S(2)}) async-start(bf16[32,9,2,32,128]{4,3,2,1,0:T(8,128)(2,1)} %bitcast.18), calls=%async_computation | async-start | bytes 9437184 | tf_op jit(solution)/shard_map/all_to_all | solution.py:329
  23.1 6.4 %row_transform.8 = bf16[256,32,128]{2,1,0:T(8,128)(2,1)} custom-call(s32[1]{0:T(128)} %constant.378.clone.1.which_ref, bf16[1,256,1024]{2,1,0:T(8,128)(2,1)} %constant.395.table_ref, bf16[32,128,1024]{2,1,0:T(8,128)(2,1)} %heights_ref.6), custom_call_target="tpu_custom_call" | custom-call | flops 1099511627776 | bytes 1048576 | tf_op jit(solution)/shard_map/row_transform/pallas_call | solution.py:96
  29.4 17.9 %collective-permute-done = bf16[4,1,4,2,2,32,128]{6,5,4,3,2,1,0:T(8,128)(2,1)} collective-permute-done((bf16[4,1,4,2,2,32,128]{6,5,4,3,2,1,0:T(8,128)(2,1)}, bf16[4,1,4,2,2,32,128]{6,5,4,3,2,1,0:T(8,128)(2,1)}, u32[]{:S(2)}, u32[]{:S(2)}) %collective-permute-start) | collective-permute-done | bytes 524320 | tf_op jit(solution)/shard_map/ppermute | solution.py:355
  47.3 5.8 %row_transform.11 = bf16[64,32,128]{2,1,0:T(8,128)(2,1)} custom-call(s32[1]{0:T(128)} %bitcast.6.which_ref, bf16[2,64,1024]{2,1,0:T(8,128)(2,1)} %constant.391.clone.table_ref, bf16[32,128,1024]{2,1,0:T(8,128)(2,1)} %heights_ref.6), custom_call_target="tpu_custom_call" | custom-call | flops 1048576 | bytes 1048576 | tf_op jit(solution)/shard_map/row_transform/pallas_call | solution.py:96
  59.5 5.6 %row_transform.9 = bf16[32,32,128]{2,1,0:T(8,128)(2,1)} custom-call(s32[1]{0:T(128)} %bitcast.which_ref, bf16[2,32,1024]{2,1,0:T(8,128)(2,1)} %constant.394.clone.table_ref, bf16[32,128,1024]{2,1,0:T(8,128)(2,1)} %heights_ref.6), custom_call_target="tpu_custom_call" | custom-call | flops 1048576 | bytes 1048576 | tf_op jit(solution)/shard_map/row_transform/pallas_call | solution.py:96
  65.1 5.6 %row_transform.10 = bf16[32,32,128]{2,1,0:T(8,128)(2,1)} custom-call(s32[1]{0:T(128)} %bitcast.6.which_ref, bf16[2,32,1024]{2,1,0:T(8,128)(2,1)} %constant.394.clone.table_ref, bf16[32,128,1024]{2,1,0:T(8,128)(2,1)} %heights_ref.6), custom_call_target="tpu_custom_call" | custom-call | flops 1048576 | bytes 1048576 | tf_op jit(solution)/shard_map/row_transform/pallas_call | solution.py:96
  70.7 36.8 %collective-permute-done.1 = bf16[4,2,1,2,2,32,128]{6,5,4,3,2,1,0:T(8,128)(2,1)S(1)} collective-permute-done((bf16[4,2,1,2,2,32,128]{6,5,4,3,2,1,0:T(8,128)(2,1)}, bf16[4,2,1,2,2,32,128]{6,5,4,3,2,1,0:T(8,128)(2,1)S(1)}, u32[]{:S(2)}, u32[]{:S(2)}) %collective-permute-start.1) | collective-permute-done | bytes 262176 | tf_op jit(solution)/shard_map/ppermute | solution.py:295
  117.1 4.7 %collective-permute-start.7 = (bf16[4,1,4,1,2,32,128]{6,5,4,2,1,0,3:T(8,128)(2,1)}, bf16[4,1,4,1,2,32,128]{6,5,4,2,1,0,3:T(8,128)(2,1)}, u32[]{:S(2)}, u32[]{:S(2)}) collective-permute-start(bf16[4,1,4,1,2,32,128]{6,5,4,2,1,0,3:T(8,128)(2,1)} %bitcast.24), channel_id=1, source_target_pairs={{0,4},{4,0},{1,5},{5,1},{2,6},{6,2},{3,7},{7,3},{8,12},{12,8},{9,1... | collective-permute-start | bytes 786440 | tf_op jit(solution)/shard_map/ppermute | solution.py:355
  121.9 3.0 %collective-permute-done.4 = bf16[1,2,4,2,2,32,128]{6,5,4,3,2,1,0:T(8,128)(2,1)S(1)} collective-permute-done((bf16[1,2,4,2,2,32,128]{6,5,4,3,2,1,0:T(8,128)(2,1)}, bf16[1,2,4,2,2,32,128]{6,5,4,3,2,1,0:T(8,128)(2,1)S(1)}, u32[]{:S(2)}, u32[]{:S(2)}) %collective-permute-start.4) | collective-permute-done | bytes 262176 | tf_op jit(solution)/shard_map/ppermute | solution.py:295
  124.9 5.5 %collective-permute-done.6 = bf16[1,2,4,2,2,32,128]{6,5,4,3,2,1,0:T(8,128)(2,1)} collective-permute-done((bf16[1,2,4,2,2,32,128]{6,5,4,3,2,1,0:T(8,128)(2,1)}, bf16[1,2,4,2,2,32,128]{6,5,4,3,2,1,0:T(8,128)(2,1)}, u32[]{:S(2)}, u32[]{:S(2)}) %collective-permute-start.6) | collective-permute-done | bytes 262176 | tf_op jit(solution)/shard_map/ppermute | solution.py:295
  132.7 5.4 %all-to-all-done = bf16[32,9,2,32,128]{4,3,2,1,0:T(8,128)(2,1)} async-done(((bf16[32,9,2,32,128]{4,3,2,1,0:T(8,128)(2,1)}), bf16[32,9,2,32,128]{4,3,2,1,0:T(8,128)(2,1)}, u32[]{:S(2)}, u32[]{:S(2)}) %all-to-all-start) | async-done | bytes 4718624 | tf_op jit(solution)/shard_map/all_to_all | solution.py:329
  138.1 6.9 %all-to-all-start.1 = ((bf16[32,4,2,32,128]{4,3,2,1,0:T(8,128)(2,1)}), bf16[32,4,2,32,128]{4,3,2,1,0:T(8,128)(2,1)}, u32[]{:S(2)}, u32[]{:S(2)}) async-start(bf16[32,4,2,32,128]{4,3,2,1,0:T(8,128)(2,1)} %bitcast.4), calls=%async_computation.1 | async-start | bytes 4194304 | tf_op jit(solution)/shard_map/all_to_all | solution.py:329
  145.0 6.2 %edge_spectrum.1 = (f32[1,64,1024]{2,1,0:T(8,128)}, bf16[1,64,1024]{2,1,0:T(8,128)(2,1)}) custom-call(s32[1]{0:T(128)} %bitcast.12.paired_ref, bf16[4,8,9,2,32,128]{5,4,3,2,1,0:T(8,128)(2,1)} %bitcast.11.pieces_ref, bf16[1024,2048]{1,0:T(8,128)(2,1)} %constant.387.clone.x_ref, bf16[384,256]{1,0:T(8,128)(2,1)} %constant.388.clone.window_ref, ...), custom_call_target="tpu_custom_call" | custom-call | flops 1048576 | bytes 1048576 | tf_op jit(solution)/shard_map/edge_spectrum/pallas_call | solution.py:221
  151.1 2.1 collective-permute-start.11
  156.1 3.0 %collective-permute-start.9 = (bf16[4,2,1,1,2,32,128]{6,5,4,2,1,0,3:T(8,128)(2,1)}, bf16[4,2,1,1,2,32,128]{6,5,4,2,1,0,3:T(8,128)(2,1)}, u32[]{:S(2)}, u32[]{:S(2)}) collective-permute-start(bf16[4,2,1,1,2,32,128]{6,5,4,2,1,0,3:T(8,128)(2,1)} %get-tuple-element.89), channel_id=1, source_target_pairs={{0,2},{1,3},{2,0},{3,1},{4,6},{5,7},{6,4},{7,5},{8,10},{9,11},{10,... | collective-permute-start | bytes 393224 | tf_op jit(solution)/shard_map/ppermute | solution.py:295
  159.1 19.0 %spectrum.4 = (f32[8,64,1024]{2,1,0:T(8,128)}, bf16[8,64,1024]{2,1,0:T(8,128)(2,1)}) custom-call(bf16[4,8,9,2,32,128]{5,4,3,2,1,0:T(8,128)(2,1)} %bitcast.11.pieces_ref, bf16[1024,2048]{1,0:T(8,128)(2,1)} %constant.387.clone.x_ref, bf16[384,256]{1,0:T(8,128)(2,1)} %constant.388.clone.window_ref, bf16[64,64]{1,0:T(8,128)(2,1)} %constant.389.clone.flip_w_ref, ...), custom_call_target="tpu_custom_call" | custom-call | flops 1099511627776 | bytes 1048576 | tf_op jit(solution)/shard_map/spectrum/pallas_call | solution.py:221
  179.5 7.7 %spectrum.5 = (f32[2,64,1024]{2,1,0:T(8,128)}, bf16[2,64,1024]{2,1,0:T(8,128)(2,1)}) custom-call(bf16[4,8,2,2,32,128]{5,4,3,2,1,0:T(8,128)(2,1)} %bitcast.19, bf16[1024,2048]{1,0:T(8,128)(2,1)} %constant.387.clone.x_ref, bf16[384,256]{1,0:T(8,128)(2,1)} %constant.388.clone.window_ref, bf16[64,64]{1,0:T(8,128)(2,1)} %constant.389.clone.flip_w_ref, ...), custom_call_target="tpu_custom_call" | custom-call | flops 1048576 | bytes 1048576 | tf_op jit(solution)/shard_map/spectrum/pallas_call | solution.py:221
  193.7 21.8 %all-to-all-done.1 = bf16[32,4,2,32,128]{4,3,2,1,0:T(8,128)(2,1)} async-done(((bf16[32,4,2,32,128]{4,3,2,1,0:T(8,128)(2,1)}), bf16[32,4,2,32,128]{4,3,2,1,0:T(8,128)(2,1)}, u32[]{:S(2)}, u32[]{:S(2)}) %all-to-all-start.1) | async-done | bytes 2097184 | tf_op jit(solution)/shard_map/all_to_all | solution.py:329
  215.5 6.5 %collective-permute-done.11 = bf16[1,64,1024]{2,1,0:T(8,128)(2,1)} collective-permute-done((bf16[1,64,1024]{2,1,0:T(8,128)(2,1)}, bf16[1,64,1024]{2,1,0:T(8,128)(2,1)}, u32[]{:S(2)}, u32[]{:S(2)}) %collective-permute-start.11) | collective-permute-done | bytes 131104 | tf_op jit(solution)/shard_map/ppermute | solution.py:333
  222.0 11.5 %spectrum.6 = (f32[4,64,1024]{2,1,0:T(8,128)}, bf16[4,64,1024]{2,1,0:T(8,128)(2,1)}) custom-call(bf16[4,8,4,2,32,128]{5,4,3,2,1,0:T(8,128)(2,1)} %bitcast.15.pieces_ref, bf16[1024,2048]{1,0:T(8,128)(2,1)} %constant.387.clone.x_ref, bf16[384,256]{1,0:T(8,128)(2,1)} %constant.388.clone.window_ref, bf16[64,64]{1,0:T(8,128)(2,1)} %constant.389.clone.flip_w_ref, ...), custom_call_target="tpu_custom_call" | custom-call | flops 1099511627776 | bytes 1048576 | tf_op jit(solution)/shard_map/spectrum/pallas_call | solution.py:221
  236.6 2.1 collective-permute-start.18
  238.7 2.2 collective-permute-done.12
  242.7 4.0 %collective-permute-done.14 = bf16[1,2,4,1,2,32,128]{6,5,4,2,1,0,3:T(8,128)(2,1)S(1)} collective-permute-done((bf16[1,2,4,1,2,32,128]{6,5,4,2,1,0,3:T(8,128)(2,1)S(1)}, bf16[1,2,4,1,2,32,128]{6,5,4,2,1,0,3:T(8,128)(2,1)S(1)}, u32[]{:S(2)}, u32[]{:S(2)}) %collective-permute-start.14) | collective-permute-done | bytes 131104 | tf_op jit(solution)/shard_map/ppermute | solution.py:295
  247.6 13.6 %collective-permute-done.15.refs_1_ = bf16[8,64,1024]{2,1,0:T(8,128)(2,1)} collective-permute-done((bf16[8,64,1024]{2,1,0:T(8,128)(2,1)}, bf16[8,64,1024]{2,1,0:T(8,128)(2,1)}, u32[]{:S(2)}, u32[]{:S(2)}) %collective-permute-start.15) | collective-permute-done | bytes 1048608 | tf_op jit(solution)/shard_map/ppermute | solution.py:333
  261.3 5.8 %spectrum.7 = (f32[1,64,1024]{2,1,0:T(8,128)}, bf16[1,64,1024]{2,1,0:T(8,128)(2,1)}) custom-call(bf16[4,8,1,2,32,128]{5,4,3,2,1,0:T(8,128)(2,1)} %bitcast.21, bf16[1024,2048]{1,0:T(8,128)(2,1)} %constant.387.clone.x_ref, bf16[384,256]{1,0:T(8,128)(2,1)} %constant.388.clone.window_ref, bf16[64,64]{1,0:T(8,128)(2,1)} %constant.389.clone.flip_w_ref, ...), custom_call_target="tpu_custom_call" | custom-call | flops 1048576 | bytes 1048576 | tf_op jit(solution)/shard_map/spectrum/pallas_call | solution.py:221
  271.9 2.7 write_rows.2.refs_0_
  274.6 6.3 %collective-permute-done.18.refs_4_ = bf16[4,64,1024]{2,1,0:T(8,128)(2,1)} collective-permute-done((bf16[4,64,1024]{2,1,0:T(8,128)(2,1)}, bf16[4,64,1024]{2,1,0:T(8,128)(2,1)}, u32[]{:S(2)}, u32[]{:S(2)}) %collective-permute-start.18) | collective-permute-done | bytes 524320 | tf_op jit(solution)/shard_map/ppermute | solution.py:333
  280.9 2.0 collective-permute-done.17.refs_3_
  283.0 3.6 %write_rows.3 = f32[64,32,1024]{2,1,0:T(8,128)} custom-call(f32[64,32,1024]{2,1,0:T(8,128)} %write_rows.2.refs_0_, bf16[8,64,1024]{2,1,0:T(8,128)(2,1)} %collective-permute-done.15.refs_1_, bf16[2,64,1024]{2,1,0:T(8,128)(2,1)S(1)} %collective-permute-done.16.refs_2_, ...), custom_call_target="tpu_custom_call", output_to_operand_aliasing={{}: (0, {})} | custom-call | tf_op jit(solution)/shard_map/write_rows/pallas_call | solution.py:257
  (76 shorter events, 39.8 us)
Async XLA Ops:
  5.8 41.4 %collective-permute-start = (bf16[4,1,4,2,2,32,128]{6,5,4,3,2,1,0:T(8,128)(2,1)}, bf16[4,1,4,2,2,32,128]{6,5,4,3,2,1,0:T(8,128)(2,1)}, u32[]{:S(2)}, u32[]{:S(2)}) collective-permute-start(bf16[4,1,4,2,2,32,128]{6,5,4,3,2,1,0:T(8,128)(2,1)} %bitcast.23), channel_id=1, source_target_pairs={{0,4},{4,0},{1,5},{5,1},{2,6},{6,2},{3,7},{7,3},{8,12},{12,8},{9,1... | collective-permute-start | bytes 1572872 | tf_op jit(solution)/shard_map/ppermute | solution.py:355
  18.4 119.6 %all-to-all-start = ((bf16[32,9,2,32,128]{4,3,2,1,0:T(8,128)(2,1)}), bf16[32,9,2,32,128]{4,3,2,1,0:T(8,128)(2,1)}, u32[]{:S(2)}, u32[]{:S(2)}) async-start(bf16[32,9,2,32,128]{4,3,2,1,0:T(8,128)(2,1)} %bitcast.18), calls=%async_computation | async-start | bytes 9437184 | tf_op jit(solution)/shard_map/all_to_all | solution.py:329
  54.6 1.2 copy-start.4
  57.0 50.5 %collective-permute-start.1 = (bf16[4,2,1,2,2,32,128]{6,5,4,3,2,1,0:T(8,128)(2,1)}, bf16[4,2,1,2,2,32,128]{6,5,4,3,2,1,0:T(8,128)(2,1)S(1)}, u32[]{:S(2)}, u32[]{:S(2)}) collective-permute-start(bf16[4,2,1,2,2,32,128]{6,5,4,3,2,1,0:T(8,128)(2,1)} %get-tuple-element.82), channel_id=1, source_target_pairs={{0,3},{1,0},{2,1},{3,2},{4,7},{5,4},{6,5},{7,6},{8,11},{9,8},{10,9... | collective-permute-start | bytes 786440 | tf_op jit(solution)/shard_map/ppermute | solution.py:295
  57.9 50.3 %collective-permute-start.2 = (bf16[4,2,1,2,2,32,128]{6,5,4,3,2,1,0:T(8,128)(2,1)}, bf16[4,2,1,2,2,32,128]{6,5,4,3,2,1,0:T(8,128)(2,1)S(1)}, u32[]{:S(2)}, u32[]{:S(2)}) collective-permute-start(bf16[4,2,1,2,2,32,128]{6,5,4,3,2,1,0:T(8,128)(2,1)} %get-tuple-element.81), channel_id=1, source_target_pairs={{0,2},{1,3},{2,0},{3,1},{4,6},{5,7},{6,4},{7,5},{8,10},{9,11},{10,... | collective-permute-start | bytes 786440 | tf_op jit(solution)/shard_map/ppermute | solution.py:295
  57.9 51.1 %collective-permute-start.3 = (bf16[4,2,1,2,2,32,128]{6,5,4,3,2,1,0:T(8,128)(2,1)}, bf16[4,2,1,2,2,32,128]{6,5,4,3,2,1,0:T(8,128)(2,1)S(1)}, u32[]{:S(2)}, u32[]{:S(2)}) collective-permute-start(bf16[4,2,1,2,2,32,128]{6,5,4,3,2,1,0:T(8,128)(2,1)} %get-tuple-element.79), channel_id=1, source_target_pairs={{0,1},{1,2},{2,3},{3,0},{4,5},{5,6},{6,7},{7,4},{8,9},{9,10},{10,1... | collective-permute-start | bytes 786440 | tf_op jit(solution)/shard_map/ppermute | solution.py:295
  115.2 9.6 %collective-permute-start.4 = (bf16[1,2,4,2,2,32,128]{6,5,4,3,2,1,0:T(8,128)(2,1)}, bf16[1,2,4,2,2,32,128]{6,5,4,3,2,1,0:T(8,128)(2,1)S(1)}, u32[]{:S(2)}, u32[]{:S(2)}) collective-permute-start(bf16[1,2,4,2,2,32,128]{6,5,4,3,2,1,0:T(8,128)(2,1)} %get-tuple-element.86), channel_id=1, source_target_pairs={{0,24},{8,0},{16,8},{24,16},{1,25},{9,1},{17,9},{25,17},{2,26},{10... | collective-permute-start | bytes 786440 | tf_op jit(solution)/shard_map/ppermute | solution.py:295
  116.0 8.9 %collective-permute-start.5 = (bf16[1,2,4,2,2,32,128]{6,5,4,3,2,1,0:T(8,128)(2,1)}, bf16[1,2,4,2,2,32,128]{6,5,4,3,2,1,0:T(8,128)(2,1)S(1)}, u32[]{:S(2)}, u32[]{:S(2)}) collective-permute-start(bf16[1,2,4,2,2,32,128]{6,5,4,3,2,1,0:T(8,128)(2,1)} %get-tuple-element.85), channel_id=1, source_target_pairs={{0,16},{8,24},{16,0},{24,8},{1,17},{9,25},{17,1},{25,9},{2,18},{10... | collective-permute-start | bytes 786440 | tf_op jit(solution)/shard_map/ppermute | solution.py:295
  117.1 13.3 %collective-permute-start.6 = (bf16[1,2,4,2,2,32,128]{6,5,4,3,2,1,0:T(8,128)(2,1)}, bf16[1,2,4,2,2,32,128]{6,5,4,3,2,1,0:T(8,128)(2,1)}, u32[]{:S(2)}, u32[]{:S(2)}) collective-permute-start(bf16[1,2,4,2,2,32,128]{6,5,4,3,2,1,0:T(8,128)(2,1)} %get-tuple-element.83), channel_id=1, source_target_pairs={{0,8},{8,16},{16,24},{24,0},{1,9},{9,17},{17,25},{25,1},{2,10},{10... | collective-permute-start | bytes 786440 | tf_op jit(solution)/shard_map/ppermute | solution.py:295
  117.1 36.1 %collective-permute-start.7 = (bf16[4,1,4,1,2,32,128]{6,5,4,2,1,0,3:T(8,128)(2,1)}, bf16[4,1,4,1,2,32,128]{6,5,4,2,1,0,3:T(8,128)(2,1)}, u32[]{:S(2)}, u32[]{:S(2)}) collective-permute-start(bf16[4,1,4,1,2,32,128]{6,5,4,2,1,0,3:T(8,128)(2,1)} %bitcast.24), channel_id=1, source_target_pairs={{0,4},{4,0},{1,5},{5,1},{2,6},{6,2},{3,7},{7,3},{8,12},{12,8},{9,1... | collective-permute-start | bytes 786440 | tf_op jit(solution)/shard_map/ppermute | solution.py:355
  138.1 77.4 %all-to-all-start.1 = ((bf16[32,4,2,32,128]{4,3,2,1,0:T(8,128)(2,1)}), bf16[32,4,2,32,128]{4,3,2,1,0:T(8,128)(2,1)}, u32[]{:S(2)}, u32[]{:S(2)}) async-start(bf16[32,4,2,32,128]{4,3,2,1,0:T(8,128)(2,1)} %bitcast.4), calls=%async_computation.1 | async-start | bytes 4194304 | tf_op jit(solution)/shard_map/all_to_all | solution.py:329
  145.0 8.3 %copy-start.7 = (bf16[32,32,128]{2,1,0:T(8,128)(2,1)S(1)}, bf16[32,32,128]{2,1,0:T(8,128)(2,1)}, u32[]{:S(2)}) copy-start(bf16[32,32,128]{2,1,0:T(8,128)(2,1)} %row_transform.10) | copy-start | bytes 786436
  151.1 70.9 %collective-permute-start.11 = (bf16[1,64,1024]{2,1,0:T(8,128)(2,1)}, bf16[1,64,1024]{2,1,0:T(8,128)(2,1)}, u32[]{:S(2)}, u32[]{:S(2)}) collective-permute-start(bf16[1,64,1024]{2,1,0:T(8,128)(2,1)} %get-tuple-element.57), channel_id=1, source_target_pairs={{0,31},{1,30},{2,29},{3,28},{4,27},{5,26},{6,25},{7,24},{8,23},{9,... | collective-permute-start | bytes 393224 | tf_op jit(solution)/shard_map/ppermute | solution.py:333
  154.3 0.9 copy-start.6
  156.1 33.0 %collective-permute-start.10 = (bf16[4,2,1,1,2,32,128]{6,5,4,2,1,0,3:T(8,128)(2,1)}, bf16[4,2,1,1,2,32,128]{6,5,4,2,1,0,3:T(8,128)(2,1)}, u32[]{:S(2)}, u32[]{:S(2)}) collective-permute-start(bf16[4,2,1,1,2,32,128]{6,5,4,2,1,0,3:T(8,128)(2,1)} %get-tuple-element.87), channel_id=1, source_target_pairs={{0,1},{1,2},{2,3},{3,0},{4,5},{5,6},{6,7},{7,4},{8,9},{9,10},{10,1... | collective-permute-start | bytes 393224 | tf_op jit(solution)/shard_map/ppermute | solution.py:295
  156.1 32.1 %collective-permute-start.9 = (bf16[4,2,1,1,2,32,128]{6,5,4,2,1,0,3:T(8,128)(2,1)}, bf16[4,2,1,1,2,32,128]{6,5,4,2,1,0,3:T(8,128)(2,1)}, u32[]{:S(2)}, u32[]{:S(2)}) collective-permute-start(bf16[4,2,1,1,2,32,128]{6,5,4,2,1,0,3:T(8,128)(2,1)} %get-tuple-element.89), channel_id=1, source_target_pairs={{0,2},{1,3},{2,0},{3,1},{4,6},{5,7},{6,4},{7,5},{8,10},{9,11},{10,... | collective-permute-start | bytes 393224 | tf_op jit(solution)/shard_map/ppermute | solution.py:295
  159.1 28.2 %collective-permute-start.8 = (bf16[4,2,1,1,2,32,128]{6,5,4,2,1,0,3:T(8,128)(2,1)}, bf16[4,2,1,1,2,32,128]{6,5,4,2,1,0,3:T(8,128)(2,1)}, u32[]{:S(2)}, u32[]{:S(2)}) collective-permute-start(bf16[4,2,1,1,2,32,128]{6,5,4,2,1,0,3:T(8,128)(2,1)} %get-tuple-element.90), channel_id=1, source_target_pairs={{0,3},{1,0},{2,1},{3,2},{4,7},{5,4},{6,5},{7,6},{8,11},{9,8},{10,9... | collective-permute-start | bytes 393224 | tf_op jit(solution)/shard_map/ppermute | solution.py:295
  178.0 9.2 %copy-start.8 = (bf16[4,2,7,1,2,32,128]{6,5,4,2,1,0,3:T(8,128)(2,1)S(1)}, bf16[4,2,7,1,2,32,128]{6,5,4,2,1,0,3:T(8,128)(2,1)}, u32[]{:S(2)}) copy-start(bf16[4,2,7,1,2,32,128]{6,5,4,2,1,0,3:T(8,128)(2,1)} %get-tuple-element.88) | copy-start | bytes 2752516
  178.0 83.2 %collective-permute-start.15 = (bf16[8,64,1024]{2,1,0:T(8,128)(2,1)}, bf16[8,64,1024]{2,1,0:T(8,128)(2,1)}, u32[]{:S(2)}, u32[]{:S(2)}) collective-permute-start(bf16[8,64,1024]{2,1,0:T(8,128)(2,1)} %get-tuple-element.69), channel_id=1, source_target_pairs={{0,31},{1,30},{2,29},{3,28},{4,27},{5,26},{6,25},{7,24},{8,23},{9,... | collective-permute-start | bytes 3145736 | tf_op jit(solution)/shard_map/ppermute | solution.py:333
  222.0 11.5 %copy-start.5 = (bf16[4,2,4,1,2,32,128]{6,5,4,2,1,0,3:T(8,128)(2,1)S(1)}, bf16[4,2,4,1,2,32,128]{6,5,4,2,1,0,3:T(8,128)(2,1)}, u32[]{:S(2)}) copy-start(bf16[4,2,4,1,2,32,128]{6,5,4,2,1,0,3:T(8,128)(2,1)} %constant_dynamic-slice_fusion.4) | copy-start | bytes 1572868
  233.5 7.3 %collective-permute-start.12 = (bf16[1,2,4,1,2,32,128]{6,5,4,2,1,0,3:T(8,128)(2,1)S(1)}, bf16[1,2,4,1,2,32,128]{6,5,4,2,1,0,3:T(8,128)(2,1)S(1)}, u32[]{:S(2)}, u32[]{:S(2)}) collective-permute-start(bf16[1,2,4,1,2,32,128]{6,5,4,2,1,0,3:T(8,128)(2,1)S(1)} %get-tuple-element.94), channel_id=1, source_target_pairs={{0,24},{8,0},{16,8},{24,16},{1,25},{9,1},{17,9},{25,17},{2,26},{10... | collective-permute-start | bytes 393224 | tf_op jit(solution)/shard_map/ppermute | solution.py:295
  233.6 9.1 %collective-permute-start.13 = (bf16[1,2,4,1,2,32,128]{6,5,4,2,1,0,3:T(8,128)(2,1)S(1)}, bf16[1,2,4,1,2,32,128]{6,5,4,2,1,0,3:T(8,128)(2,1)S(1)}, u32[]{:S(2)}, u32[]{:S(2)}) collective-permute-start(bf16[1,2,4,1,2,32,128]{6,5,4,2,1,0,3:T(8,128)(2,1)S(1)} %get-tuple-element.93), channel_id=1, source_target_pairs={{0,16},{8,24},{16,0},{24,8},{1,17},{9,25},{17,1},{25,9},{2,18},{10... | collective-permute-start | bytes 393224 | tf_op jit(solution)/shard_map/ppermute | solution.py:295
  235.1 39.5 %collective-permute-start.16 = (bf16[2,64,1024]{2,1,0:T(8,128)(2,1)}, bf16[2,64,1024]{2,1,0:T(8,128)(2,1)S(1)}, u32[]{:S(2)}, u32[]{:S(2)}) collective-permute-start(bf16[2,64,1024]{2,1,0:T(8,128)(2,1)} %get-tuple-element.76), channel_id=1, source_target_pairs={{0,31},{1,30},{2,29},{3,28},{4,27},{5,26},{6,25},{7,24},{8,23},{9,... | collective-permute-start | bytes 786440 | tf_op jit(solution)/shard_map/ppermute | solution.py:333
  236.6 44.4 %collective-permute-start.18 = (bf16[4,64,1024]{2,1,0:T(8,128)(2,1)}, bf16[4,64,1024]{2,1,0:T(8,128)(2,1)}, u32[]{:S(2)}, u32[]{:S(2)}) collective-permute-start(bf16[4,64,1024]{2,1,0:T(8,128)(2,1)} %get-tuple-element.78), channel_id=1, source_target_pairs={{0,31},{1,30},{2,29},{3,28},{4,27},{5,26},{6,25},{7,24},{8,23},{9,... | collective-permute-start | bytes 1572872 | tf_op jit(solution)/shard_map/ppermute | solution.py:333
  240.8 5.8 %collective-permute-start.14 = (bf16[1,2,4,1,2,32,128]{6,5,4,2,1,0,3:T(8,128)(2,1)S(1)}, bf16[1,2,4,1,2,32,128]{6,5,4,2,1,0,3:T(8,128)(2,1)S(1)}, u32[]{:S(2)}, u32[]{:S(2)}) collective-permute-start(bf16[1,2,4,1,2,32,128]{6,5,4,2,1,0,3:T(8,128)(2,1)S(1)} %get-tuple-element.91), channel_id=1, source_target_pairs={{0,8},{8,16},{16,24},{24,0},{1,9},{9,17},{17,25},{25,1},{2,10},{10... | collective-permute-start | bytes 393224 | tf_op jit(solution)/shard_map/ppermute | solution.py:295
  261.3 6.9 %copy-start.2 = (f32[2,64,1024]{2,1,0:T(8,128)S(1)}, f32[2,64,1024]{2,1,0:T(8,128)}, u32[]{:S(2)}) copy-start(f32[2,64,1024]{2,1,0:T(8,128)} %get-tuple-element.67.refs_1_) | copy-start | bytes 1572868
  267.1 15.9 %collective-permute-start.17 = (bf16[1,64,1024]{2,1,0:T(8,128)(2,1)}, bf16[1,64,1024]{2,1,0:T(8,128)(2,1)S(1)}, u32[]{:S(2)}, u32[]{:S(2)}) collective-permute-start(bf16[1,64,1024]{2,1,0:T(8,128)(2,1)} %get-tuple-element.77), channel_id=1, source_target_pairs={{0,31},{1,30},{2,29},{3,28},{4,27},{5,26},{6,25},{7,24},{8,23},{9,... | collective-permute-start | bytes 393224 | tf_op jit(solution)/shard_map/ppermute | solution.py:333
  268.1 1.6 copy-start
  269.7 1.2 copy-start.1
  271.0 0.9 copy-start.3

commit v6 on v5

--- a/solution.py
+++ b/solution.py
@@ -272,7 +272,7 @@
 
 def assemble(arrays, places):
     total = len(places)
-    late = total // 2 if total // 2 % TILE == 0 else 0
+    late = total * 3 // 4 if total // 4 % TILE == 0 else 0
     given = []
     if late:
         given.append(write_rows([], arrays, places[:late], 0, total))

time: 287 us -> 286 us (level)
  waiting for transfers between devices: 125 us -> 121 us
    ppermute x5, waiting for transfers between devices: 28.5 us -> 24.8 us  [image_of(): return lax.ppermute(image, AXES, partner)]
  transfers between devices with their start and end apart: 21 -> 21, of which waited for: 12 -> 12; matrix products, arithmetic and copies ran while one was open for 8% -> 8% of each run, Pallas kernels for 30% -> 31%
where the time goes in v6:
time: 286 us
  waiting for transfers between devices  121 us (42%)
  Pallas kernels  96.6 us (34%)
  starting transfers between devices  36.5 us (13%)
  local copies, waits for them, and re-layouts  27.2 us (10%)
  other arithmetic  3.59 us (1%)
    ppermute x12, waiting for transfers between devices, exchange(): moved.append(lax.ppermute(pick((me + shift) % count), axis, to))  51.5 us
    pallas_call x5, Pallas kernels, spectrum(): pl.pallas_call(functools.partial(spectrum_kernel if paired is None else e...  50.1 us
    pallas_call x6, Pallas kernels, row_transform(): pl.pallas_call(row_transform_kernel, out_shape=jax.ShapeDtypeStruct((colu...  39.5 us
    all_to_all x2, waiting for transfers between devices, arrive(): got = lax.all_to_all(mixed, AXES, split_axis=0, concat_axis=0, tiled=True)  27.2 us
    ppermute x5, waiting for transfers between devices, image_of(): return lax.ppermute(image, AXES, partner)  24.8 us
    unnamed x38, local copies, waits for them, and re-layouts  18.4 us
    ppermute x2, waiting for transfers between devices, swapped(): return lax.ppermute(away, 'half', [(0, 1), (1, 0)])  17.9 us
    all_to_all x2, starting transfers between devices, arrive(): got = lax.all_to_all(mixed, AXES, split_axis=0, concat_axis=0, tiled=True)  11.5 us
  transfers between devices with their start and end apart: 21, of which 12 were waited for; matrix products, arithmetic and copies ran while one was open for 8% of the time, Pallas kernels for 31%

profile of v6, /device:TPU:13, one launch (start us, length us, event | category | flops | bytes accessed | tf_op | source)
XLA Modules:
  0.0 285.6 jit_solution(8703827614452771004)
XLA Ops:
  0.0 5.8 %row_transform.6 = bf16[64,32,128]{2,1,0:T(8,128)(2,1)} custom-call(s32[1]{0:T(128)} %bitcast.which_ref, bf16[2,64,1024]{2,1,0:T(8,128)(2,1)} %constant.391.clone.table_ref, bf16[32,128,1024]{2,1,0:T(8,128)(2,1)} %heights_ref.6), custom_call_target="tpu_custom_call" | custom-call | flops 1048576 | bytes 1048576 | tf_op jit(solution)/shard_map/row_transform/pallas_call | solution.py:96
  5.8 2.3 collective-permute-start
  8.1 10.3 %row_transform.7 = bf16[576,32,128]{2,1,0:T(8,128)(2,1)} custom-call(s32[1]{0:T(128)} %constant.378.clone.1.which_ref, bf16[1,576,1024]{2,1,0:T(8,128)(2,1)} %constant.396.table_ref, bf16[32,128,1024]{2,1,0:T(8,128)(2,1)} %heights_ref.6), custom_call_target="tpu_custom_call" | custom-call | flops 1048576 | bytes 1048576 | tf_op jit(solution)/shard_map/row_transform/pallas_call | solution.py:96
  18.4 4.6 %all-to-all-start = ((bf16[32,9,2,32,128]{4,3,2,1,0:T(8,128)(2,1)}), bf16[32,9,2,32,128]{4,3,2,1,0:T(8,128)(2,1)}, u32[]{:S(2)}, u32[]{:S(2)}) async-start(bf16[32,9,2,32,128]{4,3,2,1,0:T(8,128)(2,1)} %bitcast.18), calls=%async_computation | async-start | bytes 9437184 | tf_op jit(solution)/shard_map/all_to_all | solution.py:329
  23.1 6.4 %row_transform.8 = bf16[256,32,128]{2,1,0:T(8,128)(2,1)} custom-call(s32[1]{0:T(128)} %constant.378.clone.1.which_ref, bf16[1,256,1024]{2,1,0:T(8,128)(2,1)} %constant.395.table_ref, bf16[32,128,1024]{2,1,0:T(8,128)(2,1)} %heights_ref.6), custom_call_target="tpu_custom_call" | custom-call | flops 1099511627776 | bytes 1048576 | tf_op jit(solution)/shard_map/row_transform/pallas_call | solution.py:96
  29.4 17.9 %collective-permute-done = bf16[4,1,4,2,2,32,128]{6,5,4,3,2,1,0:T(8,128)(2,1)} collective-permute-done((bf16[4,1,4,2,2,32,128]{6,5,4,3,2,1,0:T(8,128)(2,1)}, bf16[4,1,4,2,2,32,128]{6,5,4,3,2,1,0:T(8,128)(2,1)}, u32[]{:S(2)}, u32[]{:S(2)}) %collective-permute-start) | collective-permute-done | bytes 524320 | tf_op jit(solution)/shard_map/ppermute | solution.py:355
  47.3 5.8 %row_transform.11 = bf16[64,32,128]{2,1,0:T(8,128)(2,1)} custom-call(s32[1]{0:T(128)} %bitcast.6.which_ref, bf16[2,64,1024]{2,1,0:T(8,128)(2,1)} %constant.391.clone.table_ref, bf16[32,128,1024]{2,1,0:T(8,128)(2,1)} %heights_ref.6), custom_call_target="tpu_custom_call" | custom-call | flops 1048576 | bytes 1048576 | tf_op jit(solution)/shard_map/row_transform/pallas_call | solution.py:96
  59.5 5.6 %row_transform.9 = bf16[32,32,128]{2,1,0:T(8,128)(2,1)} custom-call(s32[1]{0:T(128)} %bitcast.which_ref, bf16[2,32,1024]{2,1,0:T(8,128)(2,1)} %constant.394.clone.table_ref, bf16[32,128,1024]{2,1,0:T(8,128)(2,1)} %heights_ref.6), custom_call_target="tpu_custom_call" | custom-call | flops 1048576 | bytes 1048576 | tf_op jit(solution)/shard_map/row_transform/pallas_call | solution.py:96
  65.1 5.6 %row_transform.10 = bf16[32,32,128]{2,1,0:T(8,128)(2,1)} custom-call(s32[1]{0:T(128)} %bitcast.6.which_ref, bf16[2,32,1024]{2,1,0:T(8,128)(2,1)} %constant.394.clone.table_ref, bf16[32,128,1024]{2,1,0:T(8,128)(2,1)} %heights_ref.6), custom_call_target="tpu_custom_call" | custom-call | flops 1048576 | bytes 1048576 | tf_op jit(solution)/shard_map/row_transform/pallas_call | solution.py:96
  70.7 36.8 %collective-permute-done.1 = bf16[4,2,1,2,2,32,128]{6,5,4,3,2,1,0:T(8,128)(2,1)S(1)} collective-permute-done((bf16[4,2,1,2,2,32,128]{6,5,4,3,2,1,0:T(8,128)(2,1)}, bf16[4,2,1,2,2,32,128]{6,5,4,3,2,1,0:T(8,128)(2,1)S(1)}, u32[]{:S(2)}, u32[]{:S(2)}) %collective-permute-start.1) | collective-permute-done | bytes 262176 | tf_op jit(solution)/shard_map/ppermute | solution.py:295
  117.1 4.7 %collective-permute-start.7 = (bf16[4,1,4,1,2,32,128]{6,5,4,2,1,0,3:T(8,128)(2,1)}, bf16[4,1,4,1,2,32,128]{6,5,4,2,1,0,3:T(8,128)(2,1)}, u32[]{:S(2)}, u32[]{:S(2)}) collective-permute-start(bf16[4,1,4,1,2,32,128]{6,5,4,2,1,0,3:T(8,128)(2,1)} %bitcast.24), channel_id=1, source_target_pairs={{0,4},{4,0},{1,5},{5,1},{2,6},{6,2},{3,7},{7,3},{8,12},{12,8},{9,1... | collective-permute-start | bytes 786440 | tf_op jit(solution)/shard_map/ppermute | solution.py:355
  121.9 3.0 %collective-permute-done.4 = bf16[1,2,4,2,2,32,128]{6,5,4,3,2,1,0:T(8,128)(2,1)S(1)} collective-permute-done((bf16[1,2,4,2,2,32,128]{6,5,4,3,2,1,0:T(8,128)(2,1)}, bf16[1,2,4,2,2,32,128]{6,5,4,3,2,1,0:T(8,128)(2,1)S(1)}, u32[]{:S(2)}, u32[]{:S(2)}) %collective-permute-start.4) | collective-permute-done | bytes 262176 | tf_op jit(solution)/shard_map/ppermute | solution.py:295
  124.9 5.5 %collective-permute-done.6 = bf16[1,2,4,2,2,32,128]{6,5,4,3,2,1,0:T(8,128)(2,1)} collective-permute-done((bf16[1,2,4,2,2,32,128]{6,5,4,3,2,1,0:T(8,128)(2,1)}, bf16[1,2,4,2,2,32,128]{6,5,4,3,2,1,0:T(8,128)(2,1)}, u32[]{:S(2)}, u32[]{:S(2)}) %collective-permute-start.6) | collective-permute-done | bytes 262176 | tf_op jit(solution)/shard_map/ppermute | solution.py:295
  132.7 5.4 %all-to-all-done = bf16[32,9,2,32,128]{4,3,2,1,0:T(8,128)(2,1)} async-done(((bf16[32,9,2,32,128]{4,3,2,1,0:T(8,128)(2,1)}), bf16[32,9,2,32,128]{4,3,2,1,0:T(8,128)(2,1)}, u32[]{:S(2)}, u32[]{:S(2)}) %all-to-all-start) | async-done | bytes 4718624 | tf_op jit(solution)/shard_map/all_to_all | solution.py:329
  138.1 6.9 %all-to-all-start.1 = ((bf16[32,4,2,32,128]{4,3,2,1,0:T(8,128)(2,1)}), bf16[32,4,2,32,128]{4,3,2,1,0:T(8,128)(2,1)}, u32[]{:S(2)}, u32[]{:S(2)}) async-start(bf16[32,4,2,32,128]{4,3,2,1,0:T(8,128)(2,1)} %bitcast.4), calls=%async_computation.1 | async-start | bytes 4194304 | tf_op jit(solution)/shard_map/all_to_all | solution.py:329
  145.0 6.2 %edge_spectrum.1 = (f32[1,64,1024]{2,1,0:T(8,128)}, bf16[1,64,1024]{2,1,0:T(8,128)(2,1)}) custom-call(s32[1]{0:T(128)} %bitcast.12.paired_ref, bf16[4,8,9,2,32,128]{5,4,3,2,1,0:T(8,128)(2,1)} %bitcast.11.pieces_ref, bf16[1024,2048]{1,0:T(8,128)(2,1)} %constant.387.clone.x_ref, bf16[384,256]{1,0:T(8,128)(2,1)} %constant.388.clone.window_ref, ...), custom_call_target="tpu_custom_call" | custom-call | flops 1048576 | bytes 1048576 | tf_op jit(solution)/shard_map/edge_spectrum/pallas_call | solution.py:221
  151.1 2.1 collective-permute-start.11
  156.1 3.0 %collective-permute-start.9 = (bf16[4,2,1,1,2,32,128]{6,5,4,2,1,0,3:T(8,128)(2,1)}, bf16[4,2,1,1,2,32,128]{6,5,4,2,1,0,3:T(8,128)(2,1)}, u32[]{:S(2)}, u32[]{:S(2)}) collective-permute-start(bf16[4,2,1,1,2,32,128]{6,5,4,2,1,0,3:T(8,128)(2,1)} %get-tuple-element.89), channel_id=1, source_target_pairs={{0,2},{1,3},{2,0},{3,1},{4,6},{5,7},{6,4},{7,5},{8,10},{9,11},{10,... | collective-permute-start | bytes 393224 | tf_op jit(solution)/shard_map/ppermute | solution.py:295
  159.1 19.0 %spectrum.4 = (f32[8,64,1024]{2,1,0:T(8,128)}, bf16[8,64,1024]{2,1,0:T(8,128)(2,1)}) custom-call(bf16[4,8,9,2,32,128]{5,4,3,2,1,0:T(8,128)(2,1)} %bitcast.11.pieces_ref, bf16[1024,2048]{1,0:T(8,128)(2,1)} %constant.387.clone.x_ref, bf16[384,256]{1,0:T(8,128)(2,1)} %constant.388.clone.window_ref, bf16[64,64]{1,0:T(8,128)(2,1)} %constant.389.clone.flip_w_ref, ...), custom_call_target="tpu_custom_call" | custom-call | flops 1099511627776 | bytes 1048576 | tf_op jit(solution)/shard_map/spectrum/pallas_call | solution.py:221
  179.5 7.7 %spectrum.5 = (f32[2,64,1024]{2,1,0:T(8,128)}, bf16[2,64,1024]{2,1,0:T(8,128)(2,1)}) custom-call(bf16[4,8,2,2,32,128]{5,4,3,2,1,0:T(8,128)(2,1)} %bitcast.19, bf16[1024,2048]{1,0:T(8,128)(2,1)} %constant.387.clone.x_ref, bf16[384,256]{1,0:T(8,128)(2,1)} %constant.388.clone.window_ref, bf16[64,64]{1,0:T(8,128)(2,1)} %constant.389.clone.flip_w_ref, ...), custom_call_target="tpu_custom_call" | custom-call | flops 1048576 | bytes 1048576 | tf_op jit(solution)/shard_map/spectrum/pallas_call | solution.py:221
  193.7 21.8 %all-to-all-done.1 = bf16[32,4,2,32,128]{4,3,2,1,0:T(8,128)(2,1)} async-done(((bf16[32,4,2,32,128]{4,3,2,1,0:T(8,128)(2,1)}), bf16[32,4,2,32,128]{4,3,2,1,0:T(8,128)(2,1)}, u32[]{:S(2)}, u32[]{:S(2)}) %all-to-all-start.1) | async-done | bytes 2097184 | tf_op jit(solution)/shard_map/all_to_all | solution.py:329
  215.5 6.5 %collective-permute-done.11 = bf16[1,64,1024]{2,1,0:T(8,128)(2,1)} collective-permute-done((bf16[1,64,1024]{2,1,0:T(8,128)(2,1)}, bf16[1,64,1024]{2,1,0:T(8,128)(2,1)}, u32[]{:S(2)}, u32[]{:S(2)}) %collective-permute-start.11) | collective-permute-done | bytes 131104 | tf_op jit(solution)/shard_map/ppermute | solution.py:333
  222.0 11.5 %spectrum.6 = (f32[4,64,1024]{2,1,0:T(8,128)}, bf16[4,64,1024]{2,1,0:T(8,128)(2,1)}) custom-call(bf16[4,8,4,2,32,128]{5,4,3,2,1,0:T(8,128)(2,1)} %bitcast.15.pieces_ref, bf16[1024,2048]{1,0:T(8,128)(2,1)} %constant.387.clone.x_ref, bf16[384,256]{1,0:T(8,128)(2,1)} %constant.388.clone.window_ref, bf16[64,64]{1,0:T(8,128)(2,1)} %constant.389.clone.flip_w_ref, ...), custom_call_target="tpu_custom_call" | custom-call | flops 1099511627776 | bytes 1048576 | tf_op jit(solution)/shard_map/spectrum/pallas_call | solution.py:221
  236.6 2.1 collective-permute-start.18
  238.7 2.2 collective-permute-done.12
  242.7 4.0 %collective-permute-done.14 = bf16[1,2,4,1,2,32,128]{6,5,4,2,1,0,3:T(8,128)(2,1)S(1)} collective-permute-done((bf16[1,2,4,1,2,32,128]{6,5,4,2,1,0,3:T(8,128)(2,1)S(1)}, bf16[1,2,4,1,2,32,128]{6,5,4,2,1,0,3:T(8,128)(2,1)S(1)}, u32[]{:S(2)}, u32[]{:S(2)}) %collective-permute-start.14) | collective-permute-done | bytes 131104 | tf_op jit(solution)/shard_map/ppermute | solution.py:295
  248.5 12.7 %collective-permute-done.15.refs_4_.refs_1_ = bf16[8,64,1024]{2,1,0:T(8,128)(2,1)} collective-permute-done((bf16[8,64,1024]{2,1,0:T(8,128)(2,1)}, bf16[8,64,1024]{2,1,0:T(8,128)(2,1)}, u32[]{:S(2)}, u32[]{:S(2)}) %collective-permute-start.15) | collective-permute-done | bytes 1048608 | tf_op jit(solution)/shard_map/ppermute | solution.py:333
  261.3 5.8 %spectrum.7 = (f32[1,64,1024]{2,1,0:T(8,128)}, bf16[1,64,1024]{2,1,0:T(8,128)(2,1)}) custom-call(bf16[4,8,1,2,32,128]{5,4,3,2,1,0:T(8,128)(2,1)} %bitcast.21, bf16[1024,2048]{1,0:T(8,128)(2,1)} %constant.387.clone.x_ref, bf16[384,256]{1,0:T(8,128)(2,1)} %constant.388.clone.window_ref, bf16[64,64]{1,0:T(8,128)(2,1)} %constant.389.clone.flip_w_ref, ...), custom_call_target="tpu_custom_call" | custom-call | flops 1048576 | bytes 1048576 | tf_op jit(solution)/shard_map/spectrum/pallas_call | solution.py:221
  272.9 4.5 %write_rows.2.refs_0_ = f32[64,32,1024]{2,1,0:T(8,128)} custom-call(f32[8,64,1024]{2,1,0:T(8,128)S(1)} %copy-done, f32[2,64,1024]{2,1,0:T(8,128)S(1)} %copy-done.2, f32[1,64,1024]{2,1,0:T(8,128)S(1)} %copy-done.3, f32[4,64,1024]{2,1,0:T(8,128)S(1)} %copy-done.1, bf16[8,64,1024]{2,1,0:T(8,128)(2,1)} %collective-permute-done.15.refs_4_.refs_1_, ...), custom_call_target="tpu_custom_call" | custom-call | tf_op jit(solution)/shard_map/write_rows/pallas_call | solution.py:257
  277.4 3.5 %collective-permute-done.18.refs_4_ = bf16[4,64,1024]{2,1,0:T(8,128)(2,1)S(1)} collective-permute-done((bf16[4,64,1024]{2,1,0:T(8,128)(2,1)}, bf16[4,64,1024]{2,1,0:T(8,128)(2,1)S(1)}, u32[]{:S(2)}, u32[]{:S(2)}) %collective-permute-start.18) | collective-permute-done | bytes 524320 | tf_op jit(solution)/shard_map/ppermute | solution.py:333
  280.9 2.0 collective-permute-done.17.refs_3_
  283.0 2.6 write_rows.3
  (76 shorter events, 41.7 us)
Async XLA Ops:
  5.8 41.4 %collective-permute-start = (bf16[4,1,4,2,2,32,128]{6,5,4,3,2,1,0:T(8,128)(2,1)}, bf16[4,1,4,2,2,32,128]{6,5,4,3,2,1,0:T(8,128)(2,1)}, u32[]{:S(2)}, u32[]{:S(2)}) collective-permute-start(bf16[4,1,4,2,2,32,128]{6,5,4,3,2,1,0:T(8,128)(2,1)} %bitcast.23), channel_id=1, source_target_pairs={{0,4},{4,0},{1,5},{5,1},{2,6},{6,2},{3,7},{7,3},{8,12},{12,8},{9,1... | collective-permute-start | bytes 1572872 | tf_op jit(solution)/shard_map/ppermute | solution.py:355
  18.4 119.6 %all-to-all-start = ((bf16[32,9,2,32,128]{4,3,2,1,0:T(8,128)(2,1)}), bf16[32,9,2,32,128]{4,3,2,1,0:T(8,128)(2,1)}, u32[]{:S(2)}, u32[]{:S(2)}) async-start(bf16[32,9,2,32,128]{4,3,2,1,0:T(8,128)(2,1)} %bitcast.18), calls=%async_computation | async-start | bytes 9437184 | tf_op jit(solution)/shard_map/all_to_all | solution.py:329
  54.6 1.2 copy-start.4
  57.0 50.5 %collective-permute-start.1 = (bf16[4,2,1,2,2,32,128]{6,5,4,3,2,1,0:T(8,128)(2,1)}, bf16[4,2,1,2,2,32,128]{6,5,4,3,2,1,0:T(8,128)(2,1)S(1)}, u32[]{:S(2)}, u32[]{:S(2)}) collective-permute-start(bf16[4,2,1,2,2,32,128]{6,5,4,3,2,1,0:T(8,128)(2,1)} %get-tuple-element.82), channel_id=1, source_target_pairs={{0,3},{1,0},{2,1},{3,2},{4,7},{5,4},{6,5},{7,6},{8,11},{9,8},{10,9... | collective-permute-start | bytes 786440 | tf_op jit(solution)/shard_map/ppermute | solution.py:295
  57.9 50.3 %collective-permute-start.2 = (bf16[4,2,1,2,2,32,128]{6,5,4,3,2,1,0:T(8,128)(2,1)}, bf16[4,2,1,2,2,32,128]{6,5,4,3,2,1,0:T(8,128)(2,1)S(1)}, u32[]{:S(2)}, u32[]{:S(2)}) collective-permute-start(bf16[4,2,1,2,2,32,128]{6,5,4,3,2,1,0:T(8,128)(2,1)} %get-tuple-element.81), channel_id=1, source_target_pairs={{0,2},{1,3},{2,0},{3,1},{4,6},{5,7},{6,4},{7,5},{8,10},{9,11},{10,... | collective-permute-start | bytes 786440 | tf_op jit(solution)/shard_map/ppermute | solution.py:295
  57.9 51.1 %collective-permute-start.3 = (bf16[4,2,1,2,2,32,128]{6,5,4,3,2,1,0:T(8,128)(2,1)}, bf16[4,2,1,2,2,32,128]{6,5,4,3,2,1,0:T(8,128)(2,1)S(1)}, u32[]{:S(2)}, u32[]{:S(2)}) collective-permute-start(bf16[4,2,1,2,2,32,128]{6,5,4,3,2,1,0:T(8,128)(2,1)} %get-tuple-element.79), channel_id=1, source_target_pairs={{0,1},{1,2},{2,3},{3,0},{4,5},{5,6},{6,7},{7,4},{8,9},{9,10},{10,1... | collective-permute-start | bytes 786440 | tf_op jit(solution)/shard_map/ppermute | solution.py:295
  115.2 9.6 %collective-permute-start.4 = (bf16[1,2,4,2,2,32,128]{6,5,4,3,2,1,0:T(8,128)(2,1)}, bf16[1,2,4,2,2,32,128]{6,5,4,3,2,1,0:T(8,128)(2,1)S(1)}, u32[]{:S(2)}, u32[]{:S(2)}) collective-permute-start(bf16[1,2,4,2,2,32,128]{6,5,4,3,2,1,0:T(8,128)(2,1)} %get-tuple-element.86), channel_id=1, source_target_pairs={{0,24},{8,0},{16,8},{24,16},{1,25},{9,1},{17,9},{25,17},{2,26},{10... | collective-permute-start | bytes 786440 | tf_op jit(solution)/shard_map/ppermute | solution.py:295
  116.0 8.9 %collective-permute-start.5 = (bf16[1,2,4,2,2,32,128]{6,5,4,3,2,1,0:T(8,128)(2,1)}, bf16[1,2,4,2,2,32,128]{6,5,4,3,2,1,0:T(8,128)(2,1)S(1)}, u32[]{:S(2)}, u32[]{:S(2)}) collective-permute-start(bf16[1,2,4,2,2,32,128]{6,5,4,3,2,1,0:T(8,128)(2,1)} %get-tuple-element.85), channel_id=1, source_target_pairs={{0,16},{8,24},{16,0},{24,8},{1,17},{9,25},{17,1},{25,9},{2,18},{10... | collective-permute-start | bytes 786440 | tf_op jit(solution)/shard_map/ppermute | solution.py:295
  117.1 13.3 %collective-permute-start.6 = (bf16[1,2,4,2,2,32,128]{6,5,4,3,2,1,0:T(8,128)(2,1)}, bf16[1,2,4,2,2,32,128]{6,5,4,3,2,1,0:T(8,128)(2,1)}, u32[]{:S(2)}, u32[]{:S(2)}) collective-permute-start(bf16[1,2,4,2,2,32,128]{6,5,4,3,2,1,0:T(8,128)(2,1)} %get-tuple-element.83), channel_id=1, source_target_pairs={{0,8},{8,16},{16,24},{24,0},{1,9},{9,17},{17,25},{25,1},{2,10},{10... | collective-permute-start | bytes 786440 | tf_op jit(solution)/shard_map/ppermute | solution.py:295
  117.1 36.1 %collective-permute-start.7 = (bf16[4,1,4,1,2,32,128]{6,5,4,2,1,0,3:T(8,128)(2,1)}, bf16[4,1,4,1,2,32,128]{6,5,4,2,1,0,3:T(8,128)(2,1)}, u32[]{:S(2)}, u32[]{:S(2)}) collective-permute-start(bf16[4,1,4,1,2,32,128]{6,5,4,2,1,0,3:T(8,128)(2,1)} %bitcast.24), channel_id=1, source_target_pairs={{0,4},{4,0},{1,5},{5,1},{2,6},{6,2},{3,7},{7,3},{8,12},{12,8},{9,1... | collective-permute-start | bytes 786440 | tf_op jit(solution)/shard_map/ppermute | solution.py:355
  138.1 77.4 %all-to-all-start.1 = ((bf16[32,4,2,32,128]{4,3,2,1,0:T(8,128)(2,1)}), bf16[32,4,2,32,128]{4,3,2,1,0:T(8,128)(2,1)}, u32[]{:S(2)}, u32[]{:S(2)}) async-start(bf16[32,4,2,32,128]{4,3,2,1,0:T(8,128)(2,1)} %bitcast.4), calls=%async_computation.1 | async-start | bytes 4194304 | tf_op jit(solution)/shard_map/all_to_all | solution.py:329
  145.0 8.3 %copy-start.7 = (bf16[32,32,128]{2,1,0:T(8,128)(2,1)S(1)}, bf16[32,32,128]{2,1,0:T(8,128)(2,1)}, u32[]{:S(2)}) copy-start(bf16[32,32,128]{2,1,0:T(8,128)(2,1)} %row_transform.10) | copy-start | bytes 786436
  151.1 70.9 %collective-permute-start.11 = (bf16[1,64,1024]{2,1,0:T(8,128)(2,1)}, bf16[1,64,1024]{2,1,0:T(8,128)(2,1)}, u32[]{:S(2)}, u32[]{:S(2)}) collective-permute-start(bf16[1,64,1024]{2,1,0:T(8,128)(2,1)} %get-tuple-element.57), channel_id=1, source_target_pairs={{0,31},{1,30},{2,29},{3,28},{4,27},{5,26},{6,25},{7,24},{8,23},{9,... | collective-permute-start | bytes 393224 | tf_op jit(solution)/shard_map/ppermute | solution.py:333
  154.3 0.9 copy-start.6
  156.1 33.0 %collective-permute-start.10 = (bf16[4,2,1,1,2,32,128]{6,5,4,2,1,0,3:T(8,128)(2,1)}, bf16[4,2,1,1,2,32,128]{6,5,4,2,1,0,3:T(8,128)(2,1)}, u32[]{:S(2)}, u32[]{:S(2)}) collective-permute-start(bf16[4,2,1,1,2,32,128]{6,5,4,2,1,0,3:T(8,128)(2,1)} %get-tuple-element.87), channel_id=1, source_target_pairs={{0,1},{1,2},{2,3},{3,0},{4,5},{5,6},{6,7},{7,4},{8,9},{9,10},{10,1... | collective-permute-start | bytes 393224 | tf_op jit(solution)/shard_map/ppermute | solution.py:295
  156.1 32.1 %collective-permute-start.9 = (bf16[4,2,1,1,2,32,128]{6,5,4,2,1,0,3:T(8,128)(2,1)}, bf16[4,2,1,1,2,32,128]{6,5,4,2,1,0,3:T(8,128)(2,1)}, u32[]{:S(2)}, u32[]{:S(2)}) collective-permute-start(bf16[4,2,1,1,2,32,128]{6,5,4,2,1,0,3:T(8,128)(2,1)} %get-tuple-element.89), channel_id=1, source_target_pairs={{0,2},{1,3},{2,0},{3,1},{4,6},{5,7},{6,4},{7,5},{8,10},{9,11},{10,... | collective-permute-start | bytes 393224 | tf_op jit(solution)/shard_map/ppermute | solution.py:295
  159.1 28.2 %collective-permute-start.8 = (bf16[4,2,1,1,2,32,128]{6,5,4,2,1,0,3:T(8,128)(2,1)}, bf16[4,2,1,1,2,32,128]{6,5,4,2,1,0,3:T(8,128)(2,1)}, u32[]{:S(2)}, u32[]{:S(2)}) collective-permute-start(bf16[4,2,1,1,2,32,128]{6,5,4,2,1,0,3:T(8,128)(2,1)} %get-tuple-element.90), channel_id=1, source_target_pairs={{0,3},{1,0},{2,1},{3,2},{4,7},{5,4},{6,5},{7,6},{8,11},{9,8},{10,9... | collective-permute-start | bytes 393224 | tf_op jit(solution)/shard_map/ppermute | solution.py:295
  178.0 9.2 %copy-start.8 = (bf16[4,2,7,1,2,32,128]{6,5,4,2,1,0,3:T(8,128)(2,1)S(1)}, bf16[4,2,7,1,2,32,128]{6,5,4,2,1,0,3:T(8,128)(2,1)}, u32[]{:S(2)}) copy-start(bf16[4,2,7,1,2,32,128]{6,5,4,2,1,0,3:T(8,128)(2,1)} %get-tuple-element.88) | copy-start | bytes 2752516
  178.0 83.2 %collective-permute-start.15 = (bf16[8,64,1024]{2,1,0:T(8,128)(2,1)}, bf16[8,64,1024]{2,1,0:T(8,128)(2,1)}, u32[]{:S(2)}, u32[]{:S(2)}) collective-permute-start(bf16[8,64,1024]{2,1,0:T(8,128)(2,1)} %get-tuple-element.69), channel_id=1, source_target_pairs={{0,31},{1,30},{2,29},{3,28},{4,27},{5,26},{6,25},{7,24},{8,23},{9,... | collective-permute-start | bytes 3145736 | tf_op jit(solution)/shard_map/ppermute | solution.py:333
  222.0 11.5 %copy-start.5 = (bf16[4,2,4,1,2,32,128]{6,5,4,2,1,0,3:T(8,128)(2,1)S(1)}, bf16[4,2,4,1,2,32,128]{6,5,4,2,1,0,3:T(8,128)(2,1)}, u32[]{:S(2)}) copy-start(bf16[4,2,4,1,2,32,128]{6,5,4,2,1,0,3:T(8,128)(2,1)} %constant_dynamic-slice_fusion.4) | copy-start | bytes 1572868
  233.5 7.3 %collective-permute-start.12 = (bf16[1,2,4,1,2,32,128]{6,5,4,2,1,0,3:T(8,128)(2,1)S(1)}, bf16[1,2,4,1,2,32,128]{6,5,4,2,1,0,3:T(8,128)(2,1)S(1)}, u32[]{:S(2)}, u32[]{:S(2)}) collective-permute-start(bf16[1,2,4,1,2,32,128]{6,5,4,2,1,0,3:T(8,128)(2,1)S(1)} %get-tuple-element.94), channel_id=1, source_target_pairs={{0,24},{8,0},{16,8},{24,16},{1,25},{9,1},{17,9},{25,17},{2,26},{10... | collective-permute-start | bytes 393224 | tf_op jit(solution)/shard_map/ppermute | solution.py:295
  233.6 9.1 %collective-permute-start.13 = (bf16[1,2,4,1,2,32,128]{6,5,4,2,1,0,3:T(8,128)(2,1)S(1)}, bf16[1,2,4,1,2,32,128]{6,5,4,2,1,0,3:T(8,128)(2,1)S(1)}, u32[]{:S(2)}, u32[]{:S(2)}) collective-permute-start(bf16[1,2,4,1,2,32,128]{6,5,4,2,1,0,3:T(8,128)(2,1)S(1)} %get-tuple-element.93), channel_id=1, source_target_pairs={{0,16},{8,24},{16,0},{24,8},{1,17},{9,25},{17,1},{25,9},{2,18},{10... | collective-permute-start | bytes 393224 | tf_op jit(solution)/shard_map/ppermute | solution.py:295
  235.1 42.3 %collective-permute-start.16 = (bf16[2,64,1024]{2,1,0:T(8,128)(2,1)}, bf16[2,64,1024]{2,1,0:T(8,128)(2,1)S(1)}, u32[]{:S(2)}, u32[]{:S(2)}) collective-permute-start(bf16[2,64,1024]{2,1,0:T(8,128)(2,1)} %get-tuple-element.76), channel_id=1, source_target_pairs={{0,31},{1,30},{2,29},{3,28},{4,27},{5,26},{6,25},{7,24},{8,23},{9,... | collective-permute-start | bytes 786440 | tf_op jit(solution)/shard_map/ppermute | solution.py:333
  236.6 44.4 %collective-permute-start.18 = (bf16[4,64,1024]{2,1,0:T(8,128)(2,1)}, bf16[4,64,1024]{2,1,0:T(8,128)(2,1)S(1)}, u32[]{:S(2)}, u32[]{:S(2)}) collective-permute-start(bf16[4,64,1024]{2,1,0:T(8,128)(2,1)} %get-tuple-element.78), channel_id=1, source_target_pairs={{0,31},{1,30},{2,29},{3,28},{4,27},{5,26},{6,25},{7,24},{8,23},{9,... | collective-permute-start | bytes 1572872 | tf_op jit(solution)/shard_map/ppermute | solution.py:333
  240.8 5.8 %collective-permute-start.14 = (bf16[1,2,4,1,2,32,128]{6,5,4,2,1,0,3:T(8,128)(2,1)S(1)}, bf16[1,2,4,1,2,32,128]{6,5,4,2,1,0,3:T(8,128)(2,1)S(1)}, u32[]{:S(2)}, u32[]{:S(2)}) collective-permute-start(bf16[1,2,4,1,2,32,128]{6,5,4,2,1,0,3:T(8,128)(2,1)S(1)} %get-tuple-element.91), channel_id=1, source_target_pairs={{0,8},{8,16},{16,24},{24,0},{1,9},{9,17},{17,25},{25,1},{2,10},{10... | collective-permute-start | bytes 393224 | tf_op jit(solution)/shard_map/ppermute | solution.py:295
  267.0 15.9 %collective-permute-start.17 = (bf16[1,64,1024]{2,1,0:T(8,128)(2,1)}, bf16[1,64,1024]{2,1,0:T(8,128)(2,1)S(1)}, u32[]{:S(2)}, u32[]{:S(2)}) collective-permute-start(bf16[1,64,1024]{2,1,0:T(8,128)(2,1)} %get-tuple-element.77), channel_id=1, source_target_pairs={{0,31},{1,30},{2,29},{3,28},{4,27},{5,26},{6,25},{7,24},{8,23},{9,... | collective-permute-start | bytes 393224 | tf_op jit(solution)/shard_map/ppermute | solution.py:333
  268.1 1.6 copy-start
  269.7 1.2 copy-start.1
  270.9 1.0 copy-start.2
  271.9 0.9 copy-start.3

commit v7 on v6

--- a/solution.py
+++ b/solution.py
@@ -252,17 +252,22 @@
     _, size, length = arrays[0].shape
     step = ROWS_STEP
     used = sorted({which for which, _ in places})
-    places = [(used.index(which), plane) for which, plane in places]
+    planes = {which: {plane for at, plane in places if at == which} for which in used}
+    single = {which: min(planes[which]) for which in used if len(planes[which]) == 1}
+    places = [(used.index(which), 0 if which in single else plane) for which, plane in places]
+
+    def spec(which):
+        if which in single:
+            return pl.BlockSpec((1, step, length), lambda i: (single[which], i, 0))
+        return pl.BlockSpec((arrays[which].shape[0], step, length), lambda i: (0, i, 0))
+
     block = start // len(places)
     return pl.pallas_call(
         functools.partial(rows_kernel, places, len(given)),
         out_shape=jax.ShapeDtypeStruct((size, total, length), jnp.float32),
         grid=(size // step,),
         in_specs=[pl.BlockSpec(memory_space=pl.ANY)] * len(given)
-        + [
-            pl.BlockSpec((arrays[which].shape[0], step, length), lambda i: (0, i, 0))
-            for which in used
-        ],
+        + [spec(which) for which in used],
         out_specs=pl.BlockSpec((step, len(places), length), lambda i: (i, block, 0)),
         input_output_aliases={0: 0} if given else {},
         compiler_params=pltpu.CompilerParams(vmem_limit_bytes=ROWS_VMEM_BYTES),

time: 286 us -> 286 us (level)
  no operation moved by 1% of the time
where the time goes in v7:
time: 286 us; the launch traced here: 285 us
  waiting for transfers between devices  121 us (42%)
  Pallas kernels  96.4 us (34%)
  starting transfers between devices  36.5 us (13%)
  local copies, waits for them, and re-layouts  27.2 us (10%)
  other arithmetic  3.59 us (1%)
    ppermute x12, waiting for transfers between devices, exchange(): moved.append(lax.ppermute(pick((me + shift) % count), axis, to))  51.5 us
    pallas_call x5, Pallas kernels, spectrum(): pl.pallas_call(functools.partial(spectrum_kernel if paired is None else e...  50.1 us
    pallas_call x6, Pallas kernels, row_transform(): pl.pallas_call(row_transform_kernel, out_shape=jax.ShapeDtypeStruct((colu...  39.5 us
    all_to_all x2, waiting for transfers between devices, arrive(): got = lax.all_to_all(mixed, AXES, split_axis=0, concat_axis=0, tiled=True)  27.2 us
    ppermute x5, waiting for transfers between devices, image_of(): return lax.ppermute(image, AXES, partner)  24.8 us
    unnamed x38, local copies, waits for them, and re-layouts  18.4 us
    ppermute x2, waiting for transfers between devices, swapped(): return lax.ppermute(away, 'half', [(0, 1), (1, 0)])  17.9 us
    all_to_all x2, starting transfers between devices, arrive(): got = lax.all_to_all(mixed, AXES, split_axis=0, concat_axis=0, tiled=True)  11.5 us
  transfers between devices with their start and end apart: 21, of which 12 were waited for; matrix products, arithmetic and copies ran while one was open for 8% of the time, Pallas kernels for 31%

profile of v7, /device:TPU:13, one launch (start us, length us, event | category | flops | bytes accessed | tf_op | source)
XLA Modules:
  0.0 285.4 jit_solution(10783040875782048401)
XLA Ops:
  0.0 5.8 %row_transform.6 = bf16[64,32,128]{2,1,0:T(8,128)(2,1)} custom-call(s32[1]{0:T(128)} %bitcast.which_ref, bf16[2,64,1024]{2,1,0:T(8,128)(2,1)} %constant.391.clone.table_ref, bf16[32,128,1024]{2,1,0:T(8,128)(2,1)} %heights_ref.6), custom_call_target="tpu_custom_call" | custom-call | flops 1048576 | bytes 1048576 | tf_op jit(solution)/shard_map/row_transform/pallas_call | solution.py:96
  5.8 2.3 collective-permute-start
  8.1 10.3 %row_transform.7 = bf16[576,32,128]{2,1,0:T(8,128)(2,1)} custom-call(s32[1]{0:T(128)} %constant.378.clone.1.which_ref, bf16[1,576,1024]{2,1,0:T(8,128)(2,1)} %constant.396.table_ref, bf16[32,128,1024]{2,1,0:T(8,128)(2,1)} %heights_ref.6), custom_call_target="tpu_custom_call" | custom-call | flops 1048576 | bytes 1048576 | tf_op jit(solution)/shard_map/row_transform/pallas_call | solution.py:96
  18.4 4.6 %all-to-all-start = ((bf16[32,9,2,32,128]{4,3,2,1,0:T(8,128)(2,1)}), bf16[32,9,2,32,128]{4,3,2,1,0:T(8,128)(2,1)}, u32[]{:S(2)}, u32[]{:S(2)}) async-start(bf16[32,9,2,32,128]{4,3,2,1,0:T(8,128)(2,1)} %bitcast.18), calls=%async_computation | async-start | bytes 9437184 | tf_op jit(solution)/shard_map/all_to_all | solution.py:334
  23.1 6.4 %row_transform.8 = bf16[256,32,128]{2,1,0:T(8,128)(2,1)} custom-call(s32[1]{0:T(128)} %constant.378.clone.1.which_ref, bf16[1,256,1024]{2,1,0:T(8,128)(2,1)} %constant.395.table_ref, bf16[32,128,1024]{2,1,0:T(8,128)(2,1)} %heights_ref.6), custom_call_target="tpu_custom_call" | custom-call | flops 1099511627776 | bytes 1048576 | tf_op jit(solution)/shard_map/row_transform/pallas_call | solution.py:96
  29.4 17.9 %collective-permute-done = bf16[4,1,4,2,2,32,128]{6,5,4,3,2,1,0:T(8,128)(2,1)} collective-permute-done((bf16[4,1,4,2,2,32,128]{6,5,4,3,2,1,0:T(8,128)(2,1)}, bf16[4,1,4,2,2,32,128]{6,5,4,3,2,1,0:T(8,128)(2,1)}, u32[]{:S(2)}, u32[]{:S(2)}) %collective-permute-start) | collective-permute-done | bytes 524320 | tf_op jit(solution)/shard_map/ppermute | solution.py:360
  47.3 5.8 %row_transform.11 = bf16[64,32,128]{2,1,0:T(8,128)(2,1)} custom-call(s32[1]{0:T(128)} %bitcast.6.which_ref, bf16[2,64,1024]{2,1,0:T(8,128)(2,1)} %constant.391.clone.table_ref, bf16[32,128,1024]{2,1,0:T(8,128)(2,1)} %heights_ref.6), custom_call_target="tpu_custom_call" | custom-call | flops 1048576 | bytes 1048576 | tf_op jit(solution)/shard_map/row_transform/pallas_call | solution.py:96
  59.5 5.6 %row_transform.9 = bf16[32,32,128]{2,1,0:T(8,128)(2,1)} custom-call(s32[1]{0:T(128)} %bitcast.which_ref, bf16[2,32,1024]{2,1,0:T(8,128)(2,1)} %constant.394.clone.table_ref, bf16[32,128,1024]{2,1,0:T(8,128)(2,1)} %heights_ref.6), custom_call_target="tpu_custom_call" | custom-call | flops 1048576 | bytes 1048576 | tf_op jit(solution)/shard_map/row_transform/pallas_call | solution.py:96
  65.1 5.6 %row_transform.10 = bf16[32,32,128]{2,1,0:T(8,128)(2,1)} custom-call(s32[1]{0:T(128)} %bitcast.6.which_ref, bf16[2,32,1024]{2,1,0:T(8,128)(2,1)} %constant.394.clone.table_ref, bf16[32,128,1024]{2,1,0:T(8,128)(2,1)} %heights_ref.6), custom_call_target="tpu_custom_call" | custom-call | flops 1048576 | bytes 1048576 | tf_op jit(solution)/shard_map/row_transform/pallas_call | solution.py:96
  70.7 36.8 %collective-permute-done.1 = bf16[4,2,1,2,2,32,128]{6,5,4,3,2,1,0:T(8,128)(2,1)S(1)} collective-permute-done((bf16[4,2,1,2,2,32,128]{6,5,4,3,2,1,0:T(8,128)(2,1)}, bf16[4,2,1,2,2,32,128]{6,5,4,3,2,1,0:T(8,128)(2,1)S(1)}, u32[]{:S(2)}, u32[]{:S(2)}) %collective-permute-start.1) | collective-permute-done | bytes 262176 | tf_op jit(solution)/shard_map/ppermute | solution.py:300
  117.1 4.7 %collective-permute-start.7 = (bf16[4,1,4,1,2,32,128]{6,5,4,2,1,0,3:T(8,128)(2,1)}, bf16[4,1,4,1,2,32,128]{6,5,4,2,1,0,3:T(8,128)(2,1)}, u32[]{:S(2)}, u32[]{:S(2)}) collective-permute-start(bf16[4,1,4,1,2,32,128]{6,5,4,2,1,0,3:T(8,128)(2,1)} %bitcast.24), channel_id=1, source_target_pairs={{0,4},{4,0},{1,5},{5,1},{2,6},{6,2},{3,7},{7,3},{8,12},{12,8},{9,1... | collective-permute-start | bytes 786440 | tf_op jit(solution)/shard_map/ppermute | solution.py:360
  121.9 3.0 %collective-permute-done.4 = bf16[1,2,4,2,2,32,128]{6,5,4,3,2,1,0:T(8,128)(2,1)S(1)} collective-permute-done((bf16[1,2,4,2,2,32,128]{6,5,4,3,2,1,0:T(8,128)(2,1)}, bf16[1,2,4,2,2,32,128]{6,5,4,3,2,1,0:T(8,128)(2,1)S(1)}, u32[]{:S(2)}, u32[]{:S(2)}) %collective-permute-start.4) | collective-permute-done | bytes 262176 | tf_op jit(solution)/shard_map/ppermute | solution.py:300
  124.9 5.5 %collective-permute-done.6 = bf16[1,2,4,2,2,32,128]{6,5,4,3,2,1,0:T(8,128)(2,1)} collective-permute-done((bf16[1,2,4,2,2,32,128]{6,5,4,3,2,1,0:T(8,128)(2,1)}, bf16[1,2,4,2,2,32,128]{6,5,4,3,2,1,0:T(8,128)(2,1)}, u32[]{:S(2)}, u32[]{:S(2)}) %collective-permute-start.6) | collective-permute-done | bytes 262176 | tf_op jit(solution)/shard_map/ppermute | solution.py:300
  132.7 5.4 %all-to-all-done = bf16[32,9,2,32,128]{4,3,2,1,0:T(8,128)(2,1)} async-done(((bf16[32,9,2,32,128]{4,3,2,1,0:T(8,128)(2,1)}), bf16[32,9,2,32,128]{4,3,2,1,0:T(8,128)(2,1)}, u32[]{:S(2)}, u32[]{:S(2)}) %all-to-all-start) | async-done | bytes 4718624 | tf_op jit(solution)/shard_map/all_to_all | solution.py:334
  138.1 6.9 %all-to-all-start.1 = ((bf16[32,4,2,32,128]{4,3,2,1,0:T(8,128)(2,1)}), bf16[32,4,2,32,128]{4,3,2,1,0:T(8,128)(2,1)}, u32[]{:S(2)}, u32[]{:S(2)}) async-start(bf16[32,4,2,32,128]{4,3,2,1,0:T(8,128)(2,1)} %bitcast.4), calls=%async_computation.1 | async-start | bytes 4194304 | tf_op jit(solution)/shard_map/all_to_all | solution.py:334
  145.0 6.2 %edge_spectrum.1 = (f32[1,64,1024]{2,1,0:T(8,128)}, bf16[1,64,1024]{2,1,0:T(8,128)(2,1)}) custom-call(s32[1]{0:T(128)} %bitcast.12.paired_ref, bf16[4,8,9,2,32,128]{5,4,3,2,1,0:T(8,128)(2,1)} %bitcast.11.pieces_ref, bf16[1024,2048]{1,0:T(8,128)(2,1)} %constant.387.clone.x_ref, bf16[384,256]{1,0:T(8,128)(2,1)} %constant.388.clone.window_ref, ...), custom_call_target="tpu_custom_call" | custom-call | flops 1048576 | bytes 1048576 | tf_op jit(solution)/shard_map/edge_spectrum/pallas_call | solution.py:221
  151.1 2.1 collective-permute-start.11
  156.1 3.0 %collective-permute-start.9 = (bf16[4,2,1,1,2,32,128]{6,5,4,2,1,0,3:T(8,128)(2,1)}, bf16[4,2,1,1,2,32,128]{6,5,4,2,1,0,3:T(8,128)(2,1)}, u32[]{:S(2)}, u32[]{:S(2)}) collective-permute-start(bf16[4,2,1,1,2,32,128]{6,5,4,2,1,0,3:T(8,128)(2,1)} %get-tuple-element.89), channel_id=1, source_target_pairs={{0,2},{1,3},{2,0},{3,1},{4,6},{5,7},{6,4},{7,5},{8,10},{9,11},{10,... | collective-permute-start | bytes 393224 | tf_op jit(solution)/shard_map/ppermute | solution.py:300
  159.1 19.0 %spectrum.4 = (f32[8,64,1024]{2,1,0:T(8,128)}, bf16[8,64,1024]{2,1,0:T(8,128)(2,1)}) custom-call(bf16[4,8,9,2,32,128]{5,4,3,2,1,0:T(8,128)(2,1)} %bitcast.11.pieces_ref, bf16[1024,2048]{1,0:T(8,128)(2,1)} %constant.387.clone.x_ref, bf16[384,256]{1,0:T(8,128)(2,1)} %constant.388.clone.window_ref, bf16[64,64]{1,0:T(8,128)(2,1)} %constant.389.clone.flip_w_ref, ...), custom_call_target="tpu_custom_call" | custom-call | flops 1099511627776 | bytes 1048576 | tf_op jit(solution)/shard_map/spectrum/pallas_call | solution.py:221
  179.5 7.7 %spectrum.5 = (f32[2,64,1024]{2,1,0:T(8,128)}, bf16[2,64,1024]{2,1,0:T(8,128)(2,1)}) custom-call(bf16[4,8,2,2,32,128]{5,4,3,2,1,0:T(8,128)(2,1)} %bitcast.19, bf16[1024,2048]{1,0:T(8,128)(2,1)} %constant.387.clone.x_ref, bf16[384,256]{1,0:T(8,128)(2,1)} %constant.388.clone.window_ref, bf16[64,64]{1,0:T(8,128)(2,1)} %constant.389.clone.flip_w_ref, ...), custom_call_target="tpu_custom_call" | custom-call | flops 1048576 | bytes 1048576 | tf_op jit(solution)/shard_map/spectrum/pallas_call | solution.py:221
  193.7 21.8 %all-to-all-done.1 = bf16[32,4,2,32,128]{4,3,2,1,0:T(8,128)(2,1)} async-done(((bf16[32,4,2,32,128]{4,3,2,1,0:T(8,128)(2,1)}), bf16[32,4,2,32,128]{4,3,2,1,0:T(8,128)(2,1)}, u32[]{:S(2)}, u32[]{:S(2)}) %all-to-all-start.1) | async-done | bytes 2097184 | tf_op jit(solution)/shard_map/all_to_all | solution.py:334
  215.5 6.5 %collective-permute-done.11 = bf16[1,64,1024]{2,1,0:T(8,128)(2,1)} collective-permute-done((bf16[1,64,1024]{2,1,0:T(8,128)(2,1)}, bf16[1,64,1024]{2,1,0:T(8,128)(2,1)}, u32[]{:S(2)}, u32[]{:S(2)}) %collective-permute-start.11) | collective-permute-done | bytes 131104 | tf_op jit(solution)/shard_map/ppermute | solution.py:338
  222.0 11.5 %spectrum.6 = (f32[4,64,1024]{2,1,0:T(8,128)}, bf16[4,64,1024]{2,1,0:T(8,128)(2,1)}) custom-call(bf16[4,8,4,2,32,128]{5,4,3,2,1,0:T(8,128)(2,1)} %bitcast.15.pieces_ref, bf16[1024,2048]{1,0:T(8,128)(2,1)} %constant.387.clone.x_ref, bf16[384,256]{1,0:T(8,128)(2,1)} %constant.388.clone.window_ref, bf16[64,64]{1,0:T(8,128)(2,1)} %constant.389.clone.flip_w_ref, ...), custom_call_target="tpu_custom_call" | custom-call | flops 1099511627776 | bytes 1048576 | tf_op jit(solution)/shard_map/spectrum/pallas_call | solution.py:221
  236.6 2.1 collective-permute-start.18
  238.7 2.2 collective-permute-done.12
  242.7 4.0 %collective-permute-done.14 = bf16[1,2,4,1,2,32,128]{6,5,4,2,1,0,3:T(8,128)(2,1)S(1)} collective-permute-done((bf16[1,2,4,1,2,32,128]{6,5,4,2,1,0,3:T(8,128)(2,1)S(1)}, bf16[1,2,4,1,2,32,128]{6,5,4,2,1,0,3:T(8,128)(2,1)S(1)}, u32[]{:S(2)}, u32[]{:S(2)}) %collective-permute-start.14) | collective-permute-done | bytes 131104 | tf_op jit(solution)/shard_map/ppermute | solution.py:300
  248.5 12.7 %collective-permute-done.15.refs_4_.refs_1_ = bf16[8,64,1024]{2,1,0:T(8,128)(2,1)} collective-permute-done((bf16[8,64,1024]{2,1,0:T(8,128)(2,1)}, bf16[8,64,1024]{2,1,0:T(8,128)(2,1)}, u32[]{:S(2)}, u32[]{:S(2)}) %collective-permute-start.15) | collective-permute-done | bytes 1048608 | tf_op jit(solution)/shard_map/ppermute | solution.py:338
  261.3 5.8 %spectrum.7 = (f32[1,64,1024]{2,1,0:T(8,128)}, bf16[1,64,1024]{2,1,0:T(8,128)(2,1)}) custom-call(bf16[4,8,1,2,32,128]{5,4,3,2,1,0:T(8,128)(2,1)} %bitcast.21, bf16[1024,2048]{1,0:T(8,128)(2,1)} %constant.387.clone.x_ref, bf16[384,256]{1,0:T(8,128)(2,1)} %constant.388.clone.window_ref, bf16[64,64]{1,0:T(8,128)(2,1)} %constant.389.clone.flip_w_ref, ...), custom_call_target="tpu_custom_call" | custom-call | flops 1048576 | bytes 1048576 | tf_op jit(solution)/shard_map/spectrum/pallas_call | solution.py:221
  272.9 4.5 %write_rows.2.refs_0_ = f32[64,32,1024]{2,1,0:T(8,128)} custom-call(f32[8,64,1024]{2,1,0:T(8,128)S(1)} %copy-done, f32[2,64,1024]{2,1,0:T(8,128)S(1)} %copy-done.2, f32[1,64,1024]{2,1,0:T(8,128)S(1)} %copy-done.3, f32[4,64,1024]{2,1,0:T(8,128)S(1)} %copy-done.1, bf16[8,64,1024]{2,1,0:T(8,128)(2,1)} %collective-permute-done.15.refs_4_.refs_1_, ...), custom_call_target="tpu_custom_call" | custom-call | tf_op jit(solution)/shard_map/write_rows/pallas_call | solution.py:265
  277.4 3.5 %collective-permute-done.18.refs_4_ = bf16[4,64,1024]{2,1,0:T(8,128)(2,1)S(1)} collective-permute-done((bf16[4,64,1024]{2,1,0:T(8,128)(2,1)}, bf16[4,64,1024]{2,1,0:T(8,128)(2,1)S(1)}, u32[]{:S(2)}, u32[]{:S(2)}) %collective-permute-start.18) | collective-permute-done | bytes 524320 | tf_op jit(solution)/shard_map/ppermute | solution.py:338
  280.9 2.0 collective-permute-done.17.refs_3_
  283.0 2.4 write_rows.3
  (76 shorter events, 41.7 us)
Async XLA Ops:
  5.8 41.4 %collective-permute-start = (bf16[4,1,4,2,2,32,128]{6,5,4,3,2,1,0:T(8,128)(2,1)}, bf16[4,1,4,2,2,32,128]{6,5,4,3,2,1,0:T(8,128)(2,1)}, u32[]{:S(2)}, u32[]{:S(2)}) collective-permute-start(bf16[4,1,4,2,2,32,128]{6,5,4,3,2,1,0:T(8,128)(2,1)} %bitcast.23), channel_id=1, source_target_pairs={{0,4},{4,0},{1,5},{5,1},{2,6},{6,2},{3,7},{7,3},{8,12},{12,8},{9,1... | collective-permute-start | bytes 1572872 | tf_op jit(solution)/shard_map/ppermute | solution.py:360
  18.4 119.6 %all-to-all-start = ((bf16[32,9,2,32,128]{4,3,2,1,0:T(8,128)(2,1)}), bf16[32,9,2,32,128]{4,3,2,1,0:T(8,128)(2,1)}, u32[]{:S(2)}, u32[]{:S(2)}) async-start(bf16[32,9,2,32,128]{4,3,2,1,0:T(8,128)(2,1)} %bitcast.18), calls=%async_computation | async-start | bytes 9437184 | tf_op jit(solution)/shard_map/all_to_all | solution.py:334
  54.6 1.2 copy-start.4
  57.0 50.5 %collective-permute-start.1 = (bf16[4,2,1,2,2,32,128]{6,5,4,3,2,1,0:T(8,128)(2,1)}, bf16[4,2,1,2,2,32,128]{6,5,4,3,2,1,0:T(8,128)(2,1)S(1)}, u32[]{:S(2)}, u32[]{:S(2)}) collective-permute-start(bf16[4,2,1,2,2,32,128]{6,5,4,3,2,1,0:T(8,128)(2,1)} %get-tuple-element.82), channel_id=1, source_target_pairs={{0,3},{1,0},{2,1},{3,2},{4,7},{5,4},{6,5},{7,6},{8,11},{9,8},{10,9... | collective-permute-start | bytes 786440 | tf_op jit(solution)/shard_map/ppermute | solution.py:300
  57.9 50.3 %collective-permute-start.2 = (bf16[4,2,1,2,2,32,128]{6,5,4,3,2,1,0:T(8,128)(2,1)}, bf16[4,2,1,2,2,32,128]{6,5,4,3,2,1,0:T(8,128)(2,1)S(1)}, u32[]{:S(2)}, u32[]{:S(2)}) collective-permute-start(bf16[4,2,1,2,2,32,128]{6,5,4,3,2,1,0:T(8,128)(2,1)} %get-tuple-element.81), channel_id=1, source_target_pairs={{0,2},{1,3},{2,0},{3,1},{4,6},{5,7},{6,4},{7,5},{8,10},{9,11},{10,... | collective-permute-start | bytes 786440 | tf_op jit(solution)/shard_map/ppermute | solution.py:300
  57.9 51.1 %collective-permute-start.3 = (bf16[4,2,1,2,2,32,128]{6,5,4,3,2,1,0:T(8,128)(2,1)}, bf16[4,2,1,2,2,32,128]{6,5,4,3,2,1,0:T(8,128)(2,1)S(1)}, u32[]{:S(2)}, u32[]{:S(2)}) collective-permute-start(bf16[4,2,1,2,2,32,128]{6,5,4,3,2,1,0:T(8,128)(2,1)} %get-tuple-element.79), channel_id=1, source_target_pairs={{0,1},{1,2},{2,3},{3,0},{4,5},{5,6},{6,7},{7,4},{8,9},{9,10},{10,1... | collective-permute-start | bytes 786440 | tf_op jit(solution)/shard_map/ppermute | solution.py:300
  115.2 9.6 %collective-permute-start.4 = (bf16[1,2,4,2,2,32,128]{6,5,4,3,2,1,0:T(8,128)(2,1)}, bf16[1,2,4,2,2,32,128]{6,5,4,3,2,1,0:T(8,128)(2,1)S(1)}, u32[]{:S(2)}, u32[]{:S(2)}) collective-permute-start(bf16[1,2,4,2,2,32,128]{6,5,4,3,2,1,0:T(8,128)(2,1)} %get-tuple-element.86), channel_id=1, source_target_pairs={{0,24},{8,0},{16,8},{24,16},{1,25},{9,1},{17,9},{25,17},{2,26},{10... | collective-permute-start | bytes 786440 | tf_op jit(solution)/shard_map/ppermute | solution.py:300
  116.0 8.9 %collective-permute-start.5 = (bf16[1,2,4,2,2,32,128]{6,5,4,3,2,1,0:T(8,128)(2,1)}, bf16[1,2,4,2,2,32,128]{6,5,4,3,2,1,0:T(8,128)(2,1)S(1)}, u32[]{:S(2)}, u32[]{:S(2)}) collective-permute-start(bf16[1,2,4,2,2,32,128]{6,5,4,3,2,1,0:T(8,128)(2,1)} %get-tuple-element.85), channel_id=1, source_target_pairs={{0,16},{8,24},{16,0},{24,8},{1,17},{9,25},{17,1},{25,9},{2,18},{10... | collective-permute-start | bytes 786440 | tf_op jit(solution)/shard_map/ppermute | solution.py:300
  117.1 13.3 %collective-permute-start.6 = (bf16[1,2,4,2,2,32,128]{6,5,4,3,2,1,0:T(8,128)(2,1)}, bf16[1,2,4,2,2,32,128]{6,5,4,3,2,1,0:T(8,128)(2,1)}, u32[]{:S(2)}, u32[]{:S(2)}) collective-permute-start(bf16[1,2,4,2,2,32,128]{6,5,4,3,2,1,0:T(8,128)(2,1)} %get-tuple-element.83), channel_id=1, source_target_pairs={{0,8},{8,16},{16,24},{24,0},{1,9},{9,17},{17,25},{25,1},{2,10},{10... | collective-permute-start | bytes 786440 | tf_op jit(solution)/shard_map/ppermute | solution.py:300
  117.1 36.1 %collective-permute-start.7 = (bf16[4,1,4,1,2,32,128]{6,5,4,2,1,0,3:T(8,128)(2,1)}, bf16[4,1,4,1,2,32,128]{6,5,4,2,1,0,3:T(8,128)(2,1)}, u32[]{:S(2)}, u32[]{:S(2)}) collective-permute-start(bf16[4,1,4,1,2,32,128]{6,5,4,2,1,0,3:T(8,128)(2,1)} %bitcast.24), channel_id=1, source_target_pairs={{0,4},{4,0},{1,5},{5,1},{2,6},{6,2},{3,7},{7,3},{8,12},{12,8},{9,1... | collective-permute-start | bytes 786440 | tf_op jit(solution)/shard_map/ppermute | solution.py:360
  138.1 77.4 %all-to-all-start.1 = ((bf16[32,4,2,32,128]{4,3,2,1,0:T(8,128)(2,1)}), bf16[32,4,2,32,128]{4,3,2,1,0:T(8,128)(2,1)}, u32[]{:S(2)}, u32[]{:S(2)}) async-start(bf16[32,4,2,32,128]{4,3,2,1,0:T(8,128)(2,1)} %bitcast.4), calls=%async_computation.1 | async-start | bytes 4194304 | tf_op jit(solution)/shard_map/all_to_all | solution.py:334
  145.0 8.3 %copy-start.7 = (bf16[32,32,128]{2,1,0:T(8,128)(2,1)S(1)}, bf16[32,32,128]{2,1,0:T(8,128)(2,1)}, u32[]{:S(2)}) copy-start(bf16[32,32,128]{2,1,0:T(8,128)(2,1)} %row_transform.10) | copy-start | bytes 786436
  151.1 70.9 %collective-permute-start.11 = (bf16[1,64,1024]{2,1,0:T(8,128)(2,1)}, bf16[1,64,1024]{2,1,0:T(8,128)(2,1)}, u32[]{:S(2)}, u32[]{:S(2)}) collective-permute-start(bf16[1,64,1024]{2,1,0:T(8,128)(2,1)} %get-tuple-element.57), channel_id=1, source_target_pairs={{0,31},{1,30},{2,29},{3,28},{4,27},{5,26},{6,25},{7,24},{8,23},{9,... | collective-permute-start | bytes 393224 | tf_op jit(solution)/shard_map/ppermute | solution.py:338
  154.3 0.9 copy-start.6
  156.1 33.0 %collective-permute-start.10 = (bf16[4,2,1,1,2,32,128]{6,5,4,2,1,0,3:T(8,128)(2,1)}, bf16[4,2,1,1,2,32,128]{6,5,4,2,1,0,3:T(8,128)(2,1)}, u32[]{:S(2)}, u32[]{:S(2)}) collective-permute-start(bf16[4,2,1,1,2,32,128]{6,5,4,2,1,0,3:T(8,128)(2,1)} %get-tuple-element.87), channel_id=1, source_target_pairs={{0,1},{1,2},{2,3},{3,0},{4,5},{5,6},{6,7},{7,4},{8,9},{9,10},{10,1... | collective-permute-start | bytes 393224 | tf_op jit(solution)/shard_map/ppermute | solution.py:300
  156.1 32.1 %collective-permute-start.9 = (bf16[4,2,1,1,2,32,128]{6,5,4,2,1,0,3:T(8,128)(2,1)}, bf16[4,2,1,1,2,32,128]{6,5,4,2,1,0,3:T(8,128)(2,1)}, u32[]{:S(2)}, u32[]{:S(2)}) collective-permute-start(bf16[4,2,1,1,2,32,128]{6,5,4,2,1,0,3:T(8,128)(2,1)} %get-tuple-element.89), channel_id=1, source_target_pairs={{0,2},{1,3},{2,0},{3,1},{4,6},{5,7},{6,4},{7,5},{8,10},{9,11},{10,... | collective-permute-start | bytes 393224 | tf_op jit(solution)/shard_map/ppermute | solution.py:300
  159.1 28.2 %collective-permute-start.8 = (bf16[4,2,1,1,2,32,128]{6,5,4,2,1,0,3:T(8,128)(2,1)}, bf16[4,2,1,1,2,32,128]{6,5,4,2,1,0,3:T(8,128)(2,1)}, u32[]{:S(2)}, u32[]{:S(2)}) collective-permute-start(bf16[4,2,1,1,2,32,128]{6,5,4,2,1,0,3:T(8,128)(2,1)} %get-tuple-element.90), channel_id=1, source_target_pairs={{0,3},{1,0},{2,1},{3,2},{4,7},{5,4},{6,5},{7,6},{8,11},{9,8},{10,9... | collective-permute-start | bytes 393224 | tf_op jit(solution)/shard_map/ppermute | solution.py:300
  178.0 9.2 %copy-start.8 = (bf16[4,2,7,1,2,32,128]{6,5,4,2,1,0,3:T(8,128)(2,1)S(1)}, bf16[4,2,7,1,2,32,128]{6,5,4,2,1,0,3:T(8,128)(2,1)}, u32[]{:S(2)}) copy-start(bf16[4,2,7,1,2,32,128]{6,5,4,2,1,0,3:T(8,128)(2,1)} %get-tuple-element.88) | copy-start | bytes 2752516
  178.0 83.2 %collective-permute-start.15 = (bf16[8,64,1024]{2,1,0:T(8,128)(2,1)}, bf16[8,64,1024]{2,1,0:T(8,128)(2,1)}, u32[]{:S(2)}, u32[]{:S(2)}) collective-permute-start(bf16[8,64,1024]{2,1,0:T(8,128)(2,1)} %get-tuple-element.69), channel_id=1, source_target_pairs={{0,31},{1,30},{2,29},{3,28},{4,27},{5,26},{6,25},{7,24},{8,23},{9,... | collective-permute-start | bytes 3145736 | tf_op jit(solution)/shard_map/ppermute | solution.py:338
  222.0 11.5 %copy-start.5 = (bf16[4,2,4,1,2,32,128]{6,5,4,2,1,0,3:T(8,128)(2,1)S(1)}, bf16[4,2,4,1,2,32,128]{6,5,4,2,1,0,3:T(8,128)(2,1)}, u32[]{:S(2)}) copy-start(bf16[4,2,4,1,2,32,128]{6,5,4,2,1,0,3:T(8,128)(2,1)} %constant_dynamic-slice_fusion.4) | copy-start | bytes 1572868
  233.5 7.3 %collective-permute-start.12 = (bf16[1,2,4,1,2,32,128]{6,5,4,2,1,0,3:T(8,128)(2,1)S(1)}, bf16[1,2,4,1,2,32,128]{6,5,4,2,1,0,3:T(8,128)(2,1)S(1)}, u32[]{:S(2)}, u32[]{:S(2)}) collective-permute-start(bf16[1,2,4,1,2,32,128]{6,5,4,2,1,0,3:T(8,128)(2,1)S(1)} %get-tuple-element.94), channel_id=1, source_target_pairs={{0,24},{8,0},{16,8},{24,16},{1,25},{9,1},{17,9},{25,17},{2,26},{10... | collective-permute-start | bytes 393224 | tf_op jit(solution)/shard_map/ppermute | solution.py:300
  233.6 9.1 %collective-permute-start.13 = (bf16[1,2,4,1,2,32,128]{6,5,4,2,1,0,3:T(8,128)(2,1)S(1)}, bf16[1,2,4,1,2,32,128]{6,5,4,2,1,0,3:T(8,128)(2,1)S(1)}, u32[]{:S(2)}, u32[]{:S(2)}) collective-permute-start(bf16[1,2,4,1,2,32,128]{6,5,4,2,1,0,3:T(8,128)(2,1)S(1)} %get-tuple-element.93), channel_id=1, source_target_pairs={{0,16},{8,24},{16,0},{24,8},{1,17},{9,25},{17,1},{25,9},{2,18},{10... | collective-permute-start | bytes 393224 | tf_op jit(solution)/shard_map/ppermute | solution.py:300
  235.1 42.3 %collective-permute-start.16 = (bf16[2,64,1024]{2,1,0:T(8,128)(2,1)}, bf16[2,64,1024]{2,1,0:T(8,128)(2,1)S(1)}, u32[]{:S(2)}, u32[]{:S(2)}) collective-permute-start(bf16[2,64,1024]{2,1,0:T(8,128)(2,1)} %get-tuple-element.76), channel_id=1, source_target_pairs={{0,31},{1,30},{2,29},{3,28},{4,27},{5,26},{6,25},{7,24},{8,23},{9,... | collective-permute-start | bytes 786440 | tf_op jit(solution)/shard_map/ppermute | solution.py:338
  236.6 44.4 %collective-permute-start.18 = (bf16[4,64,1024]{2,1,0:T(8,128)(2,1)}, bf16[4,64,1024]{2,1,0:T(8,128)(2,1)S(1)}, u32[]{:S(2)}, u32[]{:S(2)}) collective-permute-start(bf16[4,64,1024]{2,1,0:T(8,128)(2,1)} %get-tuple-element.78), channel_id=1, source_target_pairs={{0,31},{1,30},{2,29},{3,28},{4,27},{5,26},{6,25},{7,24},{8,23},{9,... | collective-permute-start | bytes 1572872 | tf_op jit(solution)/shard_map/ppermute | solution.py:338
  240.8 5.8 %collective-permute-start.14 = (bf16[1,2,4,1,2,32,128]{6,5,4,2,1,0,3:T(8,128)(2,1)S(1)}, bf16[1,2,4,1,2,32,128]{6,5,4,2,1,0,3:T(8,128)(2,1)S(1)}, u32[]{:S(2)}, u32[]{:S(2)}) collective-permute-start(bf16[1,2,4,1,2,32,128]{6,5,4,2,1,0,3:T(8,128)(2,1)S(1)} %get-tuple-element.91), channel_id=1, source_target_pairs={{0,8},{8,16},{16,24},{24,0},{1,9},{9,17},{17,25},{25,1},{2,10},{10... | collective-permute-start | bytes 393224 | tf_op jit(solution)/shard_map/ppermute | solution.py:300
  267.0 15.9 %collective-permute-start.17 = (bf16[1,64,1024]{2,1,0:T(8,128)(2,1)}, bf16[1,64,1024]{2,1,0:T(8,128)(2,1)S(1)}, u32[]{:S(2)}, u32[]{:S(2)}) collective-permute-start(bf16[1,64,1024]{2,1,0:T(8,128)(2,1)} %get-tuple-element.77), channel_id=1, source_target_pairs={{0,31},{1,30},{2,29},{3,28},{4,27},{5,26},{6,25},{7,24},{8,23},{9,... | collective-permute-start | bytes 393224 | tf_op jit(solution)/shard_map/ppermute | solution.py:338
  268.1 1.6 copy-start
  269.7 1.2 copy-start.1
  270.9 1.0 copy-start.2
  271.9 0.9 copy-start.3
